TPU v7x, 32 devices: a whole 2x2x4 slice. The times are simulated.
32 devices in a mesh: pairs: 8 (over z, x), days: 4 (over y, core).
Axes of the slice: x: 2, y: 2, z: 4, core: 2. Of those that a mesh axis runs over, the one named last changes fastest.
Arguments:
- spectra: bfloat16 [4, 512, 2048], P('days', None, 'pairs'), may hold values from -6 to 6
- observed: bfloat16 [16, 64, 64, 128], P('pairs'), may hold values from -6 to 6
- pair_blocks: int32 [16, 2], replicated, may hold values from 0 to 7, as said below
- members: int32 [512], replicated, may hold values from 0 to 511, each once
- day_mask: int32 [16, 4], P('pairs'), may hold values from 0 to 1, as said below
Outputs:
- adjoint_spectra: float32 [4, 512, 2048], P('days', None, 'pairs')
Inputs may be any that keep to these rules, and one draw needn't show every extreme that they name: `pair_blocks`: each row holds two station block numbers, the first not above the second; no two rows are alike. `members`: every station appears once. `day_mask`: every listed pair is used on at least one day.
All inputs are finite; a program needn't handle non-finite values.
Results may differ from a plain program's by a relative error of at most 0.0025.
Values may be sent and summed in bfloat16 or wider, within the bound.
No kernel may reach another device: no remote copies, remote signals or barrier semaphores. Data moves between devices by JAX's collectives and lax.ppermute only.
A program may use at most 64 MiB of HBM per device.

v0:
```python
import math

import jax
import jax.numpy as jnp
from jax import lax
from jax.sharding import PartitionSpec as P

B = 64
F = 1024
L = 128
SLOTS = 2
DAYS_DEV = 1
NBLK = 8


def dft_tables():
    column = jnp.arange(2 * F, dtype=jnp.int32)
    frequency = column // 128 * 64 + column % 64
    part_of = column % 128 // 64
    lag_of = jnp.arange(L, dtype=jnp.int32) - L // 2
    phase_idx = frequency[:, None] * lag_of[None, :] % (2 * F)
    angles = jnp.float32(math.pi) * phase_idx.astype(jnp.float32) / F
    norm_scale = 1.0 / math.sqrt(F)
    cosine = jnp.cos(angles) * norm_scale
    sine_part = jnp.sin(angles) * norm_scale
    forward = jnp.where(part_of[:, None] == 0, cosine, -sine_part).astype(jnp.bfloat16)
    backward = jnp.where(part_of[:, None] == 0, cosine, sine_part).T.astype(jnp.bfloat16)
    return (forward, backward)


def hilbert_table():
    lag_rows = jnp.arange(L, dtype=jnp.int32)[:, None]
    lag_cols = jnp.arange(L, dtype=jnp.int32)[None, :]
    offset = (lag_cols - lag_rows) % L
    is_odd = offset % 2 == 1
    angles = jnp.float32(math.pi) * offset.astype(jnp.float32) / L
    safe_sin = jnp.where(is_odd, jnp.sin(angles), jnp.float32(1.0))
    return jnp.where(is_odd, 2.0 / L * jnp.cos(angles) / safe_sin, jnp.float32(0.0))


def weighted_residual(stacked, observed_f, hilbert):
    flat_s = stacked.reshape(-1, L)
    flat_o = observed_f.reshape(-1, L)
    hil_s = jnp.dot(
        flat_s, hilbert, precision=lax.Precision.HIGHEST, preferred_element_type=jnp.float32
    )
    hil_o = jnp.dot(
        flat_o, hilbert, precision=lax.Precision.HIGHEST, preferred_element_type=jnp.float32
    )
    env_s = jnp.sqrt(flat_s * flat_s + hil_s * hil_s)
    env_o = jnp.sqrt(flat_o * flat_o + hil_o * hil_o)
    weight = (1.0 + env_s) / (1.0 + env_s + env_o)
    return ((flat_s - flat_o) * weight).reshape(stacked.shape)


def tile_parts(spec_block, tile_idx):
    tile_piece = lax.dynamic_slice_in_dim(spec_block, tile_idx * 128, 128, 3).astype(jnp.float32)
    return (tile_piece[..., :64], tile_piece[..., 64:])


def body(spectra, observed, pair_blocks, members, day_mask):
    my_pair = lax.axis_index("pairs")
    my_day = lax.axis_index("days")
    stations = spectra.shape[1]
    n_tiles = 2 * F // 128
    forward, backward = dft_tables()
    backward_f = backward.astype(jnp.float32)
    hilbert = hilbert_table()
    offsets = jnp.arange(B, dtype=jnp.int32)
    my_blocks = lax.dynamic_slice_in_dim(pair_blocks, my_pair * SLOTS, SLOTS, 0)
    mask_here = lax.dynamic_slice_in_dim(day_mask, my_day * DAYS_DEV, DAYS_DEV, 1).astype(
        jnp.float32
    )
    day_count = jnp.sum(day_mask.astype(jnp.float32), axis=1)
    day_share = mask_here / day_count[:, None]
    gathered = lax.all_gather(spectra, "pairs", axis=2, tiled=True)
    my_rows = members[my_blocks[:, :, None] * B + offsets[None, None, :]].reshape(-1)
    arrived = jnp.take(gathered, my_rows, axis=1)
    arrived = arrived.reshape(DAYS_DEV, SLOTS, 2, B, 2 * F)
    side_a = arrived[:, :, 0]
    side_b = arrived[:, :, 1]
    day_weight = mask_here.T[:, :, None, None]

    def forward_tile(tile_idx, accum):
        a_real, a_imag = tile_parts(side_a, tile_idx)
        b_real, b_imag = tile_parts(side_b, tile_idx)
        masked_real = a_real * day_weight
        masked_imag = a_imag * day_weight
        cross_real = jnp.einsum("dsaj,dsbj->sabdj", masked_real, b_real) + jnp.einsum(
            "dsaj,dsbj->sabdj", masked_imag, b_imag
        )
        cross_imag = jnp.einsum("dsaj,dsbj->sabdj", masked_imag, b_real) - jnp.einsum(
            "dsaj,dsbj->sabdj", masked_real, b_imag
        )
        cross_tile = jnp.concatenate([cross_real, cross_imag], axis=-1).astype(jnp.bfloat16)
        cross_tile = cross_tile.reshape(SLOTS * B * B, DAYS_DEV * 128)
        table_rows = jnp.tile(
            lax.dynamic_slice_in_dim(forward, tile_idx * 128, 128, 0), (DAYS_DEV, 1)
        )
        return accum + jnp.dot(cross_tile, table_rows, preferred_element_type=jnp.float32)

    partial_value = lax.fori_loop(
        0, n_tiles, forward_tile, jnp.zeros((SLOTS * B * B, L), jnp.float32)
    )
    partial_value = partial_value.reshape(SLOTS, B, B, L)
    summed = lax.psum(partial_value, "days")
    residual = weighted_residual(
        summed / day_count[:, None, None, None], observed.astype(jnp.float32), hilbert
    )
    residual_flat = residual.reshape(SLOTS * B * B, L)
    share_weight = day_share.T[:, :, None, None]

    def adjoint_tile(tile_idx, contrib):
        cols_here = lax.dynamic_slice_in_dim(backward_f, tile_idx * 128, 128, 1)
        response = jnp.dot(
            residual_flat,
            cols_here,
            precision=lax.Precision.HIGHEST,
            preferred_element_type=jnp.float32,
        ).reshape(SLOTS, B, B, 128)
        g_cos = response[..., :64]
        g_sin = response[..., 64:]
        a_real, a_imag = tile_parts(side_a, tile_idx)
        b_real, b_imag = tile_parts(side_b, tile_idx)
        adj_a_real = jnp.einsum("sabj,dsbj->dsaj", g_cos, b_real) + jnp.einsum(
            "sabj,dsbj->dsaj", g_sin, b_imag
        )
        adj_a_imag = jnp.einsum("sabj,dsbj->dsaj", g_cos, b_imag) - jnp.einsum(
            "sabj,dsbj->dsaj", g_sin, b_real
        )
        adj_b_real = jnp.einsum("sabj,dsaj->dsbj", g_cos, a_real) - jnp.einsum(
            "sabj,dsaj->dsbj", g_sin, a_imag
        )
        adj_b_imag = jnp.einsum("sabj,dsaj->dsbj", g_cos, a_imag) + jnp.einsum(
            "sabj,dsaj->dsbj", g_sin, a_real
        )
        new_a = jnp.concatenate([adj_a_real, adj_a_imag], axis=-1) * share_weight
        new_b = jnp.concatenate([adj_b_real, adj_b_imag], axis=-1) * share_weight
        both_sides = jnp.stack([new_a, new_b], axis=2)
        return lax.dynamic_update_slice_in_dim(contrib, both_sides, tile_idx * 128, 4)

    contrib = lax.fori_loop(
        0, n_tiles, adjoint_tile, jnp.zeros((DAYS_DEV, SLOTS, 2, B, 2 * F), jnp.float32)
    )
    contrib = contrib.reshape(DAYS_DEV, 2 * SLOTS, B, 2 * F)
    block_ids = jnp.arange(NBLK, dtype=jnp.int32)[:, None]
    returned = lax.all_to_all(contrib, "pairs", split_axis=3, concat_axis=1, tiled=True)
    onehot = (block_ids == pair_blocks.reshape(-1)[None, :]).astype(jnp.float32)
    block_sum = jnp.einsum("nr,drbc->dnbc", onehot, returned, precision=lax.Precision.HIGHEST)
    flat_rows = block_sum.reshape(DAYS_DEV, NBLK * B, block_sum.shape[3])
    inverse = (
        jnp.zeros((stations,), jnp.int32).at[members].set(jnp.arange(stations, dtype=jnp.int32))
    )
    return jnp.take(flat_rows, inverse, axis=1)


def solution(mesh):
    return jax.shard_map(
        body,
        mesh=mesh,
        in_specs=(
            P("days", None, "pairs"),
            P("pairs", None, None, None),
            P(),
            P(),
            P("pairs", None),
        ),
        out_specs=P("days", None, "pairs"),
        check_vma=False,
    )
```

profile of v0, /device:TPU:0, one launch (start us, length us, event | category | flops | bytes accessed | tf_op | source)
XLA Modules:
  0.0 904.0 jit_solution(12786745865015730583)
XLA Ops:
  17.6 45.6 %all-gather.2.cloned.1.call-done = bf16[1,512,2048]{2,1,0:T(8,128)(2,1)} async-done(((bf16[1,512,256]{2,1,0:T(8,128)(2,1)}), bf16[1,512,2048]{2,1,0:T(8,128)(2,1)}) %all-gather.2.cloned.1.call-update) | async-done | bytes 2097168 | tf_op jit(solution)/shard_map/all_gather | solution.py:76
  72.4 254.9 %while.28 = (s32[]{:T(128)}, f32[8192,128]{1,0:T(8,128)}, bf16[1,2,64,2048]{2,1,3,0:T(2,128)(2,1)S(1)}, bf16[1,2,64,2048]{2,1,3,0:T(2,128)(2,1)S(1)}, f32[1,2,1,...) while((s32[]{:T(128)}, f32[8192,128]{1,0:T(8,128)}, ...), condition=%wide.region_2.3_spmd.clone, body=%wide.region_1.2_spmd.clone.sunk | while | flops 278970368 | bytes 25657664 | solution.py:102
  336.1 75.1 %all-reduce.2.cloned.1.call-done = f32[2,64,64,128]{3,2,1,0:T(8,128)} async-done(((f32[2,64,64,128]{3,2,1,0:T(8,128)}), f32[2,64,64,128]{3,2,1,0:T(8,128)}) %all-reduce.2.cloned.1.call-update) | async-done | bytes 4194320 | tf_op jit(solution)/shard_map/psum | solution.py:106
  425.0 380.9 %while.27 = (s32[]{:T(128)}, f32[1,2,2,64,2048]{4,3,2,1,0:T(8,128)S(1)}, bf16[1,2,64,2048]{3,2,1,0:T(8,128)(2,1)}, f32[128,2048]{1,0:T(8,128)S(1)}, f32[8192,128...) while((s32[]{:T(128)}, ...), condition=%wide.region_6.7_spmd, body=%wide.region_5.6_spmd.sunk | while | flops 1619099648 | bytes 43516140 | solution.py:142
  425.0 7.9 convolution_bitcast_fusion.3
  439.4 6.8 multiply_reduce_fusion.10
  448.6 8.1 convolution_bitcast_fusion.3
  463.3 6.8 multiply_reduce_fusion.10
  472.5 8.1 convolution_bitcast_fusion.3
  496.3 8.1 convolution_bitcast_fusion.3
  520.2 7.9 convolution_bitcast_fusion.3
  534.6 6.8 multiply_reduce_fusion.10
  543.9 8.1 convolution_bitcast_fusion.3
  558.4 6.8 multiply_reduce_fusion.10
  567.7 8.1 convolution_bitcast_fusion.3
  582.3 6.8 multiply_reduce_fusion.10
  591.5 8.1 convolution_bitcast_fusion.3
  606.1 6.8 multiply_reduce_fusion.10
  615.4 7.9 convolution_bitcast_fusion.3
  629.8 6.8 multiply_reduce_fusion.10
  639.1 8.1 convolution_bitcast_fusion.3
  653.7 6.8 multiply_reduce_fusion.10
  663.0 8.1 convolution_bitcast_fusion.3
  677.5 6.8 multiply_reduce_fusion.10
  686.8 8.1 convolution_bitcast_fusion.3
  710.7 7.9 convolution_bitcast_fusion.3
  734.4 8.1 convolution_bitcast_fusion.3
  758.2 8.1 convolution_bitcast_fusion.3
  782.0 8.1 convolution_bitcast_fusion.3
  810.3 7.9 reshape.493
  826.6 45.1 %all-to-all-done = f32[8,1,65536]{2,1,0:T(1,128)S(1)} async-done(((f32[8,1,65536]{2,1,0:T(1,128)}), f32[8,1,65536]{2,1,0:T(1,128)S(1)}, u32[]{:S(2)}, u32[]{:S(2)}) %all-to-all-start) | async-done | bytes 2097184 | tf_op jit(solution)/shard_map/all_to_all | solution.py:147
  873.6 7.2 reduce.16
  (488 shorter events, 516.1 us)
Async XLA Ops:
  6.5 56.7 %all-gather.2.cloned.1.call-start = ((), (), s32[]{:S(2)}) async-start(), calls=%async_computation.1 | async-start | bytes 2359296 | tf_op jit(solution)/shard_map/all_gather | solution.py:76
  7.3 403.9 %all-reduce.2.cloned.1.call-start = ((), (), s32[]{:S(2)}) async-start(), calls=%async_computation.2 | async-start | bytes 8388608 | tf_op jit(solution)/shard_map/psum | solution.py:106
  97.7 5.4 copy-start.4
  97.7 5.4 copy-start.6
  113.7 5.4 copy-start.4
  113.7 5.4 copy-start.6
  129.7 5.4 copy-start.6
  145.7 5.4 copy-start.6
  161.7 5.4 copy-start.4
  161.7 5.4 copy-start.6
  209.7 5.4 copy-start.6
  257.7 5.4 copy-start.6
  305.7 5.4 copy-start.6
  439.4 6.9 copy-start
  463.2 6.9 copy-start
  487.1 6.9 copy-start
  510.9 6.9 copy-start
  534.6 6.9 copy-start
  558.4 6.9 copy-start
  582.3 6.9 copy-start
  606.1 6.9 copy-start
  629.8 6.9 copy-start
  653.7 6.9 copy-start
  677.5 6.9 copy-start
  701.4 6.9 copy-start
  725.1 6.9 copy-start
  748.9 6.9 copy-start
  772.8 6.9 copy-start
  796.6 6.9 copy-start
  810.3 13.4 %copy-start.7 = (s32[16,2]{0,1:T(2,128)S(1)}, s32[16,2]{0,1:T(2,128)}, u32[]{:S(2)}) copy-start(s32[16,2]{0,1:T(2,128)} %param.11) | copy-start | bytes 388
  810.3 13.6 %copy-start.1 = (s32[512]{0:T(512)S(1)}, s32[512]{0:T(512)}, u32[]{:S(2)}) copy-start(s32[512]{0:T(512)} %param.12) | copy-start | bytes 6148
  818.1 53.6 %all-to-all-start = ((f32[8,1,65536]{2,1,0:T(1,128)}), f32[8,1,65536]{2,1,0:T(1,128)S(1)}, u32[]{:S(2)}, u32[]{:S(2)}) async-start(f32[8,1,65536]{2,1,0:T(1,128)} %reshape.493), calls=%async_computation | async-start | bytes 4194304 | tf_op jit(solution)/shard_map/all_to_all | solution.py:147
  (56 other events, 153.6 us)
Sparse Core Ops, SparseCore 0:
  9.4 53.7 all-gather.1
  327.4 83.6 all-reduce.1
where the time goes:
time: 915 us; the launch traced here: 904 us
  other arithmetic  245 us (27%)
  local copies, waits for them, and re-layouts  245 us (27%)
  matrix products  225 us (25%)
  waiting for transfers between devices  167 us (18%)
  between operations  14.1 us (2%)
    dot_general x16, matrix products, adjoint_tile(): jnp.dot(residual_flat, cols_here, precision=lax.Precision.HIGHEST, prefer...  129 us
    dot_general x16, other arithmetic, adjoint_tile(): jnp.einsum('sabj,dsbj->dsaj', g_sin, b_imag)  109 us
    concatenate x32, local copies, waits for them, and re-layouts, forward_tile(): jnp.concatenate([cross_real, cross_imag], axis=-1).astype(jnp.bfloat16)  93.1 us
    dot_general x16, local copies, waits for them, and re-layouts, adjoint_tile(): jnp.dot(residual_flat, cols_here, precision=lax.Precision.HIGHEST, prefer...  89 us
    dot_general x16, matrix products, forward_tile(): jnp.dot(cross_tile, table_rows, preferred_element_type=jnp.float32)  84.3 us
    psum x1, waiting for transfers between devices, body(): summed = lax.psum(partial_value, 'days')  75.1 us
    add x16, other arithmetic, forward_tile(): jnp.einsum('dsaj,dsbj->sabdj', masked_real, b_real)  55.9 us
    all_gather x1, waiting for transfers between devices, body(): gathered = lax.all_gather(spectra, 'pairs', axis=2, tiled=True)  45.6 us
  transfers between devices with their start and end apart: 3, of which 3 were waited for; matrix products, arithmetic and copies ran while one was open for 2% of the time, Pallas kernels for 0%

commit v1 on v0

v1 whole, which is shorter than its diff:
```python
import functools
import math

import jax
import jax.numpy as jnp
import ml_dtypes
import numpy as np
from jax import lax
from jax.experimental import pallas as pl
from jax.experimental.pallas import tpu as pltpu
from jax.sharding import Mesh, PartitionSpec as P

HALF = 64
TILE = 128
CORES = 2
F32 = jnp.float32
BF16 = jnp.bfloat16


def dft_tables(columns, lags):
    freqs = columns // 2
    column = np.arange(columns)
    frequency = column // TILE * HALF + column % HALF
    is_real = column % TILE < HALF
    phase = frequency[:, None] * (np.arange(lags) - lags // 2)[None, :] % (2 * freqs)
    angles = np.float32(math.pi) * phase.astype(np.float32) / np.float32(freqs)
    scale = np.float32(1.0 / math.sqrt(freqs))
    cosine = np.cos(angles) * scale
    sine = np.sin(angles) * scale
    forward = np.where(is_real[:, None], cosine, -sine).astype(ml_dtypes.bfloat16)
    backward = np.where(is_real[:, None], cosine, sine).T.astype(ml_dtypes.bfloat16)
    return forward, backward


def hilbert_parts(lags):
    offset = (np.arange(lags)[None, :] - np.arange(lags)[:, None]) % lags
    angles = np.float32(math.pi) * offset.astype(np.float32) / np.float32(lags)
    odd = offset % 2 == 1
    safe = np.where(odd, np.sin(angles), np.float32(1.0))
    table = np.where(odd, np.float32(2.0 / lags) * np.cos(angles) / safe, np.float32(0.0))
    table = table.astype(np.float32)
    high = table.astype(ml_dtypes.bfloat16)
    low = (table - high.astype(np.float32)).astype(ml_dtypes.bfloat16)
    return high, low


def left_lanes(shape):
    return lax.broadcasted_iota(jnp.int32, shape, len(shape) - 1) % TILE < HALF


def swap_halves(x):
    return pltpu.roll(x, HALF, 1)


def dot(a, b):
    return jnp.dot(a, b, preferred_element_type=F32)


def dot_split(x, high, low):
    x_high = x.astype(BF16)
    x_low = (x - x_high.astype(F32)).astype(BF16)
    return dot(x_high, high) + (dot(x_high, low) + dot(x_low, high))


def pack_kernel(blocks_ref, members_ref, spectra_ref, out_ref, ordered):
    stations = spectra_ref.shape[1]
    b = out_ref.shape[1] // 2
    station = lax.broadcasted_iota(jnp.int32, (stations, stations), 0)
    chosen = (station == members_ref[...]).astype(F32).astype(BF16)
    ordered[...] = lax.dot_general(
        chosen, spectra_ref[0], (((0,), (0,)), ((), ())), preferred_element_type=F32
    ).astype(BF16)
    for p in range(out_ref.shape[0]):
        for side in range(2):
            row = pl.multiple_of(blocks_ref[p, side] * b, b)
            out_ref[p, side * b:(side + 1) * b, :] = ordered[pl.ds(row, b), :]


def pack(pair_blocks, members, spectra, b):
    _, stations, cols = spectra.shape
    n_pairs = pair_blocks.shape[0]
    return pl.pallas_call(
        pack_kernel,
        out_shape=jax.ShapeDtypeStruct((n_pairs, 2 * b, cols), BF16),
        in_specs=[
            pl.BlockSpec(memory_space=pltpu.SMEM),
            pl.BlockSpec(memory_space=pltpu.VMEM),
            pl.BlockSpec(memory_space=pltpu.VMEM),
        ],
        out_specs=pl.BlockSpec(memory_space=pltpu.VMEM),
        scratch_shapes=[pltpu.VMEM((stations, cols), BF16)],
        compiler_params=pltpu.CompilerParams(vmem_limit_bytes=32 << 20),
        name="pack",
    )(pair_blocks, members, spectra)


def unpack_kernel(blocks_ref, members_ref, got_ref, out_ref, total):
    stations = out_ref.shape[1]
    b = got_ref.shape[1] // 2
    total[...] = jnp.zeros_like(total)
    for p in range(got_ref.shape[0]):
        for side in range(2):
            rows = pl.ds(pl.multiple_of(blocks_ref[p, side] * b, b), b)
            total[rows, :] += got_ref[p, side * b:(side + 1) * b, :].astype(F32)
    station = lax.broadcasted_iota(jnp.int32, (stations, stations), 0)
    chosen = (station == members_ref[...]).astype(F32).astype(BF16)
    whole = total[...]
    high = whole.astype(BF16)
    rest = whole - high.astype(F32)
    mid = rest.astype(BF16)
    low = (rest - mid.astype(F32)).astype(BF16)
    out_ref[0] = dot(chosen, high) + (dot(chosen, mid) + dot(chosen, low))


def unpack(pair_blocks, members, got, stations):
    cols = got.shape[2]
    return pl.pallas_call(
        unpack_kernel,
        out_shape=jax.ShapeDtypeStruct((1, stations, cols), F32),
        in_specs=[
            pl.BlockSpec(memory_space=pltpu.SMEM),
            pl.BlockSpec(memory_space=pltpu.VMEM),
            pl.BlockSpec(memory_space=pltpu.VMEM),
        ],
        out_specs=pl.BlockSpec(memory_space=pltpu.VMEM),
        scratch_shapes=[pltpu.VMEM((stations, cols), F32)],
        compiler_params=pltpu.CompilerParams(vmem_limit_bytes=32 << 20),
        name="unpack",
    )(pair_blocks, members, got)


def forward_kernel(b, group, mask_ref, got_ref, table_ref, out_ref, rows_one, rows_two, cols_one, cols_two):
    days = got_ref.shape[0]
    cols = got_ref.shape[2]
    lanes = left_lanes((b, TILE))
    sign = jnp.where(lanes, F32(1.0), F32(-1.0))

    @pl.when(pl.program_id(0) == 0)
    def _():
        out_ref[...] = jnp.zeros_like(out_ref)

    for d in range(days):
        for t in range(cols // TILE):
            at = slice((d * (cols // TILE) + t) * TILE, (d * (cols // TILE) + t + 1) * TILE)
            u_a = got_ref[d, :b, t * TILE:(t + 1) * TILE].astype(F32) * mask_ref[d]
            u_b = got_ref[d, b:, t * TILE:(t + 1) * TILE].astype(F32)
            v_a = swap_halves(u_a)
            v_b = swap_halves(u_b)
            rows_one[:, at] = u_a
            rows_two[:, at] = v_a * sign
            cols_one[:, at] = jnp.where(lanes, u_b, v_b)
            cols_two[:, at] = jnp.where(lanes, v_b, u_b)

    def some_rows(step, carry):
        first = pl.multiple_of(step * group, group)
        sums = jnp.zeros((group * b, out_ref.shape[1]), F32)
        for d in range(days):
            pieces = []
            for t in range(cols // TILE):
                at = slice((d * (cols // TILE) + t) * TILE, (d * (cols // TILE) + t + 1) * TILE)
                b_one = cols_one[:, at]
                b_two = cols_two[:, at]
                a_one = rows_one[pl.ds(first, group), at]
                a_two = rows_two[pl.ds(first, group), at]
                pieces.append(
                    jnp.concatenate(
                        [
                            (a_one[k:k + 1] * b_one + a_two[k:k + 1] * b_two).astype(BF16)
                            for k in range(group)
                        ],
                        axis=0,
                    )
                )
            cross = jnp.concatenate(pieces, axis=1)
            sums = sums + dot(cross, table_ref[...])
        at_rows = pl.ds(pl.multiple_of(first * b, group * b), group * b)
        out_ref[at_rows, :] += sums
        return carry

    lax.fori_loop(0, b // group, some_rows, 0)


def forward_pass(mask, got, table, b):
    shares, days, rows, cols = got.shape
    lags = table.shape[1]
    group = 8
    return pl.pallas_call(
        functools.partial(forward_kernel, b, group),
        out_shape=jax.ShapeDtypeStruct((b * b, lags), F32),
        grid=(shares,),
        in_specs=[
            pl.BlockSpec(memory_space=pltpu.SMEM),
            pl.BlockSpec((None, days, rows, cols), lambda s: (s, 0, 0, 0)),
            pl.BlockSpec((cols, lags), lambda s: (s, 0)),
        ],
        out_specs=pl.BlockSpec((b * b, lags), lambda s: (0, 0)),
        scratch_shapes=[pltpu.VMEM((b, days * cols), F32)] * 4,
        compiler_params=pltpu.CompilerParams(vmem_limit_bytes=40 << 20),
        name="forward",
    )(mask, got, table)


def adjoint_kernel(
    b, group, scalars_ref, slot_ref, mine_ref, other_ref, observed_ref, hil_high, hil_low, got_ref, table_ref,
    out_ref, residual, u_one, u_two, part_p, part_q, side_a, response,
):
    days = got_ref.shape[0]
    cols = got_ref.shape[2]
    lags = mine_ref.shape[1]
    tiles = cols // TILE
    chunk = group * b

    @pl.when(pl.program_id(0) == 0)
    def _():
        def some(step, carry):
            at = pl.ds(pl.multiple_of(step * chunk, chunk), chunk)
            stacked = (mine_ref[at, :] + other_ref[at, :]) / scalars_ref[days]
            seen = observed_ref[at, :]
            seen_f = seen.astype(F32)
            hil_s = dot_split(stacked, hil_high[...], hil_low[...])
            hil_o = dot(seen, hil_high[...]) + dot(seen, hil_low[...])
            env_s = jnp.sqrt(stacked * stacked + hil_s * hil_s)
            env_o = jnp.sqrt(seen_f * seen_f + hil_o * hil_o)
            value = (stacked - seen_f) * ((1.0 + env_s) / (1.0 + env_s + env_o))
            high = value.astype(BF16)
            residual[at, :lags] = high
            residual[at, lags:] = (value - high.astype(F32)).astype(BF16)
            return carry

        lax.fori_loop(0, b * b // chunk, some, 0)

    for d in range(days):
        for t in range(tiles):
            at = slice((d * tiles + t) * TILE, (d * tiles + t + 1) * TILE)
            u = got_ref[d, :, t * TILE:(t + 1) * TILE].astype(F32)
            u_one[:, at] = u
            u_two[:, at] = swap_halves(u)
    part_p[...] = jnp.zeros_like(part_p)
    part_q[...] = jnp.zeros_like(part_q)
    lanes = left_lanes((group, TILE))
    table_two = jnp.concatenate([table_ref[...], table_ref[...]], axis=0)

    def some_rows(step, carry):
        first = pl.multiple_of(step * group, group)
        at_rows = pl.ds(pl.multiple_of(first * b, chunk), chunk)
        response[...] = dot(residual[at_rows, :], table_two)
        for t in range(tiles):
            for d in range(days):
                at = slice((d * tiles + t) * TILE, (d * tiles + t + 1) * TILE)
                b_one = u_one[b:, at]
                b_two = u_two[b:, at]
                a_one = u_one[pl.ds(first, group), at]
                a_two = u_two[pl.ds(first, group), at]
                p_b = part_p[:, at]
                q_b = part_q[:, at]
                p_rows = []
                q_rows = []
                for k in range(group):
                    g = response[k * b:(k + 1) * b, t * TILE:(t + 1) * TILE]
                    p_rows.append(jnp.sum(g * b_one, axis=0, keepdims=True))
                    q_rows.append(jnp.sum(g * b_two, axis=0, keepdims=True))
                    p_b = p_b + g * a_one[k:k + 1]
                    q_b = q_b + g * a_two[k:k + 1]
                part_p[:, at] = p_b
                part_q[:, at] = q_b
                p_a = jnp.concatenate(p_rows, axis=0)
                q_a = jnp.concatenate(q_rows, axis=0)
                value = jnp.where(lanes, p_a + swap_halves(p_a), swap_halves(q_a) - q_a)
                side_a[pl.ds(first, group), at] = value * scalars_ref[d]
        return carry

    lax.fori_loop(0, b // group, some_rows, 0)
    lanes_b = left_lanes((b, TILE))
    for d in range(days):
        for t in range(tiles):
            at = slice((d * tiles + t) * TILE, (d * tiles + t + 1) * TILE)
            here = slice(t * TILE, (t + 1) * TILE)
            p_b = part_p[:, at]
            q_b = part_q[:, at]
            value = jnp.where(lanes_b, p_b - swap_halves(p_b), q_b + swap_halves(q_b))
            out_ref[d, :b, here] = side_a[:, at].astype(BF16)
            out_ref[d, b:, here] = (value * scalars_ref[d]).astype(BF16)


def adjoint_pass(scalars, slot, mine, other, observed, hil_high, hil_low, got, table):
    shares, days, rows, cols = got.shape
    b = rows // 2
    lags = mine.shape[1]
    group = 8
    whole = lambda s, slot_ref: (0, 0)
    spec = pltpu.PrefetchScalarGridSpec(
        num_scalar_prefetch=1,
        grid=(shares,),
        in_specs=[
            pl.BlockSpec(memory_space=pltpu.SMEM),
            pl.BlockSpec((b * b, lags), whole),
            pl.BlockSpec((b * b, lags), whole),
            pl.BlockSpec((None, b * b, lags), lambda s, slot_ref: (slot_ref[0], 0, 0)),
            pl.BlockSpec((lags, lags), whole),
            pl.BlockSpec((lags, lags), whole),
            pl.BlockSpec((None, days, rows, cols), lambda s, slot_ref: (s, 0, 0, 0)),
            pl.BlockSpec((lags, cols), lambda s, slot_ref: (0, s)),
        ],
        out_specs=pl.BlockSpec((None, days, rows, cols), lambda s, slot_ref: (s, 0, 0, 0)),
        scratch_shapes=[
            pltpu.VMEM((b * b, 2 * lags), BF16),
            pltpu.VMEM((rows, days * cols), F32),
            pltpu.VMEM((rows, days * cols), F32),
            pltpu.VMEM((b, days * cols), F32),
            pltpu.VMEM((b, days * cols), F32),
            pltpu.VMEM((b, days * cols), F32),
            pltpu.VMEM((group * b, cols), F32),
        ],
    )

    def kernel(slot_ref, scalars_ref, *refs):
        adjoint_kernel(b, group, scalars_ref, slot_ref, *refs)

    return pl.pallas_call(
        kernel,
        out_shape=jax.ShapeDtypeStruct(got.shape, BF16),
        grid_spec=spec,
        compiler_params=pltpu.CompilerParams(vmem_limit_bytes=48 << 20),
        name="adjoint",
    )(slot, scalars, mine, other, observed, hil_high, hil_low, got, table)


def body(spectra, observed, pair_blocks, members, day_mask):
    shares = lax.axis_size("pairs")
    slots, b, _, lags = observed.shape
    _, stations, cols = spectra.shape
    forward, backward = dft_tables(shares * cols, lags)
    hil_high, hil_low = hilbert_parts(lags)
    slot = lax.axis_index("slot")
    members = members.reshape(1, stations)
    first_day = lax.axis_index("outer") * slots * CORES + lax.axis_index("core")
    mask = lax.dynamic_slice_in_dim(day_mask, slot, 1, 0)[0].astype(F32)
    mask_here = jnp.stack([lax.dynamic_index_in_dim(mask, first_day + k * CORES, 0, False) for k in range(slots)])
    count = jnp.sum(mask)
    scalars = jnp.concatenate([mask_here / count, count[None]])

    sent = pack(pair_blocks, members, spectra, b)
    got = lax.all_to_all(sent, ("pairs", "slot"), 0, 0, tiled=True)
    got = got.reshape(shares, slots, 2 * b, cols)
    mine = forward_pass(mask_here, got, forward, b)
    for axis in ("outer", "core"):
        n = lax.axis_size(axis)
        others = [lax.ppermute(mine, axis, [(i, (i + k) % n) for i in range(n)]) for k in range(1, n)]
        if axis == "outer":
            for other in others:
                mine = mine + other
    contrib = adjoint_pass(
        scalars, slot[None], mine, others[0], observed.reshape(slots, b * b, lags), hil_high, hil_low, got, backward
    )
    returned = lax.all_to_all(
        contrib.reshape(shares * slots, 2 * b, cols), ("pairs", "slot"), 0, 0, tiled=True
    )
    return unpack(pair_blocks, members, returned, stations)


def solution(mesh):
    shares, days = mesh.devices.shape
    names = ("pairs", "outer", "slot", "core")

    def run(spectra, observed, pair_blocks, members, day_mask):
        slots = observed.shape[0] // shares
        split = (shares, days // CORES // slots, slots, CORES)
        finer = Mesh(mesh.devices.reshape(split), names)
        day_axes = names[1:]
        return jax.shard_map(
            body,
            mesh=finer,
            in_specs=(
                P(day_axes, None, "pairs"),
                P("pairs", None, None, None),
                P(),
                P(),
                P("pairs", None),
            ),
            out_specs=P(day_axes, None, "pairs"),
            check_vma=False,
        )(spectra, observed, pair_blocks, members, day_mask)

    return run
```

time: 915 us -> 142 us (0.16); the launches traced: 904 us -> 142 us
  other arithmetic: 245 us -> 3.46 us
  local copies, waits for them, and re-layouts: 245 us -> 4.48 us
  matrix products: 225 us -> 0 us
  waiting for transfers between devices: 167 us -> 24.3 us
  Pallas kernels: 0 us -> 68.9 us
  blocking collectives: 0 us -> 32.4 us
  between operations: 14.1 us -> 0.09 us
    dot_general x35 -> x0, matrix products: 225 us -> none  [the longest x16 129 us: adjoint_tile(): jnp.dot(residual_flat, cols_here, precision=lax.Precision.HIGHEST, prefer...]
    dot_general x32 -> x0, other arithmetic: 144 us -> none  [the longest x16 109 us: adjoint_tile(): jnp.einsum('sabj,dsbj->dsaj', g_sin, b_imag)]
    concatenate x32 -> x0, local copies, waits for them, and re-layouts: 93.1 us -> none  [forward_tile(): jnp.concatenate([cross_real, cross_imag], axis=-1).astype(jnp.bfloat16)]
    dot_general x16 -> x0, local copies, waits for them, and re-layouts: 89 us -> none  [adjoint_tile(): jnp.dot(residual_flat, cols_here, precision=lax.Precision.HIGHEST, prefer...]
    psum x1 -> x0, waiting for transfers between devices: 75.1 us -> none  [body(): summed = lax.psum(partial_value, 'days')]
    pallas_call x0 -> x4, Pallas kernels: none -> 68.9 us  [the longest x1 42 us: adjoint_pass(): pl.pallas_call(kernel, out_shape=jax.ShapeDtypeStruct(got.shape, BF16), g...]
    add x17 -> x0, other arithmetic: 55.9 us -> none  [the longest x16 55.9 us: forward_tile(): jnp.einsum('dsaj,dsbj->sabdj', masked_real, b_real)]
    all_gather x1 -> x0, waiting for transfers between devices: 45.6 us -> none  [body(): gathered = lax.all_gather(spectra, 'pairs', axis=2, tiled=True)]
  transfers between devices with their start and end apart: 3 -> 2, of which waited for: 3 -> 2; matrix products, arithmetic and copies ran while one was open for 2% -> 3% of each run, Pallas kernels for 0% -> 0%
where the time goes in v1:
time: 142 us
  Pallas kernels  68.9 us (49%)
  blocking collectives  32.4 us (23%)
  waiting for transfers between devices  24.3 us (17%)
  starting transfers between devices  8.39 us (6%)
  local copies, waits for them, and re-layouts  4.48 us (3%)
  other arithmetic  3.46 us (2%)
    pallas_call x1, Pallas kernels, adjoint_pass(): pl.pallas_call(kernel, out_shape=jax.ShapeDtypeStruct(got.shape, BF16), g...  42 us
    all_to_all x1, blocking collectives, body(): lax.all_to_all(contrib.reshape(shares * slots, 2 * b, cols), ('pairs', 's...  32.4 us
    pallas_call x1, Pallas kernels, forward_pass(): pl.pallas_call(functools.partial(forward_kernel, b, group), out_shape=jax...  22.4 us
    all_to_all x1, waiting for transfers between devices, body(): got = lax.all_to_all(sent, ('pairs', 'slot'), 0, 0, tiled=True)  20.9 us
    all_to_all x1, starting transfers between devices, body(): got = lax.all_to_all(sent, ('pairs', 'slot'), 0, 0, tiled=True)  8.32 us
    unnamed x19, local copies, waits for them, and re-layouts  3.81 us
    ppermute x1, waiting for transfers between devices, body(): lax.ppermute(mine, axis, [(i, (i + k) % n) for i in range(n)])  3.38 us
  transfers between devices with their start and end apart: 2, of which 2 were waited for; matrix products, arithmetic and copies ran while one was open for 3% of the time, Pallas kernels for 0%

profile of v1, /device:TPU:0, one launch (start us, length us, event | category | flops | bytes accessed | tf_op | source)
XLA Modules:
  0.0 141.9 jit_solution(5314264819637145414)
XLA Ops:
  0.0 0.0 copy-start.1
  0.0 0.8 copy.11.blocks_ref
  0.8 0.0 copy-start.2
  0.8 0.9 copy-done.2
  1.8 0.0 copy-start.5
  1.8 0.7 copy-done.5
  2.4 0.0 copy-start.8
  2.5 2.1 %pack.1 = bf16[16,128,256]{2,1,0:T(8,128)(2,1)} custom-call(s32[16,2]{1,0:T(8,128)S(1)} %copy.11.blocks_ref, s32[1,512]{1,0:T(1,128)S(1)} %bitcast.11, bf16[1,512,256]{2,1,0:T(8,128)(2,1)S(1)} %copy-done.2), custom_call_target="tpu_custom_call" | custom-call | tf_op jit(solution)/shard_map/pack/pallas_call | solution.py:82
  4.5 8.3 %all-to-all-start = ((bf16[16,128,256]{2,1,0:T(8,128)(2,1)}), bf16[16,128,256]{2,1,0:T(8,128)(2,1)S(1)}, u32[]{:S(2)}, u32[]{:S(2)}) async-start(bf16[16,128,256]{2,1,0:T(8,128)(2,1)} %pack.1), calls=%async_computation | async-start | bytes 2097152 | tf_op jit(solution)/shard_map/all_to_all | solution.py:343
  12.8 0.0 copy-start
  12.9 0.0 copy-start.3
  12.9 0.0 copy-start.4
  12.9 0.0 copy-done.8
  12.9 0.7 fusion.1
  13.6 0.7 constant_dynamic-slice_fusion.1
  14.2 2.0 %broadcast_divide_fusion = (f32[2]{0:T(128)S(1)}, f32[2]{0:T(128)S(1)}) fusion(f32[]{:T(128)} %get-tuple-element.7, f32[1]{0:T(128)} %bitcast.3, f32[1]{0:T(128)} %bitcast.2), kind=kLoop, calls=%fused_computation.6 | loop fusion | flops 4 | bytes 28 | tf_op jit(solution)/shard_map/div | solution.py:340
  16.3 20.9 %all-to-all-done = bf16[16,128,256]{2,1,0:T(8,128)(2,1)S(1)} async-done(((bf16[16,128,256]{2,1,0:T(8,128)(2,1)}), bf16[16,128,256]{2,1,0:T(8,128)(2,1)S(1)}, u32[]{:S(2)}, u32[]{:S(2)}) %all-to-all-start) | async-done | bytes 1048608 | tf_op jit(solution)/shard_map/all_to_all | solution.py:343
  37.2 0.0 copy-done.1
  37.2 22.4 %forward.1.refs_0_ = f32[4096,128]{1,0:T(8,128)S(1)} custom-call(f32[2]{0:T(128)S(1)} %get-tuple-element.6.mask_ref, bf16[8,2,128,256]{3,2,1,0:T(8,128)(2,1)S(1)} %bitcast.8, bf16[2048,128]{1,0:T(8,128)(2,1)S(1)} %copy-done.1), custom_call_target="tpu_custom_call" | custom-call | tf_op jit(solution)/shard_map/forward/pallas_call | solution.py:187
  59.5 0.1 collective-permute-start
  59.6 0.8 pad_maximum_fusion.1.scalars_ref
  60.4 3.4 %collective-permute-done.refs_1_ = f32[4096,128]{1,0:T(8,128)S(1)} collective-permute-done((f32[4096,128]{1,0:T(8,128)S(1)}, f32[4096,128]{1,0:T(8,128)S(1)}, u32[]{:S(2)}, u32[]{:S(2)}) %collective-permute-start) | collective-permute-done | bytes 2097184 | tf_op jit(solution)/shard_map/ppermute | solution.py:348
  63.8 0.0 copy-start.7
  63.8 1.3 copy-done.7
  65.1 0.0 copy-done
  65.1 0.0 copy-done.3
  65.1 0.0 copy-done.4
  65.1 42.0 %adjoint.1 = bf16[8,2,128,256]{3,2,1,0:T(8,128)(2,1)S(1)} custom-call(s32[1]{0:T(128)} %bitcast.1.slot_ref, f32[3]{0:T(128)S(1)} %pad_maximum_fusion.1.scalars_ref, f32[4096,128]{1,0:T(8,128)S(1)} %forward.1.refs_0_, f32[4096,128]{1,0:T(8,128)} %copy-done.7, bf16[2,4096,128]{2,1,0:T(8,128)(2,1)} %bitcast.13, bf16[128,128]{1,0:T(8,128)(2,1)S(1)} %copy-done.4, ...), custom_call_target="tpu_custom_call" | custom-call | tf_op jit(solution)/shard_map/adjoint/pallas_call | solution.py:319
  107.1 0.0 copy-start.6
  107.1 32.4 %all_to_all.10.got_ref = bf16[16,128,256]{2,1,0:T(8,128)(2,1)S(1)} all-to-all(bf16[16,128,256]{2,1,0:T(8,128)(2,1)S(1)} %bitcast.10), channel_id=1, replica_groups=mesh['pairs'=8,'outer'=1,'slot'=2,'core'=2] {'pairs','slot'}, dimensions={0} | all-to-all | bytes 2097152 | tf_op jit(solution)/shard_map/all_to_all | solution.py:355
  139.5 0.0 copy-done.6
  139.5 2.4 %unpack.1 = f32[1,512,256]{2,1,0:T(8,128)} custom-call(s32[16,2]{1,0:T(8,128)S(1)} %copy.11.blocks_ref, s32[1,512]{1,0:T(1,128)S(1)} %bitcast.12, bf16[16,128,256]{2,1,0:T(8,128)(2,1)S(1)} %all_to_all.10.got_ref), custom_call_target="tpu_custom_call" | custom-call | tf_op jit(solution)/shard_map/unpack/pallas_call | solution.py:117
Async XLA Ops:
  0.0 37.2 %copy-start.1 = (bf16[2048,128]{1,0:T(8,128)(2,1)S(1)}, bf16[2048,128]{1,0:T(8,128)(2,1)}, u32[]{:S(2)}) copy-start(bf16[2048,128]{1,0:T(8,128)(2,1)} %constant.37.clone.table_ref) | copy-start | bytes 1572868
  0.8 0.9 copy-start.2
  1.8 0.7 copy-start.5
  2.4 10.4 %copy-start.8 = (s32[2,4]{1,0:T(2,128)S(1)}, s32[2,4]{1,0:T(2,128)}, u32[]{:S(2)}) copy-start(s32[2,4]{1,0:T(2,128)} %param.13) | copy-start | bytes 100
  4.5 32.6 %all-to-all-start = ((bf16[16,128,256]{2,1,0:T(8,128)(2,1)}), bf16[16,128,256]{2,1,0:T(8,128)(2,1)S(1)}, u32[]{:S(2)}, u32[]{:S(2)}) async-start(bf16[16,128,256]{2,1,0:T(8,128)(2,1)} %pack.1), calls=%async_computation | async-start | bytes 2097152 | tf_op jit(solution)/shard_map/all_to_all | solution.py:343
  12.8 52.2 %copy-start = (bf16[128,2048]{1,0:T(8,128)(2,1)S(1)}, bf16[128,2048]{1,0:T(8,128)(2,1)}, u32[]{:S(2)}) copy-start(bf16[128,2048]{1,0:T(8,128)(2,1)} %constant.40.clone.refs_6_) | copy-start | bytes 1572868
  12.9 52.2 %copy-start.3 = (bf16[128,128]{1,0:T(8,128)(2,1)S(1)}, bf16[128,128]{1,0:T(8,128)(2,1)}, u32[]{:S(2)}) copy-start(bf16[128,128]{1,0:T(8,128)(2,1)} %constant.39.clone.refs_4_) | copy-start | bytes 98308
  12.9 52.2 %copy-start.4 = (bf16[128,128]{1,0:T(8,128)(2,1)S(1)}, bf16[128,128]{1,0:T(8,128)(2,1)}, u32[]{:S(2)}) copy-start(bf16[128,128]{1,0:T(8,128)(2,1)} %constant.38.clone.refs_3_) | copy-start | bytes 98308
  59.5 4.2 %collective-permute-start = (f32[4096,128]{1,0:T(8,128)S(1)}, f32[4096,128]{1,0:T(8,128)S(1)}, u32[]{:S(2)}, u32[]{:S(2)}) collective-permute-start(f32[4096,128]{1,0:T(8,128)S(1)} %forward.1.refs_0_), channel_id=1, source_target_pairs={{0,1},{1,0},{2,3},{3,2},{4,5},{5,4},{6,7},{7,6},{8,9},{9,8},{10,11... | collective-permute-start | bytes 6291464 | tf_op jit(solution)/shard_map/ppermute | solution.py:348
  63.8 1.3 copy-start.7
  107.1 32.4 %copy-start.6 = (s32[512]{0:T(512)S(1)}, s32[512]{0:T(512)}, u32[]{:S(2)}) copy-start(s32[512]{0:T(512)} %param.12) | copy-start | bytes 6148

commit v2 on v1

--- a/solution.py
+++ b/solution.py
@@ -17,7 +17,7 @@
 BF16 = jnp.bfloat16
 
 
-def dft_tables(columns, lags):
+def dft_table(columns, lags):
     freqs = columns // 2
     column = np.arange(columns)
     frequency = column // TILE * HALF + column % HALF
@@ -27,9 +27,7 @@
     scale = np.float32(1.0 / math.sqrt(freqs))
     cosine = np.cos(angles) * scale
     sine = np.sin(angles) * scale
-    forward = np.where(is_real[:, None], cosine, -sine).astype(ml_dtypes.bfloat16)
-    backward = np.where(is_real[:, None], cosine, sine).T.astype(ml_dtypes.bfloat16)
-    return forward, backward
+    return np.where(is_real[:, None], cosine, -sine).astype(ml_dtypes.bfloat16)
 
 
 def hilbert_parts(lags):
@@ -201,120 +199,151 @@
 
 
 def adjoint_kernel(
-    b, group, scalars_ref, slot_ref, mine_ref, other_ref, observed_ref, hil_high, hil_low, got_ref, table_ref,
-    out_ref, residual, u_one, u_two, part_p, part_q, side_a, response,
+    sizes, scalars_ref, slot_ref, mine_ref, other_ref, observed_ref, hil_high, hil_low, got_ref, fine_ref, coarse_ref,
+    out_ref, lagged, res_high, res_low, turned_a, turned_b, sums_a, sums_b,
 ):
-    days = got_ref.shape[0]
-    cols = got_ref.shape[2]
+    b, n_fine, n_coarse, scale = sizes
+    shares, days, _, cols = got_ref.shape
     lags = mine_ref.shape[1]
     tiles = cols // TILE
-    chunk = group * b
-
-    @pl.when(pl.program_id(0) == 0)
-    def _():
-        def some(step, carry):
-            at = pl.ds(pl.multiple_of(step * chunk, chunk), chunk)
-            stacked = (mine_ref[at, :] + other_ref[at, :]) / scalars_ref[days]
-            seen = observed_ref[at, :]
-            seen_f = seen.astype(F32)
-            hil_s = dot_split(stacked, hil_high[...], hil_low[...])
-            hil_o = dot(seen, hil_high[...]) + dot(seen, hil_low[...])
-            env_s = jnp.sqrt(stacked * stacked + hil_s * hil_s)
-            env_o = jnp.sqrt(seen_f * seen_f + hil_o * hil_o)
-            value = (stacked - seen_f) * ((1.0 + env_s) / (1.0 + env_s + env_o))
+    chunk = 8 * b
+    pieces = [(d, t) for d in range(days) for t in range(tiles)]
+
+    def lanes_of(d, t):
+        return slice((d * tiles + t) * TILE, (d * tiles + t + 1) * TILE)
+
+    def part(t):
+        return slice(t * TILE, (t + 1) * TILE)
+
+    def residual_rows(step, carry):
+        at = pl.ds(pl.multiple_of(step * chunk, chunk), chunk)
+        stacked = (mine_ref[at, :] + other_ref[at, :]) / scalars_ref[days]
+        seen = observed_ref[at, :]
+        seen_f = seen.astype(F32)
+        hil_s = dot_split(stacked, hil_high[...], hil_low[...])
+        hil_o = dot(seen, hil_high[...]) + dot(seen, hil_low[...])
+        env_s = jnp.sqrt(stacked * stacked + hil_s * hil_s)
+        env_o = jnp.sqrt(seen_f * seen_f + hil_o * hil_o)
+        value = (stacked - seen_f) * ((1.0 + env_s) / (1.0 + env_s + env_o))
+        for k in range(0, 8, 2):
+            flipped = value[k * b:(k + 2) * b, :].T
+            left = left_lanes((n_fine, 2 * b))
+            for two in range(n_coarse // 2):
+                even = flipped[2 * two * n_fine:(2 * two + 1) * n_fine, :]
+                odd = flipped[(2 * two + 1) * n_fine:(2 * two + 2) * n_fine, :]
+                first = jnp.where(left, even, swap_halves(odd))
+                second = jnp.where(left, swap_halves(even), odd)
+                lagged[two, pl.ds(step * 8 + k, n_fine, stride=b), :] = first
+                lagged[two, pl.ds(step * 8 + k + 1, n_fine, stride=b), :] = second
+        return carry
+
+    lax.fori_loop(0, b // 8, residual_rows, 0)
+
+    def split_rows(step, carry):
+        at = pl.ds(pl.multiple_of(step * b, b), b)
+        for two in range(n_coarse // 2):
+            value = lagged[two, at, :]
             high = value.astype(BF16)
-            residual[at, :lags] = high
-            residual[at, lags:] = (value - high.astype(F32)).astype(BF16)
-            return carry
-
-        lax.fori_loop(0, b * b // chunk, some, 0)
-
-    for d in range(days):
-        for t in range(tiles):
-            at = slice((d * tiles + t) * TILE, (d * tiles + t + 1) * TILE)
-            u = got_ref[d, :, t * TILE:(t + 1) * TILE].astype(F32)
-            u_one[:, at] = u
-            u_two[:, at] = swap_halves(u)
-    part_p[...] = jnp.zeros_like(part_p)
-    part_q[...] = jnp.zeros_like(part_q)
-    lanes = left_lanes((group, TILE))
-    table_two = jnp.concatenate([table_ref[...], table_ref[...]], axis=0)
-
-    def some_rows(step, carry):
-        first = pl.multiple_of(step * group, group)
-        at_rows = pl.ds(pl.multiple_of(first * b, chunk), chunk)
-        response[...] = dot(residual[at_rows, :], table_two)
-        for t in range(tiles):
-            for d in range(days):
-                at = slice((d * tiles + t) * TILE, (d * tiles + t + 1) * TILE)
-                b_one = u_one[b:, at]
-                b_two = u_two[b:, at]
-                a_one = u_one[pl.ds(first, group), at]
-                a_two = u_two[pl.ds(first, group), at]
-                p_b = part_p[:, at]
-                q_b = part_q[:, at]
-                p_rows = []
-                q_rows = []
-                for k in range(group):
-                    g = response[k * b:(k + 1) * b, t * TILE:(t + 1) * TILE]
-                    p_rows.append(jnp.sum(g * b_one, axis=0, keepdims=True))
-                    q_rows.append(jnp.sum(g * b_two, axis=0, keepdims=True))
-                    p_b = p_b + g * a_one[k:k + 1]
-                    q_b = q_b + g * a_two[k:k + 1]
-                part_p[:, at] = p_b
-                part_q[:, at] = q_b
-                p_a = jnp.concatenate(p_rows, axis=0)
-                q_a = jnp.concatenate(q_rows, axis=0)
-                value = jnp.where(lanes, p_a + swap_halves(p_a), swap_halves(q_a) - q_a)
-                side_a[pl.ds(first, group), at] = value * scalars_ref[d]
+            res_high[at, part(two)] = high
+            res_low[at, part(two)] = (value - high.astype(F32)).astype(BF16)
         return carry
 
-    lax.fori_loop(0, b // group, some_rows, 0)
-    lanes_b = left_lanes((b, TILE))
-    for d in range(days):
-        for t in range(tiles):
-            at = slice((d * tiles + t) * TILE, (d * tiles + t + 1) * TILE)
-            here = slice(t * TILE, (t + 1) * TILE)
-            p_b = part_p[:, at]
-            q_b = part_q[:, at]
-            value = jnp.where(lanes_b, p_b - swap_halves(p_b), q_b + swap_halves(q_b))
-            out_ref[d, :b, here] = side_a[:, at].astype(BF16)
-            out_ref[d, b:, here] = (value * scalars_ref[d]).astype(BF16)
-
-
-def adjoint_pass(scalars, slot, mine, other, observed, hil_high, hil_low, got, table):
+    lax.fori_loop(0, n_fine, split_rows, 0)
+
+    def turn(share, side, table, n, into):
+        for d, t in pieces:
+            u = got_ref[share, d, side * b:(side + 1) * b, part(t)].astype(F32)
+            v = swap_halves(u)
+            for k in range(n):
+                value = u * table[share, k:k + 1, part(t)] + v * table[share, n + k:n + k + 1, part(t)]
+                into[k * b:(k + 1) * b, lanes_of(d, t)] = value.astype(BF16)
+
+    def collect(share, side, table, n, sums):
+        for d, t in pieces:
+            p = jnp.zeros((b, TILE), F32)
+            q = jnp.zeros((b, TILE), F32)
+            for k in range(n):
+                h = sums[k * b:(k + 1) * b, lanes_of(d, t)]
+                p = p + h * table[share, k:k + 1, part(t)]
+                q = q + h * table[share, n + k:n + k + 1, part(t)]
+            value = (p + swap_halves(q)) * (scalars_ref[d] * scale)
+            out_ref[share, d, side * b:(side + 1) * b, part(t)] = value.astype(BF16)
+
+    turn(0, 1, coarse_ref, n_coarse, turned_b)
+    sums_b[...] = jnp.zeros_like(sums_b)
+    first_dim = (((0,), (0,)), ((), ()))
+
+    def one_share(share, carry):
+        sums_a[...] = dot(res_high[...], turned_b[...]) + dot(res_low[...], turned_b[...])
+        turn(share, 0, fine_ref, n_fine, turned_a)
+        collect(jnp.maximum(share - 1, 0), 1, coarse_ref, n_coarse, sums_b)
+        sums_b[...] = lax.dot_general(
+            res_high[...], turned_a[...], first_dim, preferred_element_type=F32
+        ) + lax.dot_general(res_low[...], turned_a[...], first_dim, preferred_element_type=F32)
+        collect(share, 0, fine_ref, n_fine, sums_a)
+        turn(jnp.minimum(share + 1, shares - 1), 1, coarse_ref, n_coarse, turned_b)
+        return carry
+
+    lax.fori_loop(0, shares, one_share, 0)
+    collect(shares - 1, 1, coarse_ref, n_coarse, sums_b)
+
+
+def turn_tables(columns, lags, shares):
+    freqs = columns // 2
+    n_fine = 16
+    n_coarse = lags // n_fine
+    column = np.arange(columns)
+    frequency = column // TILE * HALF + column % HALF
+    is_real = column % TILE < HALF
+
+    def table(steps, sign):
+        phase = frequency[None, :] * steps[:, None] % (2 * freqs)
+        angles = np.pi * phase / freqs
+        sine = np.where(is_real[None, :], -sign, sign) * np.sin(angles)
+        rows = np.concatenate([np.cos(angles), sine]).astype(np.float32)
+        return rows.reshape(rows.shape[0], shares, columns // shares).transpose(1, 0, 2)
+
+    fine = table(np.arange(n_fine), 1)
+    coarse = table(n_fine * np.arange(n_coarse) - lags // 2, -1)
+    return np.ascontiguousarray(fine), np.ascontiguousarray(coarse)
+
+
+def adjoint_pass(scalars, slot, mine, other, observed, hil_high, hil_low, got, fine, coarse):
     shares, days, rows, cols = got.shape
     b = rows // 2
     lags = mine.shape[1]
-    group = 8
-    whole = lambda s, slot_ref: (0, 0)
+    n_fine = fine.shape[1] // 2
+    n_coarse = coarse.shape[1] // 2
+    scale = 1.0 / math.sqrt(shares * cols // 2)
+    vmem = pl.BlockSpec(memory_space=pltpu.VMEM)
     spec = pltpu.PrefetchScalarGridSpec(
         num_scalar_prefetch=1,
-        grid=(shares,),
+        grid=(1,),
         in_specs=[
             pl.BlockSpec(memory_space=pltpu.SMEM),
-            pl.BlockSpec((b * b, lags), whole),
-            pl.BlockSpec((b * b, lags), whole),
+            vmem,
+            vmem,
             pl.BlockSpec((None, b * b, lags), lambda s, slot_ref: (slot_ref[0], 0, 0)),
-            pl.BlockSpec((lags, lags), whole),
-            pl.BlockSpec((lags, lags), whole),
-            pl.BlockSpec((None, days, rows, cols), lambda s, slot_ref: (s, 0, 0, 0)),
-            pl.BlockSpec((lags, cols), lambda s, slot_ref: (0, s)),
+            vmem,
+            vmem,
+            vmem,
+            vmem,
+            vmem,
         ],
-        out_specs=pl.BlockSpec((None, days, rows, cols), lambda s, slot_ref: (s, 0, 0, 0)),
+        out_specs=vmem,
         scratch_shapes=[
-            pltpu.VMEM((b * b, 2 * lags), BF16),
-            pltpu.VMEM((rows, days * cols), F32),
-            pltpu.VMEM((rows, days * cols), F32),
-            pltpu.VMEM((b, days * cols), F32),
-            pltpu.VMEM((b, days * cols), F32),
-            pltpu.VMEM((b, days * cols), F32),
-            pltpu.VMEM((group * b, cols), F32),
+            pltpu.VMEM((n_coarse // 2, n_fine * b, 2 * b), F32),
+            pltpu.VMEM((n_fine * b, n_coarse * b), BF16),
+            pltpu.VMEM((n_fine * b, n_coarse * b), BF16),
+            pltpu.VMEM((n_fine * b, days * cols), BF16),
+            pltpu.VMEM((n_coarse * b, days * cols), BF16),
+            pltpu.VMEM((n_fine * b, days * cols), F32),
+            pltpu.VMEM((n_coarse * b, days * cols), F32),
         ],
     )
 
     def kernel(slot_ref, scalars_ref, *refs):
-        adjoint_kernel(b, group, scalars_ref, slot_ref, *refs)
+        adjoint_kernel((b, n_fine, n_coarse, scale), scalars_ref, slot_ref, *refs)
 
     return pl.pallas_call(
         kernel,
@@ -322,14 +351,15 @@
         grid_spec=spec,
         compiler_params=pltpu.CompilerParams(vmem_limit_bytes=48 << 20),
         name="adjoint",
-    )(slot, scalars, mine, other, observed, hil_high, hil_low, got, table)
+    )(slot, scalars, mine, other, observed, hil_high, hil_low, got, fine, coarse)
 
 
 def body(spectra, observed, pair_blocks, members, day_mask):
     shares = lax.axis_size("pairs")
     slots, b, _, lags = observed.shape
     _, stations, cols = spectra.shape
-    forward, backward = dft_tables(shares * cols, lags)
+    forward = dft_table(shares * cols, lags)
+    fine, coarse = turn_tables(shares * cols, lags, shares)
     hil_high, hil_low = hilbert_parts(lags)
     slot = lax.axis_index("slot")
     members = members.reshape(1, stations)
@@ -350,7 +380,7 @@
             for other in others:
                 mine = mine + other
     contrib = adjoint_pass(
-        scalars, slot[None], mine, others[0], observed.reshape(slots, b * b, lags), hil_high, hil_low, got, backward
+        scalars, slot[None], mine, others[0], observed.reshape(slots, b * b, lags), hil_high, hil_low, got, fine, coarse
     )
     returned = lax.all_to_all(
         contrib.reshape(shares * slots, 2 * b, cols), ("pairs", "slot"), 0, 0, tiled=True

time: 142 us -> 132 us (0.930)
  Pallas kernels: 68.9 us -> 58.6 us
    pallas_call x1, Pallas kernels: 42 us -> 31.7 us  [adjoint_pass(): pl.pallas_call(kernel, out_shape=jax.ShapeDtypeStruct(got.shape, BF16), g...]
    unnamed x19 -> x21, local copies, waits for them, and re-layouts: 3.81 us -> 3.81 us
where the time goes in v2:
time: 132 us
  Pallas kernels  58.6 us (44%)
  blocking collectives  32.4 us (25%)
  waiting for transfers between devices  24.5 us (19%)
  starting transfers between devices  8.39 us (6%)
  local copies, waits for them, and re-layouts  4.47 us (3%)
  other arithmetic  3.2 us (2%)
    all_to_all x1, blocking collectives, body(): lax.all_to_all(contrib.reshape(shares * slots, 2 * b, cols), ('pairs', 's...  32.4 us
    pallas_call x1, Pallas kernels, adjoint_pass(): pl.pallas_call(kernel, out_shape=jax.ShapeDtypeStruct(got.shape, BF16), g...  31.7 us
    pallas_call x1, Pallas kernels, forward_pass(): pl.pallas_call(functools.partial(forward_kernel, b, group), out_shape=jax...  22.4 us
    all_to_all x1, waiting for transfers between devices, body(): got = lax.all_to_all(sent, ('pairs', 'slot'), 0, 0, tiled=True)  21 us
    all_to_all x1, starting transfers between devices, body(): got = lax.all_to_all(sent, ('pairs', 'slot'), 0, 0, tiled=True)  8.32 us
    unnamed x21, local copies, waits for them, and re-layouts  3.81 us
    ppermute x1, waiting for transfers between devices, body(): lax.ppermute(mine, axis, [(i, (i + k) % n) for i in range(n)])  3.5 us
  transfers between devices with their start and end apart: 2, of which 2 were waited for; matrix products, arithmetic and copies ran while one was open for 3% of the time, Pallas kernels for 0%

profile of v2, /device:TPU:0, one launch (start us, length us, event | category | flops | bytes accessed | tf_op | source)
XLA Modules:
  0.0 131.7 jit_solution(13007488586574079001)
XLA Ops:
  0.0 0.0 copy-start
  0.0 0.8 copy.12.blocks_ref
  0.8 0.0 copy-start.1
  0.8 0.9 copy-done.1
  1.8 0.0 copy-start.6
  1.8 0.7 copy-done.6
  2.5 2.1 %pack.1 = bf16[16,128,256]{2,1,0:T(8,128)(2,1)} custom-call(s32[16,2]{1,0:T(8,128)S(1)} %copy.12.blocks_ref, s32[1,512]{1,0:T(1,128)S(1)} %bitcast.11, bf16[1,512,256]{2,1,0:T(8,128)(2,1)S(1)} %copy-done.1), custom_call_target="tpu_custom_call" | custom-call | tf_op jit(solution)/shard_map/pack/pallas_call | solution.py:80
  4.5 8.3 %all-to-all-start = ((bf16[16,128,256]{2,1,0:T(8,128)(2,1)}), bf16[16,128,256]{2,1,0:T(8,128)(2,1)S(1)}, u32[]{:S(2)}, u32[]{:S(2)}) async-start(bf16[16,128,256]{2,1,0:T(8,128)(2,1)} %pack.1), calls=%async_computation | async-start | bytes 2097152 | tf_op jit(solution)/shard_map/all_to_all | solution.py:373
  12.8 0.0 copy-start.2
  12.9 0.0 copy-start.3
  12.9 0.0 copy-start.4
  12.9 0.0 copy-start.5
  12.9 0.0 copy-done.9
  12.9 0.6 fusion.1
  13.5 0.7 constant_dynamic-slice_fusion.1
  14.2 2.0 %broadcast_divide_fusion = (f32[2]{0:T(128)S(1)}, f32[2]{0:T(128)S(1)}) fusion(f32[]{:T(128)} %get-tuple-element.7, f32[1]{0:T(128)} %bitcast.3, f32[1]{0:T(128)} %bitcast.2), kind=kLoop, calls=%fused_computation.6 | loop fusion | flops 4 | bytes 28 | tf_op jit(solution)/shard_map/div | solution.py:370
  16.1 21.0 %all-to-all-done = bf16[16,128,256]{2,1,0:T(8,128)(2,1)S(1)} async-done(((bf16[16,128,256]{2,1,0:T(8,128)(2,1)}), bf16[16,128,256]{2,1,0:T(8,128)(2,1)S(1)}, u32[]{:S(2)}, u32[]{:S(2)}) %all-to-all-start) | async-done | bytes 1048608 | tf_op jit(solution)/shard_map/all_to_all | solution.py:373
  37.1 0.0 copy-done
  37.2 22.4 %forward.1.refs_0_ = f32[4096,128]{1,0:T(8,128)S(1)} custom-call(f32[2]{0:T(128)S(1)} %get-tuple-element.6.mask_ref, bf16[8,2,128,256]{3,2,1,0:T(8,128)(2,1)S(1)} %bitcast.8, bf16[2048,128]{1,0:T(8,128)(2,1)S(1)} %copy-done), custom_call_target="tpu_custom_call" | custom-call | tf_op jit(solution)/shard_map/forward/pallas_call | solution.py:185
  59.6 0.1 collective-permute-start
  59.6 0.6 pad_maximum_fusion.1.scalars_ref
  60.3 3.5 %collective-permute-done.refs_1_ = f32[4096,128]{1,0:T(8,128)S(1)} collective-permute-done((f32[4096,128]{1,0:T(8,128)S(1)}, f32[4096,128]{1,0:T(8,128)S(1)}, u32[]{:S(2)}, u32[]{:S(2)}) %collective-permute-start) | collective-permute-done | bytes 2097184 | tf_op jit(solution)/shard_map/ppermute | solution.py:378
  63.8 1.3 %copy-done.8 = f32[4096,128]{1,0:T(8,128)} copy-done((f32[4096,128]{1,0:T(8,128)}, f32[4096,128]{1,0:T(8,128)S(1)}, u32[]{:S(2)}) %copy-start.8) | copy-done | bytes 2097176
  65.1 0.0 copy-done.2
  65.1 0.0 copy-done.3
  65.1 0.0 copy-done.4
  65.1 0.0 copy-done.5
  65.1 31.7 %adjoint.1 = bf16[8,2,128,256]{3,2,1,0:T(8,128)(2,1)S(1)} custom-call(s32[1]{0:T(128)} %bitcast.1.slot_ref, f32[3]{0:T(128)S(1)} %pad_maximum_fusion.1.scalars_ref, f32[4096,128]{1,0:T(8,128)S(1)} %forward.1.refs_0_, f32[4096,128]{1,0:T(8,128)} %copy-done.8, bf16[2,4096,128]{2,1,0:T(8,128)(2,1)} %bitcast.13, bf16[128,128]{1,0:T(8,128)(2,1)S(1)} %copy-done.5, ...), custom_call_target="tpu_custom_call" | custom-call | tf_op jit(solution)/shard_map/adjoint/pallas_call | solution.py:348
  96.8 0.0 copy-start.7
  96.8 32.4 %all_to_all.10.got_ref = bf16[16,128,256]{2,1,0:T(8,128)(2,1)S(1)} all-to-all(bf16[16,128,256]{2,1,0:T(8,128)(2,1)S(1)} %bitcast.10), channel_id=1, replica_groups=mesh['pairs'=8,'outer'=1,'slot'=2,'core'=2] {'pairs','slot'}, dimensions={0} | all-to-all | bytes 2097152 | tf_op jit(solution)/shard_map/all_to_all | solution.py:385
  129.3 0.0 copy-done.7
  129.3 2.4 %unpack.1 = f32[1,512,256]{2,1,0:T(8,128)} custom-call(s32[16,2]{1,0:T(8,128)S(1)} %copy.12.blocks_ref, s32[1,512]{1,0:T(1,128)S(1)} %bitcast.12, bf16[16,128,256]{2,1,0:T(8,128)(2,1)S(1)} %all_to_all.10.got_ref), custom_call_target="tpu_custom_call" | custom-call | tf_op jit(solution)/shard_map/unpack/pallas_call | solution.py:115
  (2 shorter events, 0.0 us)
Async XLA Ops:
  0.0 37.1 %copy-start = (bf16[2048,128]{1,0:T(8,128)(2,1)S(1)}, bf16[2048,128]{1,0:T(8,128)(2,1)}, u32[]{:S(2)}) copy-start(bf16[2048,128]{1,0:T(8,128)(2,1)} %constant.39.clone.table_ref) | copy-start | bytes 1572868
  0.8 0.9 copy-start.1
  1.8 0.7 copy-start.6
  2.4 10.4 %copy-start.9 = (s32[2,4]{1,0:T(2,128)S(1)}, s32[2,4]{1,0:T(2,128)}, u32[]{:S(2)}) copy-start(s32[2,4]{1,0:T(2,128)} %param.14) | copy-start | bytes 100
  4.5 32.6 %all-to-all-start = ((bf16[16,128,256]{2,1,0:T(8,128)(2,1)}), bf16[16,128,256]{2,1,0:T(8,128)(2,1)S(1)}, u32[]{:S(2)}, u32[]{:S(2)}) async-start(bf16[16,128,256]{2,1,0:T(8,128)(2,1)} %pack.1), calls=%async_computation | async-start | bytes 2097152 | tf_op jit(solution)/shard_map/all_to_all | solution.py:373
  12.8 52.3 %copy-start.2 = (f32[8,32,256]{2,1,0:T(8,128)S(1)}, f32[8,32,256]{2,1,0:T(8,128)}, u32[]{:S(2)}) copy-start(f32[8,32,256]{2,1,0:T(8,128)} %constant.42.clone.refs_6_) | copy-start | bytes 786436
  12.9 52.3 %copy-start.3 = (f32[8,16,256]{2,1,0:T(8,128)S(1)}, f32[8,16,256]{2,1,0:T(8,128)}, u32[]{:S(2)}) copy-start(f32[8,16,256]{2,1,0:T(8,128)} %constant.43.clone.refs_7_) | copy-start | bytes 393220
  12.9 52.3 %copy-start.4 = (bf16[128,128]{1,0:T(8,128)(2,1)S(1)}, bf16[128,128]{1,0:T(8,128)(2,1)}, u32[]{:S(2)}) copy-start(bf16[128,128]{1,0:T(8,128)(2,1)} %constant.41.clone.refs_4_) | copy-start | bytes 98308
  12.9 52.3 %copy-start.5 = (bf16[128,128]{1,0:T(8,128)(2,1)S(1)}, bf16[128,128]{1,0:T(8,128)(2,1)}, u32[]{:S(2)}) copy-start(bf16[128,128]{1,0:T(8,128)(2,1)} %constant.40.clone.refs_3_) | copy-start | bytes 98308
  59.6 4.2 %collective-permute-start = (f32[4096,128]{1,0:T(8,128)S(1)}, f32[4096,128]{1,0:T(8,128)S(1)}, u32[]{:S(2)}, u32[]{:S(2)}) collective-permute-start(f32[4096,128]{1,0:T(8,128)S(1)} %forward.1.refs_0_), channel_id=1, source_target_pairs={{0,1},{1,0},{2,3},{3,2},{4,5},{5,4},{6,7},{7,6},{8,9},{9,8},{10,11... | collective-permute-start | bytes 6291464 | tf_op jit(solution)/shard_map/ppermute | solution.py:378
  63.8 1.3 %copy-start.8 = (f32[4096,128]{1,0:T(8,128)}, f32[4096,128]{1,0:T(8,128)S(1)}, u32[]{:S(2)}) copy-start(f32[4096,128]{1,0:T(8,128)S(1)} %collective-permute-done.refs_1_) | copy-start | bytes 6291460
  96.8 32.4 %copy-start.7 = (s32[512]{0:T(512)S(1)}, s32[512]{0:T(512)}, u32[]{:S(2)}) copy-start(s32[512]{0:T(512)} %param.13) | copy-start | bytes 6148

commit v3 on v2

--- a/solution.py
+++ b/solution.py
@@ -200,7 +200,7 @@
 
 def adjoint_kernel(
     sizes, scalars_ref, slot_ref, mine_ref, other_ref, observed_ref, hil_high, hil_low, got_ref, fine_ref, coarse_ref,
-    out_ref, lagged, res_high, res_low, turned_a, turned_b, sums_a, sums_b,
+    out_ref, lagged, res, res_t, turned_a, turned_b, sums_a, sums_b,
 ):
     b, n_fine, n_coarse, scale = sizes
     shares, days, _, cols = got_ref.shape
@@ -239,16 +239,15 @@
 
     lax.fori_loop(0, b // 8, residual_rows, 0)
 
-    def split_rows(step, carry):
-        at = pl.ds(pl.multiple_of(step * b, b), b)
+    def round_rows(step, carry):
+        at = pl.ds(pl.multiple_of(step * 2 * b, 2 * b), 2 * b)
         for two in range(n_coarse // 2):
             value = lagged[two, at, :]
-            high = value.astype(BF16)
-            res_high[at, part(two)] = high
-            res_low[at, part(two)] = (value - high.astype(F32)).astype(BF16)
+            res[at, part(two)] = value.astype(BF16)
+            res_t[part(two), at] = value.T.astype(BF16)
         return carry
 
-    lax.fori_loop(0, n_fine, split_rows, 0)
+    lax.fori_loop(0, n_fine // 2, round_rows, 0)
 
     def turn(share, side, table, n, into):
         for d, t in pieces:
@@ -271,15 +270,12 @@
 
     turn(0, 1, coarse_ref, n_coarse, turned_b)
     sums_b[...] = jnp.zeros_like(sums_b)
-    first_dim = (((0,), (0,)), ((), ()))
 
     def one_share(share, carry):
-        sums_a[...] = dot(res_high[...], turned_b[...]) + dot(res_low[...], turned_b[...])
+        sums_a[...] = dot(res[...], turned_b[...])
         turn(share, 0, fine_ref, n_fine, turned_a)
         collect(jnp.maximum(share - 1, 0), 1, coarse_ref, n_coarse, sums_b)
-        sums_b[...] = lax.dot_general(
-            res_high[...], turned_a[...], first_dim, preferred_element_type=F32
-        ) + lax.dot_general(res_low[...], turned_a[...], first_dim, preferred_element_type=F32)
+        sums_b[...] = dot(res_t[...], turned_a[...])
         collect(share, 0, fine_ref, n_fine, sums_a)
         turn(jnp.minimum(share + 1, shares - 1), 1, coarse_ref, n_coarse, turned_b)
         return carry
@@ -334,7 +330,7 @@
         scratch_shapes=[
             pltpu.VMEM((n_coarse // 2, n_fine * b, 2 * b), F32),
             pltpu.VMEM((n_fine * b, n_coarse * b), BF16),
-            pltpu.VMEM((n_fine * b, n_coarse * b), BF16),
+            pltpu.VMEM((n_coarse * b, n_fine * b), BF16),
             pltpu.VMEM((n_fine * b, days * cols), BF16),
             pltpu.VMEM((n_coarse * b, days * cols), BF16),
             pltpu.VMEM((n_fine * b, days * cols), F32),

time: 132 us -> 124 us (0.939)
  Pallas kernels: 58.6 us -> 50.8 us
    pallas_call x1, Pallas kernels: 31.7 us -> 24 us  [adjoint_pass(): pl.pallas_call(kernel, out_shape=jax.ShapeDtypeStruct(got.shape, BF16), g...]
where the time goes in v3:
time: 124 us
  Pallas kernels  50.8 us (41%)
  blocking collectives  32.5 us (26%)
  waiting for transfers between devices  24.5 us (20%)
  starting transfers between devices  8.39 us (7%)
  local copies, waits for them, and re-layouts  4.47 us (4%)
  other arithmetic  3.2 us (3%)
    all_to_all x1, blocking collectives, body(): lax.all_to_all(contrib.reshape(shares * slots, 2 * b, cols), ('pairs', 's...  32.5 us
    pallas_call x1, Pallas kernels, adjoint_pass(): pl.pallas_call(kernel, out_shape=jax.ShapeDtypeStruct(got.shape, BF16), g...  24 us
    pallas_call x1, Pallas kernels, forward_pass(): pl.pallas_call(functools.partial(forward_kernel, b, group), out_shape=jax...  22.4 us
    all_to_all x1, waiting for transfers between devices, body(): got = lax.all_to_all(sent, ('pairs', 'slot'), 0, 0, tiled=True)  21 us
    all_to_all x1, starting transfers between devices, body(): got = lax.all_to_all(sent, ('pairs', 'slot'), 0, 0, tiled=True)  8.32 us
    unnamed x21, local copies, waits for them, and re-layouts  3.81 us
    ppermute x1, waiting for transfers between devices, body(): lax.ppermute(mine, axis, [(i, (i + k) % n) for i in range(n)])  3.5 us
  transfers between devices with their start and end apart: 2, of which 2 were waited for; matrix products, arithmetic and copies ran while one was open for 3% of the time, Pallas kernels for 0%

profile of v3, /device:TPU:0, one launch (start us, length us, event | category | flops | bytes accessed | tf_op | source)
XLA Modules:
  0.0 124.0 jit_solution(15877083521240305889)
XLA Ops:
  0.0 0.0 copy-start
  0.0 0.8 copy.12.blocks_ref
  0.8 0.0 copy-start.1
  0.8 0.9 copy-done.1
  1.8 0.0 copy-start.6
  1.8 0.7 copy-done.6
  2.5 2.1 %pack.1 = bf16[16,128,256]{2,1,0:T(8,128)(2,1)} custom-call(s32[16,2]{1,0:T(8,128)S(1)} %copy.12.blocks_ref, s32[1,512]{1,0:T(1,128)S(1)} %bitcast.11, bf16[1,512,256]{2,1,0:T(8,128)(2,1)S(1)} %copy-done.1), custom_call_target="tpu_custom_call" | custom-call | tf_op jit(solution)/shard_map/pack/pallas_call | solution.py:80
  4.5 8.3 %all-to-all-start = ((bf16[16,128,256]{2,1,0:T(8,128)(2,1)}), bf16[16,128,256]{2,1,0:T(8,128)(2,1)S(1)}, u32[]{:S(2)}, u32[]{:S(2)}) async-start(bf16[16,128,256]{2,1,0:T(8,128)(2,1)} %pack.1), calls=%async_computation | async-start | bytes 2097152 | tf_op jit(solution)/shard_map/all_to_all | solution.py:369
  12.8 0.0 copy-start.2
  12.9 0.0 copy-start.3
  12.9 0.0 copy-start.4
  12.9 0.0 copy-start.5
  12.9 0.0 copy-done.9
  12.9 0.6 fusion.1
  13.5 0.7 constant_dynamic-slice_fusion.1
  14.2 2.0 %broadcast_divide_fusion = (f32[2]{0:T(128)S(1)}, f32[2]{0:T(128)S(1)}) fusion(f32[]{:T(128)} %get-tuple-element.7, f32[1]{0:T(128)} %bitcast.3, f32[1]{0:T(128)} %bitcast.2), kind=kLoop, calls=%fused_computation.6 | loop fusion | flops 4 | bytes 28 | tf_op jit(solution)/shard_map/div | solution.py:366
  16.1 21.0 %all-to-all-done = bf16[16,128,256]{2,1,0:T(8,128)(2,1)S(1)} async-done(((bf16[16,128,256]{2,1,0:T(8,128)(2,1)}), bf16[16,128,256]{2,1,0:T(8,128)(2,1)S(1)}, u32[]{:S(2)}, u32[]{:S(2)}) %all-to-all-start) | async-done | bytes 1048608 | tf_op jit(solution)/shard_map/all_to_all | solution.py:369
  37.1 0.0 copy-done
  37.2 22.4 %forward.1.refs_0_ = f32[4096,128]{1,0:T(8,128)S(1)} custom-call(f32[2]{0:T(128)S(1)} %get-tuple-element.6.mask_ref, bf16[8,2,128,256]{3,2,1,0:T(8,128)(2,1)S(1)} %bitcast.8, bf16[2048,128]{1,0:T(8,128)(2,1)S(1)} %copy-done), custom_call_target="tpu_custom_call" | custom-call | tf_op jit(solution)/shard_map/forward/pallas_call | solution.py:185
  59.5 0.1 collective-permute-start
  59.6 0.6 pad_maximum_fusion.1.scalars_ref
  60.3 3.5 %collective-permute-done.refs_1_ = f32[4096,128]{1,0:T(8,128)S(1)} collective-permute-done((f32[4096,128]{1,0:T(8,128)S(1)}, f32[4096,128]{1,0:T(8,128)S(1)}, u32[]{:S(2)}, u32[]{:S(2)}) %collective-permute-start) | collective-permute-done | bytes 2097184 | tf_op jit(solution)/shard_map/ppermute | solution.py:374
  63.8 1.3 %copy-done.8 = f32[4096,128]{1,0:T(8,128)} copy-done((f32[4096,128]{1,0:T(8,128)}, f32[4096,128]{1,0:T(8,128)S(1)}, u32[]{:S(2)}) %copy-start.8) | copy-done | bytes 2097176
  65.1 0.0 copy-done.2
  65.1 0.0 copy-done.3
  65.1 0.0 copy-done.4
  65.1 0.0 copy-done.5
  65.1 24.0 %adjoint.1 = bf16[8,2,128,256]{3,2,1,0:T(8,128)(2,1)S(1)} custom-call(s32[1]{0:T(128)} %bitcast.1.slot_ref, f32[3]{0:T(128)S(1)} %pad_maximum_fusion.1.scalars_ref, f32[4096,128]{1,0:T(8,128)S(1)} %forward.1.refs_0_, f32[4096,128]{1,0:T(8,128)} %copy-done.8, bf16[2,4096,128]{2,1,0:T(8,128)(2,1)} %bitcast.13, bf16[128,128]{1,0:T(8,128)(2,1)S(1)} %copy-done.5, ...), custom_call_target="tpu_custom_call" | custom-call | tf_op jit(solution)/shard_map/adjoint/pallas_call | solution.py:344
  89.1 0.0 copy-start.7
  89.1 32.5 %all_to_all.10.got_ref = bf16[16,128,256]{2,1,0:T(8,128)(2,1)S(1)} all-to-all(bf16[16,128,256]{2,1,0:T(8,128)(2,1)S(1)} %bitcast.10), channel_id=1, replica_groups=mesh['pairs'=8,'outer'=1,'slot'=2,'core'=2] {'pairs','slot'}, dimensions={0} | all-to-all | bytes 2097152 | tf_op jit(solution)/shard_map/all_to_all | solution.py:381
  121.5 0.0 copy-done.7
  121.5 2.4 %unpack.1 = f32[1,512,256]{2,1,0:T(8,128)} custom-call(s32[16,2]{1,0:T(8,128)S(1)} %copy.12.blocks_ref, s32[1,512]{1,0:T(1,128)S(1)} %bitcast.12, bf16[16,128,256]{2,1,0:T(8,128)(2,1)S(1)} %all_to_all.10.got_ref), custom_call_target="tpu_custom_call" | custom-call | tf_op jit(solution)/shard_map/unpack/pallas_call | solution.py:115
  (2 shorter events, 0.0 us)
Async XLA Ops:
  0.0 37.2 %copy-start = (bf16[2048,128]{1,0:T(8,128)(2,1)S(1)}, bf16[2048,128]{1,0:T(8,128)(2,1)}, u32[]{:S(2)}) copy-start(bf16[2048,128]{1,0:T(8,128)(2,1)} %constant.39.clone.table_ref) | copy-start | bytes 1572868
  0.8 0.9 copy-start.1
  1.8 0.7 copy-start.6
  2.4 10.4 %copy-start.9 = (s32[2,4]{1,0:T(2,128)S(1)}, s32[2,4]{1,0:T(2,128)}, u32[]{:S(2)}) copy-start(s32[2,4]{1,0:T(2,128)} %param.14) | copy-start | bytes 100
  4.5 32.6 %all-to-all-start = ((bf16[16,128,256]{2,1,0:T(8,128)(2,1)}), bf16[16,128,256]{2,1,0:T(8,128)(2,1)S(1)}, u32[]{:S(2)}, u32[]{:S(2)}) async-start(bf16[16,128,256]{2,1,0:T(8,128)(2,1)} %pack.1), calls=%async_computation | async-start | bytes 2097152 | tf_op jit(solution)/shard_map/all_to_all | solution.py:369
  12.8 52.3 %copy-start.2 = (f32[8,32,256]{2,1,0:T(8,128)S(1)}, f32[8,32,256]{2,1,0:T(8,128)}, u32[]{:S(2)}) copy-start(f32[8,32,256]{2,1,0:T(8,128)} %constant.42.clone.refs_6_) | copy-start | bytes 786436
  12.9 52.2 %copy-start.3 = (f32[8,16,256]{2,1,0:T(8,128)S(1)}, f32[8,16,256]{2,1,0:T(8,128)}, u32[]{:S(2)}) copy-start(f32[8,16,256]{2,1,0:T(8,128)} %constant.43.clone.refs_7_) | copy-start | bytes 393220
  12.9 52.2 %copy-start.4 = (bf16[128,128]{1,0:T(8,128)(2,1)S(1)}, bf16[128,128]{1,0:T(8,128)(2,1)}, u32[]{:S(2)}) copy-start(bf16[128,128]{1,0:T(8,128)(2,1)} %constant.41.clone.refs_4_) | copy-start | bytes 98308
  12.9 52.2 %copy-start.5 = (bf16[128,128]{1,0:T(8,128)(2,1)S(1)}, bf16[128,128]{1,0:T(8,128)(2,1)}, u32[]{:S(2)}) copy-start(bf16[128,128]{1,0:T(8,128)(2,1)} %constant.40.clone.refs_3_) | copy-start | bytes 98308
  59.5 4.2 %collective-permute-start = (f32[4096,128]{1,0:T(8,128)S(1)}, f32[4096,128]{1,0:T(8,128)S(1)}, u32[]{:S(2)}, u32[]{:S(2)}) collective-permute-start(f32[4096,128]{1,0:T(8,128)S(1)} %forward.1.refs_0_), channel_id=1, source_target_pairs={{0,1},{1,0},{2,3},{3,2},{4,5},{5,4},{6,7},{7,6},{8,9},{9,8},{10,11... | collective-permute-start | bytes 6291464 | tf_op jit(solution)/shard_map/ppermute | solution.py:374
  63.8 1.3 %copy-start.8 = (f32[4096,128]{1,0:T(8,128)}, f32[4096,128]{1,0:T(8,128)S(1)}, u32[]{:S(2)}) copy-start(f32[4096,128]{1,0:T(8,128)S(1)} %collective-permute-done.refs_1_) | copy-start | bytes 6291460
  89.1 32.5 %copy-start.7 = (s32[512]{0:T(512)S(1)}, s32[512]{0:T(512)}, u32[]{:S(2)}) copy-start(s32[512]{0:T(512)} %param.13) | copy-start | bytes 6148

commit v4 on v3

v4 whole, which is shorter than its diff:
```python
import functools
import math

import jax
import jax.numpy as jnp
import ml_dtypes
import numpy as np
from jax import lax
from jax.experimental import pallas as pl
from jax.experimental.pallas import tpu as pltpu
from jax.sharding import Mesh, PartitionSpec as P

HALF = 64
TILE = 128
CORES = 2
F32 = jnp.float32
BF16 = jnp.bfloat16


def hilbert_parts(lags):
    offset = (np.arange(lags)[None, :] - np.arange(lags)[:, None]) % lags
    angles = np.float32(math.pi) * offset.astype(np.float32) / np.float32(lags)
    odd = offset % 2 == 1
    safe = np.where(odd, np.sin(angles), np.float32(1.0))
    table = np.where(odd, np.float32(2.0 / lags) * np.cos(angles) / safe, np.float32(0.0))
    table = table.astype(np.float32).T
    high = table.astype(ml_dtypes.bfloat16)
    low = (table - high.astype(np.float32)).astype(ml_dtypes.bfloat16)
    return np.concatenate([high, low, high], axis=1)


def left_lanes(shape):
    return lax.broadcasted_iota(jnp.int32, shape, len(shape) - 1) % TILE < HALF


def swap_halves(x):
    return pltpu.roll(x, HALF, 1)


def dot(a, b):
    return jnp.dot(a, b, preferred_element_type=F32)


def pack_kernel(blocks_ref, members_ref, spectra_ref, out_ref, ordered):
    stations = spectra_ref.shape[1]
    b = out_ref.shape[1] // 2
    station = lax.broadcasted_iota(jnp.int32, (stations, stations), 0)
    chosen = (station == members_ref[...]).astype(F32).astype(BF16)
    ordered[...] = lax.dot_general(
        chosen, spectra_ref[0], (((0,), (0,)), ((), ())), preferred_element_type=F32
    ).astype(BF16)
    for p in range(out_ref.shape[0]):
        for side in range(2):
            row = pl.multiple_of(blocks_ref[p, side] * b, b)
            out_ref[p, side * b:(side + 1) * b, :] = ordered[pl.ds(row, b), :]


def pack(pair_blocks, members, spectra, b):
    _, stations, cols = spectra.shape
    n_pairs = pair_blocks.shape[0]
    return pl.pallas_call(
        pack_kernel,
        out_shape=jax.ShapeDtypeStruct((n_pairs, 2 * b, cols), BF16),
        in_specs=[
            pl.BlockSpec(memory_space=pltpu.SMEM),
            pl.BlockSpec(memory_space=pltpu.VMEM),
            pl.BlockSpec(memory_space=pltpu.VMEM),
        ],
        out_specs=pl.BlockSpec(memory_space=pltpu.VMEM),
        scratch_shapes=[pltpu.VMEM((stations, cols), BF16)],
        compiler_params=pltpu.CompilerParams(vmem_limit_bytes=32 << 20),
        name="pack",
    )(pair_blocks, members, spectra)


def unpack_kernel(blocks_ref, members_ref, got_ref, out_ref, total):
    stations = out_ref.shape[1]
    b = got_ref.shape[1] // 2
    total[...] = jnp.zeros_like(total)
    for p in range(got_ref.shape[0]):
        for side in range(2):
            rows = pl.ds(pl.multiple_of(blocks_ref[p, side] * b, b), b)
            total[rows, :] += got_ref[p, side * b:(side + 1) * b, :].astype(F32)
    station = lax.broadcasted_iota(jnp.int32, (stations, stations), 0)
    chosen = (station == members_ref[...]).astype(F32).astype(BF16)
    whole = total[...]
    high = whole.astype(BF16)
    rest = whole - high.astype(F32)
    mid = rest.astype(BF16)
    low = (rest - mid.astype(F32)).astype(BF16)
    out_ref[0] = dot(chosen, high) + (dot(chosen, mid) + dot(chosen, low))


def unpack(pair_blocks, members, got, stations):
    cols = got.shape[2]
    return pl.pallas_call(
        unpack_kernel,
        out_shape=jax.ShapeDtypeStruct((1, stations, cols), F32),
        in_specs=[
            pl.BlockSpec(memory_space=pltpu.SMEM),
            pl.BlockSpec(memory_space=pltpu.VMEM),
            pl.BlockSpec(memory_space=pltpu.VMEM),
        ],
        out_specs=pl.BlockSpec(memory_space=pltpu.VMEM),
        scratch_shapes=[pltpu.VMEM((stations, cols), F32)],
        compiler_params=pltpu.CompilerParams(vmem_limit_bytes=32 << 20),
        name="unpack",
    )(pair_blocks, members, got)


def prepare_kernel(b, slot_ref, observed_ref, hilbert_ref, seen_ref, env_ref):
    lags = observed_ref.shape[1]
    two = 2 * b

    def some(step, carry):
        seen = [
            observed_ref[pl.ds(pl.multiple_of((2 * step + k) * two, two), two), :].astype(F32).T for k in range(2)
        ]
        seen = jnp.concatenate(seen, axis=1)
        seen_b = seen.astype(BF16)
        hil = dot(hilbert_ref[:, :2 * lags], jnp.concatenate([seen_b, seen_b], axis=0))
        seen_ref[step] = seen_b
        env_ref[step] = 1.0 + jnp.sqrt(seen * seen + hil * hil)
        return carry

    lax.fori_loop(0, b // 4, some, 0, unroll=2)


def prepare(slot, observed, hilbert):
    _, rows, lags = observed.shape
    b = math.isqrt(rows)
    vmem = pl.BlockSpec(memory_space=pltpu.VMEM)
    spec = pltpu.PrefetchScalarGridSpec(
        num_scalar_prefetch=1,
        grid=(1,),
        in_specs=[pl.BlockSpec((None, rows, lags), lambda s, slot_ref: (slot_ref[0], 0, 0)), vmem],
        out_specs=[vmem, vmem],
    )
    shape = (b // 4, lags, 4 * b)
    return pl.pallas_call(
        functools.partial(prepare_kernel, b),
        out_shape=[jax.ShapeDtypeStruct(shape, BF16), jax.ShapeDtypeStruct(shape, F32)],
        grid_spec=spec,
        compiler_params=pltpu.CompilerParams(vmem_limit_bytes=16 << 20),
        cost_estimate=pl.CostEstimate(flops=2 * rows * lags * lags, bytes_accessed=8 * rows * lags, transcendentals=0),
        name="prepare",
    )(slot, observed, hilbert)


def tile_lanes(tiles, d, t):
    return slice((d * tiles + t) * TILE, (d * tiles + t + 1) * TILE)


def part(t):
    return slice(t * TILE, (t + 1) * TILE)


def forward_kernel(b, mask_ref, got_ref, fine_ref, coarse_ref, out_ref, turned_a, turned_b, masked):
    shares, days, _, cols = got_ref.shape
    tiles = cols // TILE
    n_fine = fine_ref.shape[1] // 2
    n_coarse = coarse_ref.shape[1] // 2
    slabs = out_ref.shape[0]
    out_ref[...] = jnp.zeros_like(out_ref)

    def turn(share, side, table, n, into):
        for d in range(days):
            for t in range(tiles):
                at = tile_lanes(tiles, d, t)
                u = got_ref[share, d, side * b:(side + 1) * b, part(t)].astype(F32)
                v = swap_halves(u)
                for k in range(n):
                    value = u * table[share, k:k + 1, part(t)] + v * table[share, n + k:n + k + 1, part(t)]
                    into[share, k * b:(k + 1) * b, at] = value.astype(BF16)

    def use(share):
        for d in range(days):
            at = slice(d * cols, (d + 1) * cols)
            masked[:, at] = turned_b[share, :, at] * mask_ref[d].astype(BF16)
        sums = lax.dot_general(
            turned_a[share], masked[...], (((1,), (1,)), ((), ())), preferred_element_type=F32
        )
        for k in range(slabs):
            out_ref[k] += sums[:, k * 2 * b:(k + 1) * 2 * b]

    turn(0, 1, coarse_ref, n_coarse, turned_b)
    turn(0, 0, fine_ref, n_fine, turned_a)

    def one_share(share, carry):
        use(share)
        turn(share + 1, 1, coarse_ref, n_coarse, turned_b)
        turn(share + 1, 0, fine_ref, n_fine, turned_a)
        return carry

    lax.fori_loop(0, shares - 1, one_share, 0)
    use(shares - 1)


def forward_pass(mask, got, fine, coarse):
    shares, days, rows, cols = got.shape
    b = rows // 2
    n_fine = fine.shape[1] // 2
    n_coarse = coarse.shape[1] // 2
    vmem = pl.BlockSpec(memory_space=pltpu.VMEM)
    return pl.pallas_call(
        functools.partial(forward_kernel, b),
        out_shape=[
            jax.ShapeDtypeStruct((n_coarse // 2, n_fine * b, 2 * b), F32),
            jax.ShapeDtypeStruct((shares, n_fine * b, days * cols), BF16),
            jax.ShapeDtypeStruct((shares, n_coarse * b, days * cols), BF16),
        ],
        in_specs=[pl.BlockSpec(memory_space=pltpu.SMEM), vmem, vmem, vmem],
        out_specs=[vmem] * 3,
        scratch_shapes=[pltpu.VMEM((n_coarse * b, days * cols), BF16)],
        compiler_params=pltpu.CompilerParams(vmem_limit_bytes=24 << 20),
        name="forward",
    )(mask, got, fine, coarse)


def adjoint_kernel(
    sizes, scalars_ref, mine_ref, other_ref, seen_ref, env_ref, hilbert_ref, turned_a, turned_b, fine_ref, coarse_ref,
    out_ref, lagged, res, res_t, sums_a, sums_b,
):
    b, scale = sizes
    shares, days, _, cols = out_ref.shape
    lags = seen_ref.shape[1]
    n_fine = fine_ref.shape[1] // 2
    n_coarse = coarse_ref.shape[1] // 2
    slabs = n_coarse // 2
    tiles = cols // TILE
    left = left_lanes((n_fine, 2 * b))

    def residual_rows(step, carry):
        halves = []
        for k in (0, 2):
            rows = []
            for slab in range(slabs):
                got = []
                for j in (0, 1):
                    at = pl.ds(4 * step + k + j, n_fine, stride=b)
                    got.append((mine_ref[slab, at, :] + other_ref[slab, at, :]) * scalars_ref[days])
                rows.append(jnp.where(left, got[0], swap_halves(got[1])))
                rows.append(jnp.where(left, swap_halves(got[0]), got[1]))
            halves.append(jnp.concatenate(rows, axis=0))
        stacked = jnp.concatenate(halves, axis=1)
        high = stacked.astype(BF16)
        low = (stacked - high.astype(F32)).astype(BF16)
        hil = dot(hilbert_ref[...], jnp.concatenate([high, high, low], axis=0))
        env_s = 1.0 + jnp.sqrt(stacked * stacked + hil * hil)
        env_o = env_ref[step]
        value = (stacked - seen_ref[step].astype(F32)) * (env_s / (env_s + env_o - 1.0))
        for k in (0, 2):
            lanes = slice(k * b, (k + 2) * b)
            for slab in range(slabs):
                even = value[2 * slab * n_fine:(2 * slab + 1) * n_fine, lanes]
                odd = value[(2 * slab + 1) * n_fine:(2 * slab + 2) * n_fine, lanes]
                first = jnp.where(left, even, swap_halves(odd))
                second = jnp.where(left, swap_halves(even), odd)
                lagged[slab, pl.ds(4 * step + k, n_fine, stride=b), :] = first
                lagged[slab, pl.ds(4 * step + k + 1, n_fine, stride=b), :] = second
        return carry

    lax.fori_loop(0, b // 4, residual_rows, 0, unroll=2)

    def round_rows(step, carry):
        at = pl.ds(pl.multiple_of(step * 2 * b, 2 * b), 2 * b)
        for slab in range(slabs):
            value = lagged[slab, at, :]
            here = slice(slab * 2 * b, (slab + 1) * 2 * b)
            res[at, here] = value.astype(BF16)
            res_t[here, at] = value.T.astype(BF16)
        return carry

    lax.fori_loop(0, n_fine // 2, round_rows, 0)

    def collect(share, side, table, n, sums):
        for d in range(days):
            for t in range(tiles):
                at = tile_lanes(tiles, d, t)
                p = jnp.zeros((b, TILE), F32)
                q = jnp.zeros((b, TILE), F32)
                for k in range(n):
                    h = sums[k * b:(k + 1) * b, at]
                    p = p + h * table[share, k:k + 1, part(t)]
                    q = q + h * table[share, n + k:n + k + 1, part(t)]
                value = (p + swap_halves(q)) * (scalars_ref[d] * scale)
                out_ref[share, d, side * b:(side + 1) * b, part(t)] = value.astype(BF16)

    sums_b[...] = jnp.zeros_like(sums_b)

    def one_share(share, carry):
        sums_a[...] = dot(res[...], turned_b[share])
        collect(jnp.maximum(share - 1, 0), 1, coarse_ref, n_coarse, sums_b)
        sums_b[...] = dot(res_t[...], turned_a[share])
        collect(share, 0, fine_ref, n_fine, sums_a)
        return carry

    lax.fori_loop(0, shares, one_share, 0)
    collect(shares - 1, 1, coarse_ref, n_coarse, sums_b)


def turn_tables(columns, lags, shares):
    freqs = columns // 2
    n_fine = 16
    n_coarse = lags // n_fine
    column = np.arange(columns)
    frequency = column // TILE * HALF + column % HALF
    is_real = column % TILE < HALF

    def table(steps, sign):
        phase = frequency[None, :] * steps[:, None] % (2 * freqs)
        angles = np.pi * phase / freqs
        sine = np.where(is_real[None, :], -sign, sign) * np.sin(angles)
        rows = np.concatenate([np.cos(angles), sine]).astype(np.float32)
        return rows.reshape(rows.shape[0], shares, columns // shares).transpose(1, 0, 2)

    fine = table(np.arange(n_fine), 1)
    coarse = table(n_fine * np.arange(n_coarse) - lags // 2, -1)
    return np.ascontiguousarray(fine), np.ascontiguousarray(coarse)


def adjoint_pass(scalars, mine, other, seen, env, hilbert, turned_a, turned_b, fine, coarse):
    shares, _, days_cols = turned_a.shape
    cols = fine.shape[2]
    n_fine = fine.shape[1] // 2
    n_coarse = coarse.shape[1] // 2
    b = turned_a.shape[1] // n_fine
    days = days_cols // cols
    scale = 1.0 / math.sqrt(shares * cols // 2)
    vmem = pl.BlockSpec(memory_space=pltpu.VMEM)
    return pl.pallas_call(
        functools.partial(adjoint_kernel, (b, scale)),
        out_shape=jax.ShapeDtypeStruct((shares, days, 2 * b, cols), BF16),
        in_specs=[pl.BlockSpec(memory_space=pltpu.SMEM)] + [vmem] * 9,
        out_specs=vmem,
        scratch_shapes=[
            pltpu.VMEM((n_coarse // 2, n_fine * b, 2 * b), F32),
            pltpu.VMEM((n_fine * b, n_coarse * b), BF16),
            pltpu.VMEM((n_coarse * b, n_fine * b), BF16),
            pltpu.VMEM((n_fine * b, days_cols), F32),
            pltpu.VMEM((n_coarse * b, days_cols), F32),
        ],
        compiler_params=pltpu.CompilerParams(vmem_limit_bytes=32 << 20),
        name="adjoint",
    )(scalars, mine, other, seen, env, hilbert, turned_a, turned_b, fine, coarse)


def body(spectra, observed, pair_blocks, members, day_mask):
    shares = lax.axis_size("pairs")
    slots, b, _, lags = observed.shape
    _, stations, cols = spectra.shape
    fine, coarse = turn_tables(shares * cols, lags, shares)
    hilbert = hilbert_parts(lags)
    slot = lax.axis_index("slot")
    members = members.reshape(1, stations)
    first_day = lax.axis_index("outer") * slots * CORES + lax.axis_index("core")
    mask = lax.dynamic_slice_in_dim(day_mask, slot, 1, 0)[0].astype(F32)
    mask_here = jnp.stack([lax.dynamic_index_in_dim(mask, first_day + k * CORES, 0, False) for k in range(slots)])
    count = jnp.sum(mask)
    scale = 1.0 / math.sqrt(shares * cols // 2)
    scalars = jnp.concatenate([mask_here / count, scale / count[None]])

    sent = pack(pair_blocks, members, spectra, b)
    got = lax.all_to_all(sent, ("pairs", "slot"), 0, 0, tiled=True)
    got = got.reshape(shares, slots, 2 * b, cols)
    seen, env = prepare(slot[None], observed.reshape(slots, b * b, lags), hilbert)
    mine, turned_a, turned_b = forward_pass(mask_here, got, fine, coarse)
    for axis in ("outer", "core"):
        n = lax.axis_size(axis)
        others = [lax.ppermute(mine, axis, [(i, (i + k) % n) for i in range(n)]) for k in range(1, n)]
        if axis == "outer":
            for other in others:
                mine = mine + other
    contrib = adjoint_pass(scalars, mine, others[0], seen, env, hilbert, turned_a, turned_b, fine, coarse)
    returned = lax.all_to_all(
        contrib.reshape(shares * slots, 2 * b, cols), ("pairs", "slot"), 0, 0, tiled=True
    )
    return unpack(pair_blocks, members, returned, stations)


def solution(mesh):
    shares, days = mesh.devices.shape
    names = ("pairs", "outer", "slot", "core")

    def run(spectra, observed, pair_blocks, members, day_mask):
        slots = observed.shape[0] // shares
        split = (shares, days // CORES // slots, slots, CORES)
        finer = Mesh(mesh.devices.reshape(split), names)
        day_axes = names[1:]
        return jax.shard_map(
            body,
            mesh=finer,
            in_specs=(
                P(day_axes, None, "pairs"),
                P("pairs", None, None, None),
                P(),
                P(),
                P("pairs", None),
            ),
            out_specs=P(day_axes, None, "pairs"),
            check_vma=False,
        )(spectra, observed, pair_blocks, members, day_mask)

    return run
```

time: 124 us -> 123 us (level)
  local copies, waits for them, and re-layouts: 4.47 us -> 17.2 us
  Pallas kernels: 50.8 us -> 40.2 us
  waiting for transfers between devices: 24.5 us -> 21 us
    unnamed x21 -> x27, local copies, waits for them, and re-layouts: 3.81 us -> 16.6 us
    pallas_call x2 -> x3, Pallas kernels: 46.3 us -> 35.7 us  [the longest x1 22.2 us: adjoint_pass(): pl.pallas_call(functools.partial(adjoint_kernel, (b, scale)), out_shape=j...]
    ppermute x1, waiting for transfers between devices: 3.5 us -> 0.01 us  [body(): lax.ppermute(mine, axis, [(i, (i + k) % n) for i in range(n)])]
  transfers between devices with their start and end apart: 2 -> 2, of which waited for: 2 -> 1; matrix products, arithmetic and copies ran while one was open for 3% -> 3% of each run, Pallas kernels for 0% -> 2%
where the time goes in v4:
time: 123 us
  Pallas kernels  40.2 us (33%)
  blocking collectives  32.4 us (26%)
  waiting for transfers between devices  21 us (17%)
  local copies, waits for them, and re-layouts  17.2 us (14%)
  starting transfers between devices  8.32 us (7%)
  other arithmetic  2.73 us (2%)
    all_to_all x1, blocking collectives, body(): lax.all_to_all(contrib.reshape(shares * slots, 2 * b, cols), ('pairs', 's...  32.4 us
    pallas_call x1, Pallas kernels, adjoint_pass(): pl.pallas_call(functools.partial(adjoint_kernel, (b, scale)), out_shape=j...  22.2 us
    all_to_all x1, waiting for transfers between devices, body(): got = lax.all_to_all(sent, ('pairs', 'slot'), 0, 0, tiled=True)  21 us
    unnamed x27, local copies, waits for them, and re-layouts  16.6 us
    pallas_call x1, Pallas kernels, forward_pass(): pl.pallas_call(functools.partial(forward_kernel, b), out_shape=[jax.Shape...  10.8 us
    all_to_all x1, starting transfers between devices, body(): got = lax.all_to_all(sent, ('pairs', 'slot'), 0, 0, tiled=True)  8.31 us
    pallas_call x1, Pallas kernels, prepare(): pl.pallas_call(functools.partial(prepare_kernel, b), out_shape=[jax.Shape...  2.72 us
  transfers between devices with their start and end apart: 2, of which 1 were waited for; matrix products, arithmetic and copies ran while one was open for 3% of the time, Pallas kernels for 2%

profile of v4, /device:TPU:0, one launch (start us, length us, event | category | flops | bytes accessed | tf_op | source)
XLA Modules:
  0.0 122.7 jit_solution(3123008174648779179)
XLA Ops:
  0.0 0.0 copy-start.6
  0.0 0.8 copy.10.blocks_ref
  0.8 0.9 copy-done.9
  1.8 0.7 copy-done.10
  2.4 2.1 %pack.1 = bf16[16,128,256]{2,1,0:T(8,128)(2,1)} custom-call(s32[16,2]{1,0:T(8,128)S(1)} %copy.10.blocks_ref, s32[1,512]{1,0:T(1,128)S(1)} %bitcast.11, bf16[1,512,256]{2,1,0:T(8,128)(2,1)S(1)} %copy-done.9), custom_call_target="tpu_custom_call" | custom-call | tf_op jit(solution)/shard_map/pack/pallas_call | solution.py:61
  4.5 8.3 %all-to-all-start = ((bf16[16,128,256]{2,1,0:T(8,128)(2,1)}), bf16[16,128,256]{2,1,0:T(8,128)(2,1)S(1)}, u32[]{:S(2)}, u32[]{:S(2)}) async-start(bf16[16,128,256]{2,1,0:T(8,128)(2,1)} %pack.1), calls=%async_computation | async-start | bytes 2097152 | tf_op jit(solution)/shard_map/all_to_all | solution.py:364
  12.8 0.0 copy-done.12
  12.9 0.7 fusion.1
  13.5 0.6 constant_dynamic-slice_fusion.1
  14.2 2.0 %broadcast_divide_fusion = (f32[2]{0:T(128)S(1)}, f32[2]{0:T(128)S(1)}) fusion(f32[]{:T(128)} %get-tuple-element.17, f32[1]{0:T(128)} %bitcast.2, f32[1]{0:T(128)} %bitcast.1), kind=kLoop, calls=%fused_computation.6 | loop fusion | flops 4 | bytes 28 | tf_op jit(solution)/shard_map/div | solution.py:361
  16.1 21.0 %all-to-all-done = bf16[16,128,256]{2,1,0:T(8,128)(2,1)S(1)} async-done(((bf16[16,128,256]{2,1,0:T(8,128)(2,1)}), bf16[16,128,256]{2,1,0:T(8,128)(2,1)S(1)}, u32[]{:S(2)}, u32[]{:S(2)}) %all-to-all-start) | async-done | bytes 1048608 | tf_op jit(solution)/shard_map/all_to_all | solution.py:364
  37.2 0.0 copy-done.6
  37.2 0.0 copy-done.5
  37.2 10.8 %forward.1 = (f32[4,1024,128]{2,1,0:T(8,128)S(1)}, bf16[8,1024,512]{2,1,0:T(8,128)(2,1)S(1)}, bf16[8,512,512]{2,1,0:T(8,128)(2,1)S(1)}) custom-call(f32[2]{0:T(128)S(1)} %get-tuple-element.16.mask_ref, bf16[8,2,128,256]{3,2,1,0:T(8,128)(2,1)S(1)} %bitcast.9, f32[8,32,256]{2,1,0:T(8,128)S(1)} %copy-done.5, f32[8,16,256]{2,1,0:T(8,128)S(1)} %copy-done.6), custom_call_target="tpu_custom_call" | custom-call | tf_op jit(solution)/shard_map/forward/pallas_call | solution.py:205
  48.0 0.0 copy-start
  48.0 3.2 %copy-done = bf16[8,1024,512]{2,1,0:T(8,128)(2,1)} copy-done((bf16[8,1024,512]{2,1,0:T(8,128)(2,1)}, bf16[8,1024,512]{2,1,0:T(8,128)(2,1)S(1)}, u32[]{:S(2)}) %copy-start) | copy-done | bytes 8388632
  51.2 2.0 %copy-done.2 = bf16[8,512,512]{2,1,0:T(8,128)(2,1)} copy-done((bf16[8,512,512]{2,1,0:T(8,128)(2,1)}, bf16[8,512,512]{2,1,0:T(8,128)(2,1)S(1)}, u32[]{:S(2)}) %copy-start.2) | copy-done | bytes 4194328
  53.2 0.0 collective-permute-start
  53.9 0.0 copy-start.4
  53.9 1.6 %copy-done.4 = bf16[2,64,64,128]{3,2,1,0:T(8,128)(2,1)S(1)} copy-done((bf16[2,64,64,128]{3,2,1,0:T(8,128)(2,1)S(1)}, bf16[2,64,64,128]{3,2,1,0:T(8,128)(2,1)}, u32[]{:S(2)}) %copy-start.4) | copy-done | bytes 2097176
  55.5 0.9 copy-done.7
  56.4 2.7 %prepare.1 = (bf16[16,128,256]{2,1,0:T(8,128)(2,1)S(1)}, f32[16,128,256]{2,1,0:T(8,128)S(1)}) custom-call(s32[1]{0:T(128)} %bitcast.5.slot_ref, bf16[2,4096,128]{2,1,0:T(8,128)(2,1)S(1)} %bitcast.10, bf16[128,384]{1,0:T(8,128)(2,1)S(1)} %copy-done.7), custom_call_target="tpu_custom_call" | custom-call | flops 134217728 | bytes 4194304 | tf_op jit(solution)/shard_map/prepare/pallas_call | solution.py:140
  59.1 0.1 pad_maximum_fusion.1.scalars_ref
  59.2 0.0 collective-permute-done.other_ref
  59.2 3.4 %copy-done.1 = bf16[8,1024,512]{2,1,0:T(8,128)(2,1)S(1)} copy-done((bf16[8,1024,512]{2,1,0:T(8,128)(2,1)S(1)}, bf16[8,1024,512]{2,1,0:T(8,128)(2,1)}, u32[]{:S(2)}) %copy-start.1) | copy-done | bytes 8388632
  62.6 2.2 %copy-done.3 = bf16[8,512,512]{2,1,0:T(8,128)(2,1)S(1)} copy-done((bf16[8,512,512]{2,1,0:T(8,128)(2,1)S(1)}, bf16[8,512,512]{2,1,0:T(8,128)(2,1)}, u32[]{:S(2)}) %copy-start.3) | copy-done | bytes 4194328
  64.8 0.9 copy-done.8
  65.7 22.2 %adjoint.1 = bf16[8,2,128,256]{3,2,1,0:T(8,128)(2,1)S(1)} custom-call(f32[3]{0:T(128)S(1)} %pad_maximum_fusion.1.scalars_ref, f32[4,1024,128]{2,1,0:T(8,128)S(1)} %get-tuple-element.10.mine_ref, f32[4,1024,128]{2,1,0:T(8,128)} %collective-permute-done.other_ref, bf16[16,128,256]{2,1,0:T(8,128)(2,1)S(1)} %get-tuple-element.11.seen_ref, ...), custom_call_target="tpu_custom_call" | custom-call | tf_op jit(solution)/shard_map/adjoint/pallas_call | solution.py:331
  87.8 0.0 copy-start.11
  87.8 32.4 %all_to_all.10.got_ref = bf16[16,128,256]{2,1,0:T(8,128)(2,1)S(1)} all-to-all(bf16[16,128,256]{2,1,0:T(8,128)(2,1)S(1)} %bitcast.8), channel_id=1, replica_groups=mesh['pairs'=8,'outer'=1,'slot'=2,'core'=2] {'pairs','slot'}, dimensions={0} | all-to-all | bytes 2097152 | tf_op jit(solution)/shard_map/all_to_all | solution.py:375
  120.3 0.0 copy-done.11
  120.3 2.4 %unpack.1 = f32[1,512,256]{2,1,0:T(8,128)} custom-call(s32[16,2]{1,0:T(8,128)S(1)} %copy.10.blocks_ref, s32[1,512]{1,0:T(1,128)S(1)} %bitcast.12, bf16[16,128,256]{2,1,0:T(8,128)(2,1)S(1)} %all_to_all.10.got_ref), custom_call_target="tpu_custom_call" | custom-call | tf_op jit(solution)/shard_map/unpack/pallas_call | solution.py:96
  (9 shorter events, 0.0 us)
Async XLA Ops:
  0.0 37.2 %copy-start.6 = (f32[8,16,256]{2,1,0:T(8,128)S(1)}, f32[8,16,256]{2,1,0:T(8,128)}, u32[]{:S(2)}) copy-start(f32[8,16,256]{2,1,0:T(8,128)} %constant.40.clone.coarse_ref) | copy-start | bytes 393220
  0.0 37.2 %copy-start.5 = (f32[8,32,256]{2,1,0:T(8,128)S(1)}, f32[8,32,256]{2,1,0:T(8,128)}, u32[]{:S(2)}) copy-start(f32[8,32,256]{2,1,0:T(8,128)} %constant.39.clone.fine_ref) | copy-start | bytes 786436
  0.8 0.9 copy-start.9
  1.8 0.7 copy-start.10
  2.4 10.4 %copy-start.12 = (s32[2,4]{1,0:T(2,128)S(1)}, s32[2,4]{1,0:T(2,128)}, u32[]{:S(2)}) copy-start(s32[2,4]{1,0:T(2,128)} %param.12) | copy-start | bytes 100
  4.5 32.6 %all-to-all-start = ((bf16[16,128,256]{2,1,0:T(8,128)(2,1)}), bf16[16,128,256]{2,1,0:T(8,128)(2,1)S(1)}, u32[]{:S(2)}, u32[]{:S(2)}) async-start(bf16[16,128,256]{2,1,0:T(8,128)(2,1)} %pack.1), calls=%async_computation | async-start | bytes 2097152 | tf_op jit(solution)/shard_map/all_to_all | solution.py:364
  48.0 3.2 %copy-start = (bf16[8,1024,512]{2,1,0:T(8,128)(2,1)}, bf16[8,1024,512]{2,1,0:T(8,128)(2,1)S(1)}, u32[]{:S(2)}) copy-start(bf16[8,1024,512]{2,1,0:T(8,128)(2,1)S(1)} %get-tuple-element.13.turned_a) | copy-start | bytes 25165828
  51.2 2.0 %copy-start.2 = (bf16[8,512,512]{2,1,0:T(8,128)(2,1)}, bf16[8,512,512]{2,1,0:T(8,128)(2,1)S(1)}, u32[]{:S(2)}) copy-start(bf16[8,512,512]{2,1,0:T(8,128)(2,1)S(1)} %get-tuple-element.14.turned_b) | copy-start | bytes 12582916
  53.2 6.0 %collective-permute-start = (f32[4,1024,128]{2,1,0:T(8,128)S(1)}, f32[4,1024,128]{2,1,0:T(8,128)}, u32[]{:S(2)}, u32[]{:S(2)}) collective-permute-start(f32[4,1024,128]{2,1,0:T(8,128)S(1)} %get-tuple-element.10.mine_ref), channel_id=1, source_target_pairs={{0,1},{1,0},{2,3},{3,2},{4,5},{5,4},{6,7},{7,6},{8,9},{9,8},{10,11... | collective-permute-start | bytes 6291464 | tf_op jit(solution)/shard_map/ppermute | solution.py:370
  53.9 1.6 %copy-start.4 = (bf16[2,64,64,128]{3,2,1,0:T(8,128)(2,1)S(1)}, bf16[2,64,64,128]{3,2,1,0:T(8,128)(2,1)}, u32[]{:S(2)}) copy-start(bf16[2,64,64,128]{3,2,1,0:T(8,128)(2,1)} %param.9) | copy-start | bytes 6291460
  55.5 0.9 copy-start.7
  59.2 3.4 %copy-start.1 = (bf16[8,1024,512]{2,1,0:T(8,128)(2,1)S(1)}, bf16[8,1024,512]{2,1,0:T(8,128)(2,1)}, u32[]{:S(2)}) copy-start(bf16[8,1024,512]{2,1,0:T(8,128)(2,1)} %copy-done) | copy-start | bytes 25165828
  62.6 2.2 %copy-start.3 = (bf16[8,512,512]{2,1,0:T(8,128)(2,1)S(1)}, bf16[8,512,512]{2,1,0:T(8,128)(2,1)}, u32[]{:S(2)}) copy-start(bf16[8,512,512]{2,1,0:T(8,128)(2,1)} %copy-done.2) | copy-start | bytes 12582916
  64.8 0.9 copy-start.8
  87.8 32.4 %copy-start.11 = (s32[512]{0:T(512)S(1)}, s32[512]{0:T(512)}, u32[]{:S(2)}) copy-start(s32[512]{0:T(512)} %param.11) | copy-start | bytes 6148

commit v5 on v4

--- a/solution.py
+++ b/solution.py
@@ -139,7 +139,7 @@
     shape = (b // 4, lags, 4 * b)
     return pl.pallas_call(
         functools.partial(prepare_kernel, b),
-        out_shape=[jax.ShapeDtypeStruct(shape, BF16), jax.ShapeDtypeStruct(shape, F32)],
+        out_shape=[pltpu.VMEM(shape, BF16), pltpu.VMEM(shape, F32)],
         grid_spec=spec,
         compiler_params=pltpu.CompilerParams(vmem_limit_bytes=16 << 20),
         cost_estimate=pl.CostEstimate(flops=2 * rows * lags * lags, bytes_accessed=8 * rows * lags, transcendentals=0),
@@ -155,45 +155,69 @@
     return slice(t * TILE, (t + 1) * TILE)
 
 
-def forward_kernel(b, mask_ref, got_ref, fine_ref, coarse_ref, out_ref, turned_a, turned_b, masked):
+def forward_kernel(
+    b, mask_ref, got_ref, fine_ref, coarse_ref, out_ref, kept_a, kept_b, turned_a, turned_b, rows_u, rows_v, sems_a, sems_b
+):
     shares, days, _, cols = got_ref.shape
     tiles = cols // TILE
     n_fine = fine_ref.shape[1] // 2
     n_coarse = coarse_ref.shape[1] // 2
-    slabs = out_ref.shape[0]
+    pieces = [(d, t) for d in range(days) for t in range(tiles)]
     out_ref[...] = jnp.zeros_like(out_ref)
 
-    def turn(share, side, table, n, into):
-        for d in range(days):
-            for t in range(tiles):
-                at = tile_lanes(tiles, d, t)
-                u = got_ref[share, d, side * b:(side + 1) * b, part(t)].astype(F32)
-                v = swap_halves(u)
-                for k in range(n):
-                    value = u * table[share, k:k + 1, part(t)] + v * table[share, n + k:n + k + 1, part(t)]
-                    into[share, k * b:(k + 1) * b, at] = value.astype(BF16)
+    def make(share):
+        for d, t in pieces:
+            at = tile_lanes(tiles, d, t)
+            u = got_ref[share, d, b:, part(t)].astype(F32)
+            v = swap_halves(u)
+            for k in range(n_coarse):
+                cosine = coarse_ref[share, k:k + 1, part(t)]
+                sine = coarse_ref[share, n_coarse + k:n_coarse + k + 1, part(t)]
+                turned_b[share, k * b:(k + 1) * b, at] = (u * cosine + v * sine).astype(BF16)
+        for d, t in pieces:
+            at = tile_lanes(tiles, d, t)
+            u = got_ref[share, d, :b, part(t)].astype(F32) * mask_ref[d]
+            rows_u[:, at] = u
+            rows_v[:, at] = swap_halves(u)
+        for d, t in pieces:
+            at = tile_lanes(tiles, d, t)
+            cosine = fine_ref[share, :n_fine, part(t)]
+            sine = fine_ref[share, n_fine:, part(t)]
+            for k in range(b):
+                value = rows_u[k:k + 1, at] * cosine + rows_v[k:k + 1, at] * sine
+                turned_a[share, k * n_fine:(k + 1) * n_fine, at] = value.astype(BF16)
 
     def use(share):
-        for d in range(days):
-            at = slice(d * cols, (d + 1) * cols)
-            masked[:, at] = turned_b[share, :, at] * mask_ref[d].astype(BF16)
-        sums = lax.dot_general(
-            turned_a[share], masked[...], (((1,), (1,)), ((), ())), preferred_element_type=F32
+        out_ref[...] += lax.dot_general(
+            turned_a[share], turned_b[share], (((1,), (1,)), ((), ())), preferred_element_type=F32
         )
-        for k in range(slabs):
-            out_ref[k] += sums[:, k * 2 * b:(k + 1) * 2 * b]
-
-    turn(0, 1, coarse_ref, n_coarse, turned_b)
-    turn(0, 0, fine_ref, n_fine, turned_a)
+
+    def keep(share):
+        return (
+            pltpu.make_async_copy(turned_a.at[share], kept_a.at[share], sems_a.at[share]),
+            pltpu.make_async_copy(turned_b.at[share], kept_b.at[share], sems_b.at[share]),
+        )
+
+    make(0)
 
     def one_share(share, carry):
+        for copy in keep(share):
+            copy.start()
         use(share)
-        turn(share + 1, 1, coarse_ref, n_coarse, turned_b)
-        turn(share + 1, 0, fine_ref, n_fine, turned_a)
+        make(share + 1)
         return carry
 
     lax.fori_loop(0, shares - 1, one_share, 0)
+    for copy in keep(shares - 1):
+        copy.start()
     use(shares - 1)
+
+    def finish(share, carry):
+        for copy in keep(share):
+            copy.wait()
+        return carry
+
+    lax.fori_loop(0, shares, finish, 0)
 
 
 def forward_pass(mask, got, fine, coarse):
@@ -205,73 +229,98 @@
     return pl.pallas_call(
         functools.partial(forward_kernel, b),
         out_shape=[
-            jax.ShapeDtypeStruct((n_coarse // 2, n_fine * b, 2 * b), F32),
-            jax.ShapeDtypeStruct((shares, n_fine * b, days * cols), BF16),
-            jax.ShapeDtypeStruct((shares, n_coarse * b, days * cols), BF16),
+            jax.ShapeDtypeStruct((n_fine * b, n_coarse * b), F32),
+            pltpu.HBM((shares, n_fine * b, days * cols), BF16),
+            pltpu.HBM((shares, n_coarse * b, days * cols), BF16),
         ],
         in_specs=[pl.BlockSpec(memory_space=pltpu.SMEM), vmem, vmem, vmem],
-        out_specs=[vmem] * 3,
-        scratch_shapes=[pltpu.VMEM((n_coarse * b, days * cols), BF16)],
-        compiler_params=pltpu.CompilerParams(vmem_limit_bytes=24 << 20),
+        out_specs=[vmem] + [pl.BlockSpec(memory_space=pltpu.HBM)] * 2,
+        scratch_shapes=[
+            pltpu.VMEM((shares, n_fine * b, days * cols), BF16),
+            pltpu.VMEM((shares, n_coarse * b, days * cols), BF16),
+            pltpu.VMEM((b, days * cols), F32),
+            pltpu.VMEM((b, days * cols), F32),
+            pltpu.SemaphoreType.DMA((shares,)),
+            pltpu.SemaphoreType.DMA((shares,)),
+        ],
+        compiler_params=pltpu.CompilerParams(vmem_limit_bytes=28 << 20),
         name="forward",
     )(mask, got, fine, coarse)
 
 
 def adjoint_kernel(
-    sizes, scalars_ref, mine_ref, other_ref, seen_ref, env_ref, hilbert_ref, turned_a, turned_b, fine_ref, coarse_ref,
-    out_ref, lagged, res, res_t, sums_a, sums_b,
+    sizes, scalars_ref, mine_ref, other_ref, seen_ref, env_ref, hilbert_ref, kept_a, kept_b, fine_ref, coarse_ref,
+    out_ref, lagged, back, res, res_t, sums_a, sums_b, turned_a, turned_b, sems_a, sems_b,
 ):
     b, scale = sizes
     shares, days, _, cols = out_ref.shape
-    lags = seen_ref.shape[1]
     n_fine = fine_ref.shape[1] // 2
     n_coarse = coarse_ref.shape[1] // 2
     slabs = n_coarse // 2
     tiles = cols // TILE
+    group = 8
+    block = group * n_fine
     left = left_lanes((n_fine, 2 * b))
 
+    def fetch(share):
+        return (
+            pltpu.make_async_copy(kept_b.at[share], turned_b.at[share], sems_b.at[share]),
+            pltpu.make_async_copy(kept_a.at[share], turned_a.at[share], sems_a.at[share]),
+        )
+
+    def begin(share, carry):
+        for copy in fetch(share):
+            copy.start()
+        return carry
+
+    lax.fori_loop(0, shares, begin, 0)
+
     def residual_rows(step, carry):
-        halves = []
-        for k in (0, 2):
-            rows = []
-            for slab in range(slabs):
-                got = []
-                for j in (0, 1):
-                    at = pl.ds(4 * step + k + j, n_fine, stride=b)
-                    got.append((mine_ref[slab, at, :] + other_ref[slab, at, :]) * scalars_ref[days])
-                rows.append(jnp.where(left, got[0], swap_halves(got[1])))
-                rows.append(jnp.where(left, swap_halves(got[0]), got[1]))
-            halves.append(jnp.concatenate(rows, axis=0))
-        stacked = jnp.concatenate(halves, axis=1)
-        high = stacked.astype(BF16)
-        low = (stacked - high.astype(F32)).astype(BF16)
-        hil = dot(hilbert_ref[...], jnp.concatenate([high, high, low], axis=0))
-        env_s = 1.0 + jnp.sqrt(stacked * stacked + hil * hil)
-        env_o = env_ref[step]
-        value = (stacked - seen_ref[step].astype(F32)) * (env_s / (env_s + env_o - 1.0))
-        for k in (0, 2):
-            lanes = slice(k * b, (k + 2) * b)
-            for slab in range(slabs):
-                even = value[2 * slab * n_fine:(2 * slab + 1) * n_fine, lanes]
-                odd = value[(2 * slab + 1) * n_fine:(2 * slab + 2) * n_fine, lanes]
-                first = jnp.where(left, even, swap_halves(odd))
-                second = jnp.where(left, swap_halves(even), odd)
-                lagged[slab, pl.ds(4 * step + k, n_fine, stride=b), :] = first
-                lagged[slab, pl.ds(4 * step + k + 1, n_fine, stride=b), :] = second
-        return carry
-
-    lax.fori_loop(0, b // 4, residual_rows, 0, unroll=2)
+        for quad in range(group // 4):
+            stacked = []
+            for two in (0, 2):
+                rows = []
+                for slab in range(slabs):
+                    got = []
+                    for k in (two, two + 1):
+                        at = pl.ds(pl.multiple_of(step * block + (4 * quad + k) * n_fine, n_fine), n_fine)
+                        got.append((mine_ref[at, part(slab)] + other_ref[at, part(slab)]) * scalars_ref[days])
+                    rows.append(jnp.where(left, got[0], swap_halves(got[1])))
+                    rows.append(jnp.where(left, swap_halves(got[0]), got[1]))
+                stacked.append(jnp.concatenate(rows, axis=0))
+            stacked = jnp.concatenate(stacked, axis=1)
+            high = stacked.astype(BF16)
+            low = (stacked - high.astype(F32)).astype(BF16)
+            hil = dot(hilbert_ref[...], jnp.concatenate([high, high, low], axis=0))
+            env_s = 1.0 + jnp.sqrt(stacked * stacked + hil * hil)
+            env_o = env_ref[2 * step + quad]
+            value = (stacked - seen_ref[2 * step + quad].astype(F32)) * (env_s / (env_s + env_o - 1.0))
+            for two in (0, 2):
+                lanes = slice(two * b, (two + 2) * b)
+                for slab in range(slabs):
+                    even = value[2 * slab * n_fine:(2 * slab + 1) * n_fine, lanes]
+                    odd = value[(2 * slab + 1) * n_fine:(2 * slab + 2) * n_fine, lanes]
+                    first = jnp.where(left, even, swap_halves(odd))
+                    second = jnp.where(left, swap_halves(even), odd)
+                    for k, rows in ((0, first), (1, second)):
+                        a = step * group + 4 * quad + two + k
+                        lagged[slab, pl.ds(a, n_fine, stride=b), :] = rows
+                        at = (4 * quad + two + k) * n_fine
+                        back[at:at + n_fine, part(slab)] = rows
+        at = pl.ds(pl.multiple_of(step * block, block), block)
+        for slab in range(slabs):
+            res_t[part(slab), at] = back[:, part(slab)].T.astype(BF16)
+        return carry
+
+    lax.fori_loop(0, b // group, residual_rows, 0)
 
     def round_rows(step, carry):
-        at = pl.ds(pl.multiple_of(step * 2 * b, 2 * b), 2 * b)
+        at = pl.ds(pl.multiple_of(step * b, b), b)
         for slab in range(slabs):
-            value = lagged[slab, at, :]
-            here = slice(slab * 2 * b, (slab + 1) * 2 * b)
-            res[at, here] = value.astype(BF16)
-            res_t[here, at] = value.T.astype(BF16)
-        return carry
-
-    lax.fori_loop(0, n_fine // 2, round_rows, 0)
+            res[at, part(slab)] = lagged[slab, at, :].astype(BF16)
+        return carry
+
+    lax.fori_loop(0, n_fine, round_rows, 0)
 
     def collect(share, side, table, n, sums):
         for d in range(days):
@@ -289,6 +338,8 @@
     sums_b[...] = jnp.zeros_like(sums_b)
 
     def one_share(share, carry):
+        for copy in fetch(share):
+            copy.wait()
         sums_a[...] = dot(res[...], turned_b[share])
         collect(jnp.maximum(share - 1, 0), 1, coarse_ref, n_coarse, sums_b)
         sums_b[...] = dot(res_t[...], turned_a[share])
@@ -328,19 +379,27 @@
     days = days_cols // cols
     scale = 1.0 / math.sqrt(shares * cols // 2)
     vmem = pl.BlockSpec(memory_space=pltpu.VMEM)
+    hbm = pl.BlockSpec(memory_space=pltpu.HBM)
+    turned_a = pltpu.with_memory_space_constraint(turned_a, pltpu.HBM)
+    turned_b = pltpu.with_memory_space_constraint(turned_b, pltpu.HBM)
     return pl.pallas_call(
         functools.partial(adjoint_kernel, (b, scale)),
         out_shape=jax.ShapeDtypeStruct((shares, days, 2 * b, cols), BF16),
-        in_specs=[pl.BlockSpec(memory_space=pltpu.SMEM)] + [vmem] * 9,
+        in_specs=[pl.BlockSpec(memory_space=pltpu.SMEM)] + [vmem] * 5 + [hbm] * 2 + [vmem] * 2,
         out_specs=vmem,
         scratch_shapes=[
             pltpu.VMEM((n_coarse // 2, n_fine * b, 2 * b), F32),
+            pltpu.VMEM((8 * n_fine, n_coarse * b), F32),
             pltpu.VMEM((n_fine * b, n_coarse * b), BF16),
             pltpu.VMEM((n_coarse * b, n_fine * b), BF16),
             pltpu.VMEM((n_fine * b, days_cols), F32),
             pltpu.VMEM((n_coarse * b, days_cols), F32),
+            pltpu.VMEM(turned_a.shape, BF16),
+            pltpu.VMEM(turned_b.shape, BF16),
+            pltpu.SemaphoreType.DMA((shares,)),
+            pltpu.SemaphoreType.DMA((shares,)),
         ],
-        compiler_params=pltpu.CompilerParams(vmem_limit_bytes=32 << 20),
+        compiler_params=pltpu.CompilerParams(vmem_limit_bytes=36 << 20),
         name="adjoint",
     )(scalars, mine, other, seen, env, hilbert, turned_a, turned_b, fine, coarse)
 
@@ -363,7 +422,9 @@
     sent = pack(pair_blocks, members, spectra, b)
     got = lax.all_to_all(sent, ("pairs", "slot"), 0, 0, tiled=True)
     got = got.reshape(shares, slots, 2 * b, cols)
+    hilbert = pltpu.with_memory_space_constraint(jnp.asarray(hilbert), pltpu.VMEM)
     seen, env = prepare(slot[None], observed.reshape(slots, b * b, lags), hilbert)
+    got, seen, env = lax.optimization_barrier((got, seen, env))
     mine, turned_a, turned_b = forward_pass(mask_here, got, fine, coarse)
     for axis in ("outer", "core"):
         n = lax.axis_size(axis)

time: 123 us -> 112 us (0.911)
  local copies, waits for them, and re-layouts: 17.2 us -> 8.64 us
  waiting for transfers between devices: 21 us -> 18.6 us
    unnamed x27 -> x23, local copies, waits for them, and re-layouts: 16.6 us -> 7.99 us
    all_to_all x1, waiting for transfers between devices: 21 us -> 14.8 us  [body(): got = lax.all_to_all(sent, ('pairs', 'slot'), 0, 0, tiled=True)]
    ppermute x1, waiting for transfers between devices: 0.01 us -> 3.75 us  [body(): lax.ppermute(mine, axis, [(i, (i + k) % n) for i in range(n)])]
    pallas_call x1, Pallas kernels: 22.2 us -> 20.9 us  [adjoint_pass(): pl.pallas_call(functools.partial(adjoint_kernel, (b, scale)), out_shape=j...]
  transfers between devices with their start and end apart: 2 -> 2, of which waited for: 1 -> 2; matrix products, arithmetic and copies ran while one was open for 3% -> 3% of each run, Pallas kernels for 2% -> 2%
where the time goes in v5:
time: 112 us; the launch traced here: 111 us
  Pallas kernels  39.9 us (36%)
  blocking collectives  32.4 us (29%)
  waiting for transfers between devices  18.6 us (17%)
  local copies, waits for them, and re-layouts  8.64 us (8%)
  starting transfers between devices  8.51 us (8%)
  other arithmetic  2.73 us (2%)
    all_to_all x1, blocking collectives, body(): lax.all_to_all(contrib.reshape(shares * slots, 2 * b, cols), ('pairs', 's...  32.4 us
    pallas_call x1, Pallas kernels, adjoint_pass(): pl.pallas_call(functools.partial(adjoint_kernel, (b, scale)), out_shape=j...  20.9 us
    all_to_all x1, waiting for transfers between devices, body(): got = lax.all_to_all(sent, ('pairs', 'slot'), 0, 0, tiled=True)  14.8 us
    pallas_call x1, Pallas kernels, forward_pass(): pl.pallas_call(functools.partial(forward_kernel, b), out_shape=[jax.Shape...  11.8 us
    all_to_all x1, starting transfers between devices, body(): got = lax.all_to_all(sent, ('pairs', 'slot'), 0, 0, tiled=True)  8.44 us
    unnamed x23, local copies, waits for them, and re-layouts  7.99 us
    ppermute x1, waiting for transfers between devices, body(): lax.ppermute(mine, axis, [(i, (i + k) % n) for i in range(n)])  3.75 us
    pallas_call x1, Pallas kernels, prepare(): pl.pallas_call(functools.partial(prepare_kernel, b), out_shape=[pltpu.VME...  2.72 us
  transfers between devices with their start and end apart: 2, of which 2 were waited for; matrix products, arithmetic and copies ran while one was open for 3% of the time, Pallas kernels for 2%

profile of v5, /device:TPU:0, one launch (start us, length us, event | category | flops | bytes accessed | tf_op | source)
XLA Modules:
  0.0 111.5 jit_solution(5916770782170698703)
XLA Ops:
  0.0 0.0 copy-start.10
  0.0 0.8 copy.10.blocks_ref
  0.8 0.0 copy-start.7
  0.8 0.9 copy-done.7
  1.7 0.0 copy-start.8
  1.7 0.7 copy-done.8
  2.4 2.1 %pack.1 = bf16[16,128,256]{2,1,0:T(8,128)(2,1)} custom-call(s32[16,2]{1,0:T(8,128)S(1)} %copy.10.blocks_ref, s32[1,512]{1,0:T(1,128)S(1)} %bitcast.11, bf16[1,512,256]{2,1,0:T(8,128)(2,1)S(1)} %copy-done.7), custom_call_target="tpu_custom_call" | custom-call | tf_op jit(solution)/shard_map/pack/pallas_call | solution.py:61
  4.5 0.0 copy-start.1
  4.5 8.4 %all-to-all-start = ((bf16[16,128,256]{2,1,0:T(8,128)(2,1)}), bf16[16,128,256]{2,1,0:T(8,128)(2,1)S(1)}, u32[]{:S(2)}, u32[]{:S(2)}) async-start(bf16[16,128,256]{2,1,0:T(8,128)(2,1)} %pack.1), calls=%async_computation | async-start | bytes 2097152 | tf_op jit(solution)/shard_map/all_to_all | solution.py:423
  12.9 0.0 copy-done.10
  12.9 0.7 fusion.1
  13.6 0.7 constant_dynamic-slice_fusion.1
  14.3 1.6 %copy-done = bf16[2,64,64,128]{3,2,1,0:T(8,128)(2,1)S(1)} copy-done((bf16[2,64,64,128]{3,2,1,0:T(8,128)(2,1)S(1)}, bf16[2,64,64,128]{3,2,1,0:T(8,128)(2,1)}, u32[]{:S(2)}) %copy-start) | copy-done | bytes 2097176
  15.9 0.9 copy-done.5
  16.7 2.7 %prepare.1 = (bf16[16,128,256]{2,1,0:T(8,128)(2,1)S(1)}, f32[16,128,256]{2,1,0:T(8,128)S(1)}) custom-call(s32[1]{0:T(128)} %bitcast.5.slot_ref, bf16[2,4096,128]{2,1,0:T(8,128)(2,1)S(1)} %bitcast.10, bf16[128,384]{1,0:T(8,128)(2,1)S(1)} %copy-done.5), custom_call_target="tpu_custom_call" | custom-call | flops 134217728 | bytes 4194304 | tf_op jit(solution)/shard_map/prepare/pallas_call | solution.py:140
  19.5 0.0 copy-start.2
  19.5 1.0 copy-done.2
  20.5 2.0 %broadcast_divide_fusion = (f32[2]{0:T(128)S(1)}, f32[2]{0:T(128)S(1)}) fusion(f32[]{:T(128)} %get-tuple-element.23, f32[1]{0:T(128)} %bitcast.2, f32[1]{0:T(128)} %bitcast.1), kind=kLoop, calls=%fused_computation.6 | loop fusion | flops 4 | bytes 28 | tf_op jit(solution)/shard_map/div | solution.py:420
  22.4 14.8 %all-to-all-done = bf16[16,128,256]{2,1,0:T(8,128)(2,1)S(1)} async-done(((bf16[16,128,256]{2,1,0:T(8,128)(2,1)}), bf16[16,128,256]{2,1,0:T(8,128)(2,1)S(1)}, u32[]{:S(2)}, u32[]{:S(2)}) %all-to-all-start) | async-done | bytes 1048608 | tf_op jit(solution)/shard_map/all_to_all | solution.py:423
  37.2 0.0 copy-done.1
  37.2 0.0 copy-done.4
  37.2 11.8 %forward.1 = (f32[1024,512]{1,0:T(8,128)}, bf16[8,1024,512]{2,1,0:T(8,128)(2,1)}, bf16[8,512,512]{2,1,0:T(8,128)(2,1)}) custom-call(f32[2]{0:T(128)S(1)} %get-tuple-element.22.mask_ref, bf16[8,2,128,256]{3,2,1,0:T(8,128)(2,1)S(1)} %bitcast.9, f32[8,32,256]{2,1,0:T(8,128)S(1)} %copy-done.1, f32[8,16,256]{2,1,0:T(8,128)S(1)} %copy-done.4), custom_call_target="tpu_custom_call" | custom-call | tf_op jit(solution)/shard_map/forward/pallas_call | solution.py:229
  49.0 0.1 collective-permute-start
  49.8 0.1 pad_maximum_fusion.1.scalars_ref
  49.9 3.8 %collective-permute-done.other_ref = f32[1024,512]{1,0:T(8,128)} collective-permute-done((f32[1024,512]{1,0:T(8,128)}, f32[1024,512]{1,0:T(8,128)}, u32[]{:S(2)}, u32[]{:S(2)}) %collective-permute-start) | collective-permute-done | bytes 2097184 | tf_op jit(solution)/shard_map/ppermute | solution.py:431
  53.6 1.2 %copy-done.3 = bf16[16,128,256]{2,1,0:T(8,128)(2,1)S(1)} copy-done((bf16[16,128,256]{2,1,0:T(8,128)(2,1)S(1)}, bf16[16,128,256]{2,1,0:T(8,128)(2,1)}, u32[]{:S(2)}) %copy-start.3) | copy-done | bytes 1048600
  54.8 0.9 copy-done.6
  55.7 20.9 %adjoint.1 = bf16[8,2,128,256]{3,2,1,0:T(8,128)(2,1)S(1)} custom-call(f32[3]{0:T(128)S(1)} %pad_maximum_fusion.1.scalars_ref, f32[1024,512]{1,0:T(8,128)} %get-tuple-element.16.mine_ref, f32[1024,512]{1,0:T(8,128)} %collective-permute-done.other_ref, bf16[16,128,256]{2,1,0:T(8,128)(2,1)S(1)} %copy-done.3, f32[16,128,256]{2,1,0:T(8,128)S(1)} %get-tuple-element.18.env_ref, ...), custom_call_target="tpu_custom_call" | custom-call | tf_op jit(solution)/shard_map/adjoint/pallas_call | solution.py:385
  76.7 0.0 copy-start.9
  76.7 32.4 %all_to_all.10.got_ref = bf16[16,128,256]{2,1,0:T(8,128)(2,1)S(1)} all-to-all(bf16[16,128,256]{2,1,0:T(8,128)(2,1)S(1)} %bitcast.8), channel_id=1, replica_groups=mesh['pairs'=8,'outer'=1,'slot'=2,'core'=2] {'pairs','slot'}, dimensions={0} | all-to-all | bytes 2097152 | tf_op jit(solution)/shard_map/all_to_all | solution.py:436
  109.1 0.0 copy-done.9
  109.1 2.4 %unpack.1 = f32[1,512,256]{2,1,0:T(8,128)} custom-call(s32[16,2]{1,0:T(8,128)S(1)} %copy.10.blocks_ref, s32[1,512]{1,0:T(1,128)S(1)} %bitcast.12, bf16[16,128,256]{2,1,0:T(8,128)(2,1)S(1)} %all_to_all.10.got_ref), custom_call_target="tpu_custom_call" | custom-call | tf_op jit(solution)/shard_map/unpack/pallas_call | solution.py:96
  (5 shorter events, 0.0 us)
Async XLA Ops:
  0.0 12.9 %copy-start.10 = (s32[2,4]{1,0:T(2,128)S(1)}, s32[2,4]{1,0:T(2,128)}, u32[]{:S(2)}) copy-start(s32[2,4]{1,0:T(2,128)} %param.12) | copy-start | bytes 100
  0.8 0.9 copy-start.7
  1.7 0.7 copy-start.8
  4.5 32.8 %copy-start.1 = (f32[8,32,256]{2,1,0:T(8,128)S(1)}, f32[8,32,256]{2,1,0:T(8,128)}, u32[]{:S(2)}) copy-start(f32[8,32,256]{2,1,0:T(8,128)} %constant.39.clone.fine_ref) | copy-start | bytes 786436
  4.5 32.8 %copy-start.4 = (f32[8,16,256]{2,1,0:T(8,128)S(1)}, f32[8,16,256]{2,1,0:T(8,128)}, u32[]{:S(2)}) copy-start(f32[8,16,256]{2,1,0:T(8,128)} %constant.40.clone.coarse_ref) | copy-start | bytes 393220
  4.5 32.8 %all-to-all-start = ((bf16[16,128,256]{2,1,0:T(8,128)(2,1)}), bf16[16,128,256]{2,1,0:T(8,128)(2,1)S(1)}, u32[]{:S(2)}, u32[]{:S(2)}) async-start(bf16[16,128,256]{2,1,0:T(8,128)(2,1)} %pack.1), calls=%async_computation | async-start | bytes 2097152 | tf_op jit(solution)/shard_map/all_to_all | solution.py:423
  14.3 1.6 %copy-start = (bf16[2,64,64,128]{3,2,1,0:T(8,128)(2,1)S(1)}, bf16[2,64,64,128]{3,2,1,0:T(8,128)(2,1)}, u32[]{:S(2)}) copy-start(bf16[2,64,64,128]{3,2,1,0:T(8,128)(2,1)} %param.9) | copy-start | bytes 6291460
  15.8 0.9 copy-start.5
  19.5 1.0 copy-start.2
  49.0 4.6 %collective-permute-start = (f32[1024,512]{1,0:T(8,128)}, f32[1024,512]{1,0:T(8,128)}, u32[]{:S(2)}, u32[]{:S(2)}) collective-permute-start(f32[1024,512]{1,0:T(8,128)} %get-tuple-element.16.mine_ref), channel_id=1, source_target_pairs={{0,1},{1,0},{2,3},{3,2},{4,5},{5,4},{6,7},{7,6},{8,9},{9,8},{10,11... | collective-permute-start | bytes 6291464 | tf_op jit(solution)/shard_map/ppermute | solution.py:431
  53.6 1.2 %copy-start.3 = (bf16[16,128,256]{2,1,0:T(8,128)(2,1)S(1)}, bf16[16,128,256]{2,1,0:T(8,128)(2,1)}, u32[]{:S(2)}) copy-start(bf16[16,128,256]{2,1,0:T(8,128)(2,1)} %copy-done.2) | copy-start | bytes 3145732
  54.8 0.9 copy-start.6
  76.7 32.4 %copy-start.9 = (s32[512]{0:T(512)S(1)}, s32[512]{0:T(512)}, u32[]{:S(2)}) copy-start(s32[512]{0:T(512)} %param.11) | copy-start | bytes 6148

commit v6 on v4

v6 whole, which is shorter than its diff:
```python
import functools
import math

import jax
import jax.numpy as jnp
import ml_dtypes
import numpy as np
from jax import lax
from jax.experimental import pallas as pl
from jax.experimental.pallas import tpu as pltpu
from jax.sharding import Mesh, PartitionSpec as P

HALF = 64
TILE = 128
CORES = 2
F32 = jnp.float32
BF16 = jnp.bfloat16


def hilbert_parts(lags):
    offset = (np.arange(lags)[None, :] - np.arange(lags)[:, None]) % lags
    angles = np.float32(math.pi) * offset.astype(np.float32) / np.float32(lags)
    odd = offset % 2 == 1
    safe = np.where(odd, np.sin(angles), np.float32(1.0))
    table = np.where(odd, np.float32(2.0 / lags) * np.cos(angles) / safe, np.float32(0.0))
    table = table.astype(np.float32).T
    high = table.astype(ml_dtypes.bfloat16)
    low = (table - high.astype(np.float32)).astype(ml_dtypes.bfloat16)
    return np.concatenate([high, low, high], axis=1)


def left_lanes(shape):
    return lax.broadcasted_iota(jnp.int32, shape, len(shape) - 1) % TILE < HALF


def swap_halves(x):
    return pltpu.roll(x, HALF, 1)


def dot(a, b):
    return jnp.dot(a, b, preferred_element_type=F32)


def pack_kernel(blocks_ref, members_ref, spectra_ref, out_ref, ordered):
    stations = spectra_ref.shape[1]
    b = out_ref.shape[1] // 2
    station = lax.broadcasted_iota(jnp.int32, (stations, stations), 0)
    chosen = (station == members_ref[...]).astype(F32).astype(BF16)
    ordered[...] = lax.dot_general(
        chosen, spectra_ref[0], (((0,), (0,)), ((), ())), preferred_element_type=F32
    ).astype(BF16)
    for p in range(out_ref.shape[0]):
        for side in range(2):
            row = pl.multiple_of(blocks_ref[p, side] * b, b)
            out_ref[p, side * b:(side + 1) * b, :] = ordered[pl.ds(row, b), :]


def pack(pair_blocks, members, spectra, b):
    _, stations, cols = spectra.shape
    n_pairs = pair_blocks.shape[0]
    return pl.pallas_call(
        pack_kernel,
        out_shape=jax.ShapeDtypeStruct((n_pairs, 2 * b, cols), BF16),
        in_specs=[
            pl.BlockSpec(memory_space=pltpu.SMEM),
            pl.BlockSpec(memory_space=pltpu.VMEM),
            pl.BlockSpec(memory_space=pltpu.VMEM),
        ],
        out_specs=pl.BlockSpec(memory_space=pltpu.VMEM),
        scratch_shapes=[pltpu.VMEM((stations, cols), BF16)],
        compiler_params=pltpu.CompilerParams(vmem_limit_bytes=8 << 20),
        name="pack",
    )(pair_blocks, members, spectra)


def unpack_kernel(blocks_ref, members_ref, got_ref, out_ref, total):
    stations = out_ref.shape[1]
    b = got_ref.shape[1] // 2
    total[...] = jnp.zeros_like(total)
    for p in range(got_ref.shape[0]):
        for side in range(2):
            rows = pl.ds(pl.multiple_of(blocks_ref[p, side] * b, b), b)
            total[rows, :] += got_ref[p, side * b:(side + 1) * b, :].astype(F32)
    station = lax.broadcasted_iota(jnp.int32, (stations, stations), 0)
    chosen = (station == members_ref[...]).astype(F32).astype(BF16)
    whole = total[...]
    high = whole.astype(BF16)
    rest = whole - high.astype(F32)
    mid = rest.astype(BF16)
    low = (rest - mid.astype(F32)).astype(BF16)
    out_ref[0] = dot(chosen, high) + (dot(chosen, mid) + dot(chosen, low))


def unpack(pair_blocks, members, got, stations):
    cols = got.shape[2]
    return pl.pallas_call(
        unpack_kernel,
        out_shape=jax.ShapeDtypeStruct((1, stations, cols), F32),
        in_specs=[
            pl.BlockSpec(memory_space=pltpu.SMEM),
            pl.BlockSpec(memory_space=pltpu.VMEM),
            pl.BlockSpec(memory_space=pltpu.VMEM),
        ],
        out_specs=pl.BlockSpec(memory_space=pltpu.VMEM),
        scratch_shapes=[pltpu.VMEM((stations, cols), F32)],
        compiler_params=pltpu.CompilerParams(vmem_limit_bytes=8 << 20),
        name="unpack",
    )(pair_blocks, members, got)


def prepare_kernel(b, slot_ref, observed_ref, hilbert_ref, seen_ref, env_ref):
    lags = observed_ref.shape[1]
    two = 2 * b

    def some(step, carry):
        seen = observed_ref[pl.ds(pl.multiple_of(step * two, two), two), :].astype(F32).T
        seen_b = seen.astype(BF16)
        hil = dot(hilbert_ref[:, :2 * lags], jnp.concatenate([seen_b, seen_b], axis=0))
        seen_ref[step] = seen_b
        env_ref[step] = 1.0 + jnp.sqrt(seen * seen + hil * hil)
        return carry

    lax.fori_loop(0, seen_ref.shape[0], some, 0, unroll=4)


def prepare(slot, observed, hilbert, parts):
    _, rows, lags = observed.shape
    b = math.isqrt(rows)
    shape = (b // 2, lags, 2 * b)
    block = (b // 2 // parts, lags, 2 * b)
    spec = pltpu.PrefetchScalarGridSpec(
        num_scalar_prefetch=1,
        grid=(parts,),
        in_specs=[
            pl.BlockSpec((None, rows // parts, lags), lambda s, slot_ref: (slot_ref[0], s, 0)),
            pl.BlockSpec(hilbert.shape, lambda s, slot_ref: (0, 0)),
        ],
        out_specs=[pl.BlockSpec(block, lambda s, slot_ref: (s, 0, 0))] * 2,
    )
    return pl.pallas_call(
        functools.partial(prepare_kernel, b),
        out_shape=[pltpu.HBM(shape, BF16), pltpu.HBM(shape, F32)],
        grid_spec=spec,
        compiler_params=pltpu.CompilerParams(vmem_limit_bytes=8 << 20),
        cost_estimate=pl.CostEstimate(flops=2 * rows * lags * lags, bytes_accessed=8 * rows * lags, transcendentals=0),
        name="prepare",
    )(slot, observed, hilbert)


def tile_lanes(tiles, d, t):
    return slice((d * tiles + t) * TILE, (d * tiles + t + 1) * TILE)


def part(t):
    return slice(t * TILE, (t + 1) * TILE)


def turn_columns(got_ref, share, b, table_ref, into):
    _, days, _, cols = got_ref.shape
    tiles = cols // TILE
    n = table_ref.shape[1] // 2
    for d in range(days):
        for t in range(tiles):
            at = tile_lanes(tiles, d, t)
            u = got_ref[share, d, b:, part(t)].astype(F32)
            v = swap_halves(u)
            for k in range(n):
                cosine = table_ref[share, k:k + 1, part(t)]
                sine = table_ref[share, n + k:n + k + 1, part(t)]
                into[k * b:(k + 1) * b, at] = (u * cosine + v * sine).astype(BF16)


def turn_rows(got_ref, share, b, table_ref, into, rows_u, rows_v, mask_ref=None):
    _, days, _, cols = got_ref.shape
    tiles = cols // TILE
    n = table_ref.shape[1] // 2
    pieces = [(d, t) for d in range(days) for t in range(tiles)]
    for d, t in pieces:
        at = tile_lanes(tiles, d, t)
        u = got_ref[share, d, :b, part(t)].astype(F32)
        if mask_ref is not None:
            u = u * mask_ref[d]
        rows_u[:, at] = u
        rows_v[:, at] = swap_halves(u)
    for d, t in pieces:
        at = tile_lanes(tiles, d, t)
        cosine = table_ref[share, :n, part(t)]
        sine = table_ref[share, n:, part(t)]
        for k in range(b):
            value = rows_u[k:k + 1, at] * cosine + rows_v[k:k + 1, at] * sine
            into[k * n:(k + 1) * n, at] = value.astype(BF16)


def forward_kernel(
    b, mask_ref, got_ref, fine_ref, coarse_ref, out_ref, sent_ref, kept_ref, even_a, even_b, odd_a, odd_b, rows_u, rows_v,
    sem,
):
    shares = got_ref.shape[0]
    even = (even_a, even_b)
    odd = (odd_a, odd_b)
    keep = pltpu.make_async_copy(got_ref, kept_ref, sem)
    keep.start()

    def make(share, into):
        turn_columns(got_ref, share, b, coarse_ref, into[1])
        turn_rows(got_ref, share, b, fine_ref, into[0], rows_u, rows_v, mask_ref)

    def product(made):
        return lax.dot_general(made[0][...], made[1][...], (((1,), (1,)), ((), ())), preferred_element_type=F32)

    make(0, even)
    out_ref[...] = product(even)
    make(1, odd)

    def two_shares(step, carry):
        out_ref[...] += product(odd)
        make(2 * step + 2, even)
        out_ref[...] += product(even)
        make(2 * step + 3, odd)
        return carry

    lax.fori_loop(0, shares // 2 - 1, two_shares, 0)
    total = out_ref[...] + product(odd)
    out_ref[...] = total
    sent_ref[...] = total.astype(sent_ref.dtype)
    keep.wait()


def forward_pass(mask, got, fine, coarse):
    shares, days, rows, cols = got.shape
    assert shares % 2 == 0
    b = rows // 2
    n_fine = fine.shape[1] // 2
    n_coarse = coarse.shape[1] // 2
    vmem = pl.BlockSpec(memory_space=pltpu.VMEM)
    return pl.pallas_call(
        functools.partial(forward_kernel, b),
        out_shape=[
            pltpu.VMEM((n_fine * b, n_coarse * b), F32),
            jax.ShapeDtypeStruct((n_fine * b, n_coarse * b), BF16),
            pltpu.HBM(got.shape, BF16),
        ],
        in_specs=[pl.BlockSpec(memory_space=pltpu.SMEM), vmem, vmem, vmem],
        out_specs=[vmem, vmem, pl.BlockSpec(memory_space=pltpu.HBM)],
        scratch_shapes=[
            pltpu.VMEM((n_fine * b, days * cols), BF16),
            pltpu.VMEM((n_coarse * b, days * cols), BF16),
            pltpu.VMEM((n_fine * b, days * cols), BF16),
            pltpu.VMEM((n_coarse * b, days * cols), BF16),
            pltpu.VMEM((b, days * cols), F32),
            pltpu.VMEM((b, days * cols), F32),
            pltpu.SemaphoreType.DMA,
        ],
        compiler_params=pltpu.CompilerParams(vmem_limit_bytes=16 << 20),
        name="forward",
    )(mask, got, fine, coarse)


def adjoint_kernel(
    sizes, scalars_ref, mine_ref, other_hbm, seen_hbm, env_hbm, hilbert_hbm, kept_ref, fine_hbm, coarse_hbm, out_ref,
    other_ref, seen_ref, env_ref, hilbert_ref, got_ref, fine_ref, coarse_ref, lagged, back, res, res_t, sums_a, sums_b,
    turned_a, turned_b, rows_u, rows_v, sems_o, sems_s, sems_e, sems,
):
    b, scale, group = sizes
    shares, days, _, cols = out_ref.shape
    n_fine = fine_ref.shape[1] // 2
    n_coarse = coarse_ref.shape[1] // 2
    slabs = n_coarse // 2
    tiles = cols // TILE
    block = group * n_fine
    left = left_lanes((n_fine, 2 * b))

    def bring(step):
        at = pl.ds(pl.multiple_of(step * block, block), block)
        some = pl.ds(step * (group // 2), group // 2)
        return (
            pltpu.make_async_copy(other_hbm.at[at], other_ref.at[at], sems_o.at[step]),
            pltpu.make_async_copy(seen_hbm.at[some], seen_ref.at[some], sems_s.at[step]),
            pltpu.make_async_copy(env_hbm.at[some], env_ref.at[some], sems_e.at[step]),
        )

    first = pltpu.make_async_copy(hilbert_hbm, hilbert_ref, sems.at[0])
    later = (
        pltpu.make_async_copy(kept_ref, got_ref, sems.at[1]),
        pltpu.make_async_copy(fine_hbm, fine_ref, sems.at[2]),
        pltpu.make_async_copy(coarse_hbm, coarse_ref, sems.at[3]),
    )
    first.start()
    for step in range(b // group):
        for copy in bring(step):
            copy.start()
    for copy in later:
        copy.start()
    first.wait()

    def residual_rows(step, carry):
        for copy in bring(step):
            copy.wait()
        for two in range(0, group, 2):
            rows = []
            for slab in range(slabs):
                got = []
                for k in (two, two + 1):
                    at = pl.ds(pl.multiple_of(step * block + k * n_fine, n_fine), n_fine)
                    got.append((mine_ref[at, part(slab)] + other_ref[at, part(slab)].astype(F32)) * scalars_ref[days])
                rows.append(jnp.where(left, got[0], swap_halves(got[1])))
                rows.append(jnp.where(left, swap_halves(got[0]), got[1]))
            stacked = jnp.concatenate(rows, axis=0)
            high = stacked.astype(BF16)
            low = (stacked - high.astype(F32)).astype(BF16)
            hil = dot(hilbert_ref[...], jnp.concatenate([high, high, low], axis=0))
            env_s = 1.0 + jnp.sqrt(stacked * stacked + hil * hil)
            env_o = env_ref[step * (group // 2) + two // 2]
            value = (stacked - seen_ref[step * (group // 2) + two // 2].astype(F32)) * (env_s / (env_s + env_o - 1.0))
            for slab in range(slabs):
                even = value[2 * slab * n_fine:(2 * slab + 1) * n_fine, :]
                odd = value[(2 * slab + 1) * n_fine:(2 * slab + 2) * n_fine, :]
                first = jnp.where(left, even, swap_halves(odd))
                second = jnp.where(left, swap_halves(even), odd)
                for k, rows in ((two, first), (two + 1, second)):
                    lagged[slab, pl.ds(step * group + k, n_fine, stride=b), :] = rows
                    back[k * n_fine:(k + 1) * n_fine, part(slab)] = rows
        at = pl.ds(pl.multiple_of(step * block, block), block)
        for slab in range(slabs):
            res_t[part(slab), at] = back[:, part(slab)].T.astype(BF16)
        return carry

    lax.fori_loop(0, b // group, residual_rows, 0)

    def round_rows(step, carry):
        at = pl.ds(pl.multiple_of(step * b, b), b)
        for slab in range(slabs):
            res[at, part(slab)] = lagged[slab, at, :].astype(BF16)
        return carry

    lax.fori_loop(0, n_fine, round_rows, 0)

    def collect(share, side, table, n, sums):
        for d in range(days):
            for t in range(tiles):
                at = tile_lanes(tiles, d, t)
                p = jnp.zeros((b, TILE), F32)
                q = jnp.zeros((b, TILE), F32)
                for k in range(n):
                    h = sums[k * b:(k + 1) * b, at]
                    p = p + h * table[share, k:k + 1, part(t)]
                    q = q + h * table[share, n + k:n + k + 1, part(t)]
                value = (p + swap_halves(q)) * (scalars_ref[d] * scale)
                out_ref[share, d, side * b:(side + 1) * b, part(t)] = value.astype(BF16)

    for copy in later:
        copy.wait()
    sums_b[...] = jnp.zeros_like(sums_b)
    turn_columns(got_ref, 0, b, coarse_ref, turned_b)

    def one_share(share, carry):
        sums_a[...] = dot(res[...], turned_b[...])
        turn_rows(got_ref, share, b, fine_ref, turned_a, rows_u, rows_v)
        collect(jnp.maximum(share - 1, 0), 1, coarse_ref, n_coarse, sums_b)
        sums_b[...] = dot(res_t[...], turned_a[...])
        collect(share, 0, fine_ref, n_fine, sums_a)
        turn_columns(got_ref, jnp.minimum(share + 1, shares - 1), b, coarse_ref, turned_b)
        return carry

    lax.fori_loop(0, shares, one_share, 0)
    collect(shares - 1, 1, coarse_ref, n_coarse, sums_b)


def turn_tables(columns, lags, shares):
    freqs = columns // 2
    n_fine = 16
    n_coarse = lags // n_fine
    column = np.arange(columns)
    frequency = column // TILE * HALF + column % HALF
    is_real = column % TILE < HALF

    def table(steps, sign):
        phase = frequency[None, :] * steps[:, None] % (2 * freqs)
        angles = np.pi * phase / freqs
        sine = np.where(is_real[None, :], -sign, sign) * np.sin(angles)
        rows = np.concatenate([np.cos(angles), sine]).astype(np.float32)
        return rows.reshape(rows.shape[0], shares, columns // shares).transpose(1, 0, 2)

    fine = table(np.arange(n_fine), 1)
    coarse = table(n_fine * np.arange(n_coarse) - lags // 2, -1)
    return np.ascontiguousarray(fine), np.ascontiguousarray(coarse)


def adjoint_pass(scalars, mine, other, seen, env, hilbert, kept, fine, coarse, parts):
    shares, days, rows, cols = kept.shape
    b = rows // 2
    n_fine = fine.shape[1] // 2
    n_coarse = coarse.shape[1] // 2
    scale = 1.0 / math.sqrt(shares * cols // 2)
    group = b // parts
    lanes = days * cols
    vmem = pl.BlockSpec(memory_space=pltpu.VMEM)
    hbm = pl.BlockSpec(memory_space=pltpu.HBM)
    apart = [pltpu.with_memory_space_constraint(x, pltpu.HBM) for x in (other, seen, env, hilbert, kept, fine, coarse)]
    return pl.pallas_call(
        functools.partial(adjoint_kernel, (b, scale, group)),
        out_shape=jax.ShapeDtypeStruct(kept.shape, BF16),
        in_specs=[pl.BlockSpec(memory_space=pltpu.SMEM), vmem] + [hbm] * len(apart),
        out_specs=vmem,
        scratch_shapes=[pltpu.VMEM(x.shape, x.dtype) for x in apart]
        + [
            pltpu.VMEM((n_coarse // 2, n_fine * b, 2 * b), F32),
            pltpu.VMEM((group * n_fine, n_coarse * b), F32),
            pltpu.VMEM((n_fine * b, n_coarse * b), BF16),
            pltpu.VMEM((n_coarse * b, n_fine * b), BF16),
            pltpu.VMEM((n_fine * b, lanes), F32),
            pltpu.VMEM((n_coarse * b, lanes), F32),
            pltpu.VMEM((n_fine * b, lanes), BF16),
            pltpu.VMEM((n_coarse * b, lanes), BF16),
            pltpu.VMEM((b, lanes), F32),
            pltpu.VMEM((b, lanes), F32),
            pltpu.SemaphoreType.DMA((parts,)),
            pltpu.SemaphoreType.DMA((parts,)),
            pltpu.SemaphoreType.DMA((parts,)),
            pltpu.SemaphoreType.DMA((4,)),
        ],
        compiler_params=pltpu.CompilerParams(vmem_limit_bytes=24 << 20),
        name="adjoint",
    )(scalars, mine, *apart)


def body(spectra, observed, pair_blocks, members, day_mask):
    shares = lax.axis_size("pairs")
    slots, b, _, lags = observed.shape
    _, stations, cols = spectra.shape
    fine, coarse = turn_tables(shares * cols, lags, shares)
    hilbert = hilbert_parts(lags)
    slot = lax.axis_index("slot")
    members = members.reshape(1, stations)
    first_day = lax.axis_index("outer") * slots * CORES + lax.axis_index("core")
    mask = lax.dynamic_slice_in_dim(day_mask, slot, 1, 0)[0].astype(F32)
    mask_here = jnp.stack([lax.dynamic_index_in_dim(mask, first_day + k * CORES, 0, False) for k in range(slots)])
    count = jnp.sum(mask)
    scale = 1.0 / math.sqrt(shares * cols // 2)
    scalars = jnp.concatenate([mask_here / count, scale / count[None]])

    sent = pack(pair_blocks, members, spectra, b)
    got = lax.all_to_all(sent, ("pairs", "slot"), 0, 0, tiled=True)
    got = got.reshape(shares, slots, 2 * b, cols)
    parts = 4
    hilbert, fine, coarse = [jnp.asarray(x) for x in (hilbert, fine, coarse)]
    seen, env = prepare(slot[None], observed.reshape(slots, b * b, lags), hilbert, parts)
    got, seen, env = lax.optimization_barrier((got, seen, env))
    mine, sent, kept = forward_pass(mask_here, got, fine, coarse)
    for axis in ("outer", "core"):
        n = lax.axis_size(axis)
        others = [lax.ppermute(sent, axis, [(i, (i + k) % n) for i in range(n)]) for k in range(1, n)]
        if axis == "outer" and others:
            for other in others:
                mine = mine + other.astype(F32)
            sent = mine.astype(BF16)
    contrib = adjoint_pass(scalars, mine, others[0], seen, env, hilbert, kept, fine, coarse, parts)
    returned = lax.all_to_all(
        contrib.reshape(shares * slots, 2 * b, cols), ("pairs", "slot"), 0, 0, tiled=True
    )
    return unpack(pair_blocks, members, returned, stations)


def solution(mesh):
    shares, days = mesh.devices.shape
    names = ("pairs", "outer", "slot", "core")

    def run(spectra, observed, pair_blocks, members, day_mask):
        slots = observed.shape[0] // shares
        split = (shares, days // CORES // slots, slots, CORES)
        finer = Mesh(mesh.devices.reshape(split), names)
        day_axes = names[1:]
        return jax.shard_map(
            body,
            mesh=finer,
            in_specs=(
                P(day_axes, None, "pairs"),
                P("pairs", None, None, None),
                P(),
                P(),
                P("pairs", None),
            ),
            out_specs=P(day_axes, None, "pairs"),
            check_vma=False,
        )(spectra, observed, pair_blocks, members, day_mask)

    return run
```

time: 123 us -> 108 us (0.88)
  local copies, waits for them, and re-layouts: 17.2 us -> 5.01 us
  waiting for transfers between devices: 21 us -> 18.6 us
    unnamed x27 -> x19, local copies, waits for them, and re-layouts: 16.6 us -> 4.42 us
    all_to_all x1, waiting for transfers between devices: 21 us -> 16.5 us  [body(): got = lax.all_to_all(sent, ('pairs', 'slot'), 0, 0, tiled=True)]
    ppermute x1, waiting for transfers between devices: 0.01 us -> 2.11 us  [body(): lax.ppermute(sent, axis, [(i, (i + k) % n) for i in range(n)])]
  transfers between devices with their start and end apart: 2 -> 2, of which waited for: 1 -> 2; matrix products, arithmetic and copies ran while one was open for 3% -> 3% of each run, Pallas kernels for 2% -> 4%
where the time goes in v6:
time: 108 us; the launch traced here: 107 us
  Pallas kernels  39.5 us (37%)
  blocking collectives  32.4 us (30%)
  waiting for transfers between devices  18.6 us (17%)
  starting transfers between devices  8.51 us (8%)
  local copies, waits for them, and re-layouts  5.01 us (5%)
  other arithmetic  2.53 us (2%)
    all_to_all x1, blocking collectives, body(): lax.all_to_all(contrib.reshape(shares * slots, 2 * b, cols), ('pairs', 's...  32.4 us
    pallas_call x1, Pallas kernels, adjoint_pass(): pl.pallas_call(functools.partial(adjoint_kernel, (b, scale, group)), out_...  22.4 us
    all_to_all x1, waiting for transfers between devices, body(): got = lax.all_to_all(sent, ('pairs', 'slot'), 0, 0, tiled=True)  16.5 us
    pallas_call x1, Pallas kernels, forward_pass(): pl.pallas_call(functools.partial(forward_kernel, b), out_shape=[pltpu.VME...  8.76 us
    all_to_all x1, starting transfers between devices, body(): got = lax.all_to_all(sent, ('pairs', 'slot'), 0, 0, tiled=True)  8.44 us
    unnamed x19, local copies, waits for them, and re-layouts  4.42 us
    pallas_call x1, Pallas kernels, prepare(): pl.pallas_call(functools.partial(prepare_kernel, b), out_shape=[pltpu.HBM...  3.85 us
    pallas_call x1, Pallas kernels, unpack(): pl.pallas_call(unpack_kernel, out_shape=jax.ShapeDtypeStruct((1, stations...  2.43 us
  transfers between devices with their start and end apart: 2, of which 2 were waited for; matrix products, arithmetic and copies ran while one was open for 3% of the time, Pallas kernels for 4%

profile of v6, /device:TPU:0, one launch (start us, length us, event | category | flops | bytes accessed | tf_op | source)
XLA Modules:
  0.0 107.3 jit_solution(17666089834190745663)
XLA Ops:
  0.0 0.0 copy-start
  0.0 0.9 copy.10.blocks_ref
  0.9 0.0 copy-start.4
  0.9 0.9 copy-done.4
  1.9 0.0 copy-start.5
  1.9 0.7 copy-done.5
  2.5 0.0 copy-start.8
  2.5 2.1 %pack.1 = bf16[16,128,256]{2,1,0:T(8,128)(2,1)} custom-call(s32[16,2]{1,0:T(8,128)S(1)} %copy.10.blocks_ref, s32[1,512]{1,0:T(1,128)S(1)} %bitcast.11, bf16[1,512,256]{2,1,0:T(8,128)(2,1)S(1)} %copy-done.4), custom_call_target="tpu_custom_call" | custom-call | tf_op jit(solution)/shard_map/pack/pallas_call | solution.py:61
  4.6 0.0 copy-start.1
  4.6 0.0 copy-start.2
  4.6 8.4 %all-to-all-start = ((bf16[16,128,256]{2,1,0:T(8,128)(2,1)}), bf16[16,128,256]{2,1,0:T(8,128)(2,1)S(1)}, u32[]{:S(2)}, u32[]{:S(2)}) async-start(bf16[16,128,256]{2,1,0:T(8,128)(2,1)} %pack.1), calls=%async_computation | async-start | bytes 2097152 | tf_op jit(solution)/shard_map/all_to_all | solution.py:443
  13.1 0.0 copy-done.8
  13.1 0.6 fusion.1
  13.7 0.6 constant_dynamic-slice_fusion.1
  14.3 0.0 copy-done
  14.3 0.0 copy-start.3
  14.3 0.9 copy-done.3
  15.2 3.8 %prepare.1 = (bf16[32,128,128]{2,1,0:T(8,128)(2,1)}, f32[32,128,128]{2,1,0:T(8,128)}) custom-call(s32[1]{0:T(128)} %bitcast.5.slot_ref, bf16[2,4096,128]{2,1,0:T(8,128)(2,1)S(1)} %bitcast.10, bf16[128,384]{1,0:T(8,128)(2,1)S(1)} %copy-done.3), custom_call_target="tpu_custom_call" | custom-call | flops 134217728 | bytes 4194304 | tf_op jit(solution)/shard_map/prepare/pallas_call | solution.py:140
  19.1 1.8 %broadcast_divide_fusion = (f32[2]{0:T(128)S(1)}, f32[2]{0:T(128)S(1)}) fusion(f32[]{:T(128)} %get-tuple-element.23, f32[1]{0:T(128)} %bitcast.2, f32[1]{0:T(128)} %bitcast.1), kind=kLoop, calls=%fused_computation.6 | loop fusion | flops 4 | bytes 28 | tf_op jit(solution)/shard_map/div | solution.py:440
  20.9 16.5 %all-to-all-done = bf16[16,128,256]{2,1,0:T(8,128)(2,1)S(1)} async-done(((bf16[16,128,256]{2,1,0:T(8,128)(2,1)}), bf16[16,128,256]{2,1,0:T(8,128)(2,1)S(1)}, u32[]{:S(2)}, u32[]{:S(2)}) %all-to-all-start) | async-done | bytes 1048608 | tf_op jit(solution)/shard_map/all_to_all | solution.py:443
  37.4 0.0 copy-done.1
  37.4 0.0 copy-done.2
  37.4 8.8 %forward.1 = (f32[1024,512]{1,0:T(8,128)S(1)}, bf16[1024,512]{1,0:T(8,128)(2,1)}, bf16[8,2,128,256]{3,2,1,0:T(8,128)(2,1)}) custom-call(f32[2]{0:T(128)S(1)} %get-tuple-element.22.mask_ref, bf16[8,2,128,256]{3,2,1,0:T(8,128)(2,1)S(1)} %bitcast.9, f32[8,32,256]{2,1,0:T(8,128)S(1)} %copy-done.1, f32[8,16,256]{2,1,0:T(8,128)S(1)} %copy-done.2), custom_call_target="tpu_custom_call" | custom-call | tf_op jit(solution)/shard_map/forward/pallas_call | solution.py:236
  46.2 0.1 collective-permute-start
  46.9 0.1 pad_maximum_fusion.1.scalars_ref
  47.0 2.1 %collective-permute-done.other_hbm = bf16[1024,512]{1,0:T(8,128)(2,1)S(1)} collective-permute-done((bf16[1024,512]{1,0:T(8,128)(2,1)}, bf16[1024,512]{1,0:T(8,128)(2,1)S(1)}, u32[]{:S(2)}, u32[]{:S(2)}) %collective-permute-start) | collective-permute-done | bytes 1048608 | tf_op jit(solution)/shard_map/ppermute | solution.py:452
  49.1 1.0 copy-done.7
  50.1 22.4 %adjoint.1 = bf16[8,2,128,256]{3,2,1,0:T(8,128)(2,1)S(1)} custom-call(f32[3]{0:T(128)S(1)} %pad_maximum_fusion.1.scalars_ref, f32[1024,512]{1,0:T(8,128)S(1)} %get-tuple-element.16.mine_ref, bf16[1024,512]{1,0:T(8,128)(2,1)} %copy-done.7, bf16[32,128,128]{2,1,0:T(8,128)(2,1)} %get-tuple-element.18.seen_hbm, f32[32,128,128]{2,1,0:T(8,128)} %get-tuple-element.19.env_hbm, ...), custom_call_target="tpu_custom_call" | custom-call | tf_op jit(solution)/shard_map/adjoint/pallas_call | solution.py:400
  72.5 0.0 copy-start.6
  72.5 32.4 %all_to_all.10.got_ref = bf16[16,128,256]{2,1,0:T(8,128)(2,1)S(1)} all-to-all(bf16[16,128,256]{2,1,0:T(8,128)(2,1)S(1)} %bitcast.8), channel_id=1, replica_groups=mesh['pairs'=8,'outer'=1,'slot'=2,'core'=2] {'pairs','slot'}, dimensions={0} | all-to-all | bytes 2097152 | tf_op jit(solution)/shard_map/all_to_all | solution.py:458
  104.9 0.0 copy-done.6
  104.9 2.4 %unpack.1 = f32[1,512,256]{2,1,0:T(8,128)} custom-call(s32[16,2]{1,0:T(8,128)S(1)} %copy.10.blocks_ref, s32[1,512]{1,0:T(1,128)S(1)} %bitcast.12, bf16[16,128,256]{2,1,0:T(8,128)(2,1)S(1)} %all_to_all.10.got_ref), custom_call_target="tpu_custom_call" | custom-call | tf_op jit(solution)/shard_map/unpack/pallas_call | solution.py:96
  (1 shorter events, 0.0 us)
Async XLA Ops:
  0.0 14.3 %copy-start = (bf16[2,64,64,128]{3,2,1,0:T(8,128)(2,1)S(1)}, bf16[2,64,64,128]{3,2,1,0:T(8,128)(2,1)}, u32[]{:S(2)}) copy-start(bf16[2,64,64,128]{3,2,1,0:T(8,128)(2,1)} %param.9) | copy-start | bytes 6291460
  0.9 0.9 copy-start.4
  1.9 0.7 copy-start.5
  2.5 10.5 %copy-start.8 = (s32[2,4]{1,0:T(2,128)S(1)}, s32[2,4]{1,0:T(2,128)}, u32[]{:S(2)}) copy-start(s32[2,4]{1,0:T(2,128)} %param.12) | copy-start | bytes 100
  4.6 32.8 %copy-start.1 = (f32[8,32,256]{2,1,0:T(8,128)S(1)}, f32[8,32,256]{2,1,0:T(8,128)}, u32[]{:S(2)}) copy-start(f32[8,32,256]{2,1,0:T(8,128)} %constant.39.clone.fine_ref.fine_hbm) | copy-start | bytes 786436
  4.6 32.8 %copy-start.2 = (f32[8,16,256]{2,1,0:T(8,128)S(1)}, f32[8,16,256]{2,1,0:T(8,128)}, u32[]{:S(2)}) copy-start(f32[8,16,256]{2,1,0:T(8,128)} %constant.40.clone.coarse_ref.coarse_hbm) | copy-start | bytes 393220
  4.6 32.8 %all-to-all-start = ((bf16[16,128,256]{2,1,0:T(8,128)(2,1)}), bf16[16,128,256]{2,1,0:T(8,128)(2,1)S(1)}, u32[]{:S(2)}, u32[]{:S(2)}) async-start(bf16[16,128,256]{2,1,0:T(8,128)(2,1)} %pack.1), calls=%async_computation | async-start | bytes 2097152 | tf_op jit(solution)/shard_map/all_to_all | solution.py:443
  14.3 0.9 copy-start.3
  46.2 2.9 %collective-permute-start = (bf16[1024,512]{1,0:T(8,128)(2,1)}, bf16[1024,512]{1,0:T(8,128)(2,1)S(1)}, u32[]{:S(2)}, u32[]{:S(2)}) collective-permute-start(bf16[1024,512]{1,0:T(8,128)(2,1)} %get-tuple-element.17), channel_id=1, source_target_pairs={{0,1},{1,0},{2,3},{3,2},{4,5},{5,4},{6,7},{7,6},{8,9},{9,8},{10,11... | collective-permute-start | bytes 3145736 | tf_op jit(solution)/shard_map/ppermute | solution.py:452
  49.1 1.0 copy-start.7
  72.5 32.4 %copy-start.6 = (s32[512]{0:T(512)S(1)}, s32[512]{0:T(512)}, u32[]{:S(2)}) copy-start(s32[512]{0:T(512)} %param.11) | copy-start | bytes 6148

commit v7 on v6

--- a/solution.py
+++ b/solution.py
@@ -41,36 +41,49 @@
     return jnp.dot(a, b, preferred_element_type=F32)
 
 
-def pack_kernel(blocks_ref, members_ref, spectra_ref, out_ref, ordered):
+def pack_kernel(blocks_hbm, members_hbm, spectra_hbm, out_ref, blocks_ref, members_ref, spectra_ref, ordered, sems):
     stations = spectra_ref.shape[1]
     b = out_ref.shape[1] // 2
+    copies = (
+        pltpu.make_async_copy(spectra_hbm, spectra_ref, sems.at[0]),
+        pltpu.make_async_copy(members_hbm, members_ref, sems.at[1]),
+        pltpu.make_async_copy(blocks_hbm, blocks_ref, sems.at[2]),
+    )
+    for copy in copies:
+        copy.start()
     station = lax.broadcasted_iota(jnp.int32, (stations, stations), 0)
+    copies[1].wait()
     chosen = (station == members_ref[...]).astype(F32).astype(BF16)
+    copies[0].wait()
     ordered[...] = lax.dot_general(
         chosen, spectra_ref[0], (((0,), (0,)), ((), ())), preferred_element_type=F32
     ).astype(BF16)
+    copies[2].wait()
     for p in range(out_ref.shape[0]):
         for side in range(2):
-            row = pl.multiple_of(blocks_ref[p, side] * b, b)
+            row = pl.multiple_of(blocks_ref[side, p] * b, b)
             out_ref[p, side * b:(side + 1) * b, :] = ordered[pl.ds(row, b), :]
 
 
 def pack(pair_blocks, members, spectra, b):
     _, stations, cols = spectra.shape
-    n_pairs = pair_blocks.shape[0]
+    n_pairs = pair_blocks.shape[1]
+    arrays = [pltpu.with_memory_space_constraint(x, pltpu.HBM) for x in (pair_blocks, members, spectra)]
     return pl.pallas_call(
         pack_kernel,
         out_shape=jax.ShapeDtypeStruct((n_pairs, 2 * b, cols), BF16),
-        in_specs=[
-            pl.BlockSpec(memory_space=pltpu.SMEM),
-            pl.BlockSpec(memory_space=pltpu.VMEM),
-            pl.BlockSpec(memory_space=pltpu.VMEM),
-        ],
+        in_specs=[pl.BlockSpec(memory_space=pltpu.HBM)] * 3,
         out_specs=pl.BlockSpec(memory_space=pltpu.VMEM),
-        scratch_shapes=[pltpu.VMEM((stations, cols), BF16)],
+        scratch_shapes=[
+            pltpu.SMEM(pair_blocks.shape, pair_blocks.dtype),
+            pltpu.VMEM(members.shape, members.dtype),
+            pltpu.VMEM(spectra.shape, BF16),
+            pltpu.VMEM((stations, cols), BF16),
+            pltpu.SemaphoreType.DMA((3,)),
+        ],
         compiler_params=pltpu.CompilerParams(vmem_limit_bytes=8 << 20),
         name="pack",
-    )(pair_blocks, members, spectra)
+    )(*arrays)
 
 
 def unpack_kernel(blocks_ref, members_ref, got_ref, out_ref, total):
@@ -79,7 +92,7 @@
     total[...] = jnp.zeros_like(total)
     for p in range(got_ref.shape[0]):
         for side in range(2):
-            rows = pl.ds(pl.multiple_of(blocks_ref[p, side] * b, b), b)
+            rows = pl.ds(pl.multiple_of(blocks_ref[side, p] * b, b), b)
             total[rows, :] += got_ref[p, side * b:(side + 1) * b, :].astype(F32)
     station = lax.broadcasted_iota(jnp.int32, (stations, stations), 0)
     chosen = (station == members_ref[...]).astype(F32).astype(BF16)
@@ -257,9 +270,9 @@
 
 
 def adjoint_kernel(
-    sizes, scalars_ref, mine_ref, other_hbm, seen_hbm, env_hbm, hilbert_hbm, kept_ref, fine_hbm, coarse_hbm, out_ref,
-    other_ref, seen_ref, env_ref, hilbert_ref, got_ref, fine_ref, coarse_ref, lagged, back, res, res_t, sums_a, sums_b,
-    turned_a, turned_b, rows_u, rows_v, sems_o, sems_s, sems_e, sems,
+    sizes, scalars_ref, mine_ref, other_ref, seen_hbm, env_hbm, hilbert_hbm, kept_ref, fine_hbm, coarse_hbm, out_ref,
+    seen_ref, env_ref, hilbert_ref, got_ref, fine_ref, coarse_ref, lagged, back, res, res_t, sums_a, sums_b,
+    turned_a, turned_b, rows_u, rows_v, sems_s, sems_e, sems,
 ):
     b, scale, group = sizes
     shares, days, _, cols = out_ref.shape
@@ -271,10 +284,8 @@
     left = left_lanes((n_fine, 2 * b))
 
     def bring(step):
-        at = pl.ds(pl.multiple_of(step * block, block), block)
         some = pl.ds(step * (group // 2), group // 2)
         return (
-            pltpu.make_async_copy(other_hbm.at[at], other_ref.at[at], sems_o.at[step]),
             pltpu.make_async_copy(seen_hbm.at[some], seen_ref.at[some], sems_s.at[step]),
             pltpu.make_async_copy(env_hbm.at[some], env_ref.at[some], sems_e.at[step]),
         )
@@ -396,11 +407,11 @@
     lanes = days * cols
     vmem = pl.BlockSpec(memory_space=pltpu.VMEM)
     hbm = pl.BlockSpec(memory_space=pltpu.HBM)
-    apart = [pltpu.with_memory_space_constraint(x, pltpu.HBM) for x in (other, seen, env, hilbert, kept, fine, coarse)]
+    apart = [pltpu.with_memory_space_constraint(x, pltpu.HBM) for x in (seen, env, hilbert, kept, fine, coarse)]
     return pl.pallas_call(
         functools.partial(adjoint_kernel, (b, scale, group)),
         out_shape=jax.ShapeDtypeStruct(kept.shape, BF16),
-        in_specs=[pl.BlockSpec(memory_space=pltpu.SMEM), vmem] + [hbm] * len(apart),
+        in_specs=[pl.BlockSpec(memory_space=pltpu.SMEM), vmem, vmem] + [hbm] * len(apart),
         out_specs=vmem,
         scratch_shapes=[pltpu.VMEM(x.shape, x.dtype) for x in apart]
         + [
@@ -416,12 +427,11 @@
             pltpu.VMEM((b, lanes), F32),
             pltpu.SemaphoreType.DMA((parts,)),
             pltpu.SemaphoreType.DMA((parts,)),
-            pltpu.SemaphoreType.DMA((parts,)),
             pltpu.SemaphoreType.DMA((4,)),
         ],
         compiler_params=pltpu.CompilerParams(vmem_limit_bytes=24 << 20),
         name="adjoint",
-    )(scalars, mine, *apart)
+    )(scalars, mine, other, *apart)
 
 
 def body(spectra, observed, pair_blocks, members, day_mask):
@@ -432,6 +442,7 @@
     hilbert = hilbert_parts(lags)
     slot = lax.axis_index("slot")
     members = members.reshape(1, stations)
+    pair_blocks = pair_blocks.T
     first_day = lax.axis_index("outer") * slots * CORES + lax.axis_index("core")
     mask = lax.dynamic_slice_in_dim(day_mask, slot, 1, 0)[0].astype(F32)
     mask_here = jnp.stack([lax.dynamic_index_in_dim(mask, first_day + k * CORES, 0, False) for k in range(slots)])

time: 108 us -> 104 us (0.963)
  local copies, waits for them, and re-layouts: 5.01 us -> 1.59 us
    unnamed x19 -> x14, local copies, waits for them, and re-layouts: 4.42 us -> 0.93 us
where the time goes in v7:
time: 104 us
  Pallas kernels  39.8 us (38%)
  blocking collectives  32.4 us (31%)
  waiting for transfers between devices  18.3 us (18%)
  starting transfers between devices  8.53 us (8%)
  other arithmetic  2.78 us (3%)
  local copies, waits for them, and re-layouts  1.59 us (2%)
    all_to_all x1, blocking collectives, body(): lax.all_to_all(contrib.reshape(shares * slots, 2 * b, cols), ('pairs', 's...  32.4 us
    pallas_call x1, Pallas kernels, adjoint_pass(): pl.pallas_call(functools.partial(adjoint_kernel, (b, scale, group)), out_...  22.3 us
    all_to_all x1, waiting for transfers between devices, body(): got = lax.all_to_all(sent, ('pairs', 'slot'), 0, 0, tiled=True)  16.2 us
    pallas_call x1, Pallas kernels, forward_pass(): pl.pallas_call(functools.partial(forward_kernel, b), out_shape=[pltpu.VME...  8.75 us
    all_to_all x1, starting transfers between devices, body(): got = lax.all_to_all(sent, ('pairs', 'slot'), 0, 0, tiled=True)  8.46 us
    pallas_call x1, Pallas kernels, prepare(): pl.pallas_call(functools.partial(prepare_kernel, b), out_shape=[pltpu.HBM...  3.85 us
    pallas_call x1, Pallas kernels, pack(): pl.pallas_call(pack_kernel, out_shape=jax.ShapeDtypeStruct((n_pairs, 2 *...  2.55 us
    pallas_call x1, Pallas kernels, unpack(): pl.pallas_call(unpack_kernel, out_shape=jax.ShapeDtypeStruct((1, stations...  2.3 us
  transfers between devices with their start and end apart: 2, of which 2 were waited for; matrix products, arithmetic and copies ran while one was open for 3% of the time, Pallas kernels for 4%

profile of v7, /device:TPU:0, one launch (start us, length us, event | category | flops | bytes accessed | tf_op | source)
XLA Modules:
  0.0 104.1 jit_solution(6981145330151416047)
XLA Ops:
  0.0 0.0 copy-start.6
  0.0 0.0 copy-start
  0.0 2.5 %pack.1 = bf16[16,128,256]{2,1,0:T(8,128)(2,1)} custom-call(s32[2,16]{1,0:T(2,128)} %bitcast.14, s32[1,512]{1,0:T(1,128)} %bitcast.12, bf16[1,512,256]{2,1,0:T(8,128)(2,1)} %spectra_hbm.1), custom_call_target="tpu_custom_call" | custom-call | tf_op jit(solution)/shard_map/pack/pallas_call | solution.py:72
  2.6 0.0 copy-start.1
  2.6 0.0 copy-start.2
  2.6 8.5 %all-to-all-start = ((bf16[16,128,256]{2,1,0:T(8,128)(2,1)}), bf16[16,128,256]{2,1,0:T(8,128)(2,1)S(1)}, u32[]{:S(2)}, u32[]{:S(2)}) async-start(bf16[16,128,256]{2,1,0:T(8,128)(2,1)} %pack.1), calls=%async_computation | async-start | bytes 2097152 | tf_op jit(solution)/shard_map/all_to_all | solution.py:454
  11.1 0.0 copy-done.6
  11.1 0.6 fusion.1
  11.7 0.7 constant_dynamic-slice_fusion.1
  12.4 0.0 copy-done
  12.4 0.0 copy-start.3
  12.4 0.9 copy-done.3
  13.3 3.9 %prepare.1 = (bf16[32,128,128]{2,1,0:T(8,128)(2,1)}, f32[32,128,128]{2,1,0:T(8,128)}) custom-call(s32[1]{0:T(128)} %bitcast.6.slot_ref, bf16[2,4096,128]{2,1,0:T(8,128)(2,1)S(1)} %bitcast.11, bf16[128,384]{1,0:T(8,128)(2,1)S(1)} %copy-done.3), custom_call_target="tpu_custom_call" | custom-call | flops 134217728 | bytes 4194304 | tf_op jit(solution)/shard_map/prepare/pallas_call | solution.py:153
  17.1 2.1 %broadcast_divide_fusion = (f32[2]{0:T(128)S(1)}, f32[2]{0:T(128)S(1)}) fusion(f32[]{:T(128)} %get-tuple-element.23, f32[1]{0:T(128)} %bitcast.3, f32[1]{0:T(128)} %bitcast.2), kind=kLoop, calls=%fused_computation.6 | loop fusion | flops 4 | bytes 28 | tf_op jit(solution)/shard_map/div | solution.py:451
  19.2 16.2 %all-to-all-done = bf16[16,128,256]{2,1,0:T(8,128)(2,1)S(1)} async-done(((bf16[16,128,256]{2,1,0:T(8,128)(2,1)}), bf16[16,128,256]{2,1,0:T(8,128)(2,1)S(1)}, u32[]{:S(2)}, u32[]{:S(2)}) %all-to-all-start) | async-done | bytes 1048608 | tf_op jit(solution)/shard_map/all_to_all | solution.py:454
  35.4 0.0 copy-done.1
  35.4 0.0 copy-done.2
  35.4 8.7 %forward.1 = (f32[1024,512]{1,0:T(8,128)S(1)}, bf16[1024,512]{1,0:T(8,128)(2,1)}, bf16[8,2,128,256]{3,2,1,0:T(8,128)(2,1)}) custom-call(f32[2]{0:T(128)S(1)} %get-tuple-element.22.mask_ref, bf16[8,2,128,256]{3,2,1,0:T(8,128)(2,1)S(1)} %bitcast.10, f32[8,32,256]{2,1,0:T(8,128)S(1)} %copy-done.1, f32[8,16,256]{2,1,0:T(8,128)S(1)} %copy-done.2), custom_call_target="tpu_custom_call" | custom-call | tf_op jit(solution)/shard_map/forward/pallas_call | solution.py:249
  44.1 0.1 collective-permute-start
  44.9 0.1 pad_maximum_fusion.1.scalars_ref
  45.0 2.1 %collective-permute-done.other_ref = bf16[1024,512]{1,0:T(8,128)(2,1)S(1)} collective-permute-done((bf16[1024,512]{1,0:T(8,128)(2,1)}, bf16[1024,512]{1,0:T(8,128)(2,1)S(1)}, u32[]{:S(2)}, u32[]{:S(2)}) %collective-permute-start) | collective-permute-done | bytes 1048608 | tf_op jit(solution)/shard_map/ppermute | solution.py:463
  47.1 22.3 %adjoint.1 = bf16[8,2,128,256]{3,2,1,0:T(8,128)(2,1)S(1)} custom-call(f32[3]{0:T(128)S(1)} %pad_maximum_fusion.1.scalars_ref, f32[1024,512]{1,0:T(8,128)S(1)} %get-tuple-element.16.mine_ref, bf16[1024,512]{1,0:T(8,128)(2,1)S(1)} %collective-permute-done.other_ref, bf16[32,128,128]{2,1,0:T(8,128)(2,1)} %get-tuple-element.18.seen_hbm, ...), custom_call_target="tpu_custom_call" | custom-call | tf_op jit(solution)/shard_map/adjoint/pallas_call | solution.py:411
  69.4 0.0 copy-start.4
  69.4 0.0 copy-start.5
  69.4 32.4 %all_to_all.10.got_ref = bf16[16,128,256]{2,1,0:T(8,128)(2,1)S(1)} all-to-all(bf16[16,128,256]{2,1,0:T(8,128)(2,1)S(1)} %bitcast.9), channel_id=1, replica_groups=mesh['pairs'=8,'outer'=1,'slot'=2,'core'=2] {'pairs','slot'}, dimensions={0} | all-to-all | bytes 2097152 | tf_op jit(solution)/shard_map/all_to_all | solution.py:469
  101.8 0.0 copy-done.4
  101.8 0.0 copy-done.5
  101.8 2.3 %unpack.1 = f32[1,512,256]{2,1,0:T(8,128)} custom-call(s32[2,16]{1,0:T(2,128)S(1)} %bitcast.15, s32[1,512]{1,0:T(1,128)S(1)} %bitcast.13, bf16[16,128,256]{2,1,0:T(8,128)(2,1)S(1)} %all_to_all.10.got_ref), custom_call_target="tpu_custom_call" | custom-call | tf_op jit(solution)/shard_map/unpack/pallas_call | solution.py:109
Async XLA Ops:
  0.0 11.1 %copy-start.6 = (s32[2,4]{1,0:T(2,128)S(1)}, s32[2,4]{1,0:T(2,128)}, u32[]{:S(2)}) copy-start(s32[2,4]{1,0:T(2,128)} %param.12) | copy-start | bytes 100
  0.0 12.4 %copy-start = (bf16[2,64,64,128]{3,2,1,0:T(8,128)(2,1)S(1)}, bf16[2,64,64,128]{3,2,1,0:T(8,128)(2,1)}, u32[]{:S(2)}) copy-start(bf16[2,64,64,128]{3,2,1,0:T(8,128)(2,1)} %param.9) | copy-start | bytes 6291460
  2.6 32.8 %copy-start.1 = (f32[8,32,256]{2,1,0:T(8,128)S(1)}, f32[8,32,256]{2,1,0:T(8,128)}, u32[]{:S(2)}) copy-start(f32[8,32,256]{2,1,0:T(8,128)} %constant.39.clone.fine_ref.fine_hbm) | copy-start | bytes 786436
  2.6 32.8 %copy-start.2 = (f32[8,16,256]{2,1,0:T(8,128)S(1)}, f32[8,16,256]{2,1,0:T(8,128)}, u32[]{:S(2)}) copy-start(f32[8,16,256]{2,1,0:T(8,128)} %constant.40.clone.coarse_ref.coarse_hbm) | copy-start | bytes 393220
  2.6 32.8 %all-to-all-start = ((bf16[16,128,256]{2,1,0:T(8,128)(2,1)}), bf16[16,128,256]{2,1,0:T(8,128)(2,1)S(1)}, u32[]{:S(2)}, u32[]{:S(2)}) async-start(bf16[16,128,256]{2,1,0:T(8,128)(2,1)} %pack.1), calls=%async_computation | async-start | bytes 2097152 | tf_op jit(solution)/shard_map/all_to_all | solution.py:454
  12.4 0.9 copy-start.3
  44.1 2.9 %collective-permute-start = (bf16[1024,512]{1,0:T(8,128)(2,1)}, bf16[1024,512]{1,0:T(8,128)(2,1)S(1)}, u32[]{:S(2)}, u32[]{:S(2)}) collective-permute-start(bf16[1024,512]{1,0:T(8,128)(2,1)} %get-tuple-element.17), channel_id=1, source_target_pairs={{0,1},{1,0},{2,3},{3,2},{4,5},{5,4},{6,7},{7,6},{8,9},{9,8},{10,11... | collective-permute-start | bytes 3145736 | tf_op jit(solution)/shard_map/ppermute | solution.py:463
  69.4 32.4 %copy-start.4 = (s32[512]{0:T(512)S(1)}, s32[512]{0:T(512)}, u32[]{:S(2)}) copy-start(s32[512]{0:T(512)} %param.11) | copy-start | bytes 6148
  69.4 32.4 %copy-start.5 = (s32[16,2]{0,1:T(2,128)S(1)}, s32[16,2]{0,1:T(2,128)}, u32[]{:S(2)}) copy-start(s32[16,2]{0,1:T(2,128)} %param.10) | copy-start | bytes 388

commit v8 on v7

--- a/solution.py
+++ b/solution.py
@@ -17,16 +17,34 @@
 BF16 = jnp.bfloat16
 
 
-def hilbert_parts(lags):
+def lag_order(lags, n_fine):
+    n_coarse = lags // n_fine
+    half_f, half_c = n_fine // 2, n_coarse // 2
+    fine = np.concatenate([half_f + np.arange(half_f), half_f - 1 - np.arange(half_f)])
+    coarse = np.concatenate([half_c + np.arange(half_c), half_c - 1 - np.arange(half_c)])
+    return (n_fine * coarse[:, None] + fine[None, :]).reshape(-1)
+
+
+def split_bf16(table):
+    high = table.astype(ml_dtypes.bfloat16)
+    return high, (table - high.astype(np.float32)).astype(ml_dtypes.bfloat16)
+
+
+def hilbert_parts(lags, n_fine):
     offset = (np.arange(lags)[None, :] - np.arange(lags)[:, None]) % lags
     angles = np.float32(math.pi) * offset.astype(np.float32) / np.float32(lags)
     odd = offset % 2 == 1
     safe = np.where(odd, np.sin(angles), np.float32(1.0))
     table = np.where(odd, np.float32(2.0 / lags) * np.cos(angles) / safe, np.float32(0.0))
     table = table.astype(np.float32).T
-    high = table.astype(ml_dtypes.bfloat16)
-    low = (table - high.astype(np.float32)).astype(ml_dtypes.bfloat16)
-    return np.concatenate([high, low, high], axis=1)
+    order = lag_order(lags, n_fine)
+    high, low = split_bf16(table[order])
+    chosen = np.eye(lags, dtype=np.float32)[order].astype(ml_dtypes.bfloat16)
+    high_both, low_both = split_bf16(table[order][:, order])
+    return (
+        np.concatenate([chosen, high, low], axis=0),
+        np.concatenate([high_both, low_both, high_both], axis=1),
+    )
 
 
 def left_lanes(shape):
@@ -121,22 +139,23 @@
     )(pair_blocks, members, got)
 
 
-def prepare_kernel(b, slot_ref, observed_ref, hilbert_ref, seen_ref, env_ref):
+def prepare_kernel(b, slot_ref, observed_ref, orders_ref, seen_ref, env_ref):
     lags = observed_ref.shape[1]
     two = 2 * b
 
     def some(step, carry):
-        seen = observed_ref[pl.ds(pl.multiple_of(step * two, two), two), :].astype(F32).T
-        seen_b = seen.astype(BF16)
-        hil = dot(hilbert_ref[:, :2 * lags], jnp.concatenate([seen_b, seen_b], axis=0))
-        seen_ref[step] = seen_b
+        rows = observed_ref[pl.ds(pl.multiple_of(step * two, two), two), :]
+        turned = lax.dot_general(orders_ref[...], rows, (((1,), (1,)), ((), ())), preferred_element_type=F32)
+        seen = turned[:lags]
+        hil = turned[lags:2 * lags] + turned[2 * lags:]
+        seen_ref[step] = seen.astype(BF16)
         env_ref[step] = 1.0 + jnp.sqrt(seen * seen + hil * hil)
         return carry
 
     lax.fori_loop(0, seen_ref.shape[0], some, 0, unroll=4)
 
 
-def prepare(slot, observed, hilbert, parts):
+def prepare(slot, observed, orders, parts):
     _, rows, lags = observed.shape
     b = math.isqrt(rows)
     shape = (b // 2, lags, 2 * b)
@@ -146,7 +165,7 @@
         grid=(parts,),
         in_specs=[
             pl.BlockSpec((None, rows // parts, lags), lambda s, slot_ref: (slot_ref[0], s, 0)),
-            pl.BlockSpec(hilbert.shape, lambda s, slot_ref: (0, 0)),
+            pl.BlockSpec(orders.shape, lambda s, slot_ref: (0, 0)),
         ],
         out_specs=[pl.BlockSpec(block, lambda s, slot_ref: (s, 0, 0))] * 2,
     )
@@ -157,7 +176,7 @@
         compiler_params=pltpu.CompilerParams(vmem_limit_bytes=8 << 20),
         cost_estimate=pl.CostEstimate(flops=2 * rows * lags * lags, bytes_accessed=8 * rows * lags, transcendentals=0),
         name="prepare",
-    )(slot, observed, hilbert)
+    )(slot, observed, orders)
 
 
 def tile_lanes(tiles, d, t):
@@ -171,37 +190,47 @@
 def turn_columns(got_ref, share, b, table_ref, into):
     _, days, _, cols = got_ref.shape
     tiles = cols // TILE
-    n = table_ref.shape[1] // 2
+    half = table_ref.shape[1] // 2
     for d in range(days):
         for t in range(tiles):
             at = tile_lanes(tiles, d, t)
             u = got_ref[share, d, b:, part(t)].astype(F32)
             v = swap_halves(u)
-            for k in range(n):
-                cosine = table_ref[share, k:k + 1, part(t)]
-                sine = table_ref[share, n + k:n + k + 1, part(t)]
-                into[k * b:(k + 1) * b, at] = (u * cosine + v * sine).astype(BF16)
+            for k in range(half):
+                one = u * table_ref[share, k:k + 1, part(t)]
+                two = v * table_ref[share, half + k:half + k + 1, part(t)]
+                into[k * b:(k + 1) * b, at] = (one + two).astype(BF16)
+                into[(half + k) * b:(half + k + 1) * b, at] = (one - two).astype(BF16)
 
 
 def turn_rows(got_ref, share, b, table_ref, into, rows_u, rows_v, mask_ref=None):
     _, days, _, cols = got_ref.shape
     tiles = cols // TILE
-    n = table_ref.shape[1] // 2
+    half = table_ref.shape[1] // 2 - 1
     pieces = [(d, t) for d in range(days) for t in range(tiles)]
     for d, t in pieces:
         at = tile_lanes(tiles, d, t)
         u = got_ref[share, d, :b, part(t)].astype(F32)
         if mask_ref is not None:
             u = u * mask_ref[d]
+        u = turn_half(u, table_ref, share, t, 1)
         rows_u[:, at] = u
         rows_v[:, at] = swap_halves(u)
     for d, t in pieces:
         at = tile_lanes(tiles, d, t)
-        cosine = table_ref[share, :n, part(t)]
-        sine = table_ref[share, n:, part(t)]
+        cosine = table_ref[share, :half, part(t)]
+        sine = table_ref[share, half:2 * half, part(t)]
         for k in range(b):
-            value = rows_u[k:k + 1, at] * cosine + rows_v[k:k + 1, at] * sine
-            into[k * n:(k + 1) * n, at] = value.astype(BF16)
+            one = rows_u[k:k + 1, at] * cosine
+            two = rows_v[k:k + 1, at] * sine
+            into[2 * k * half:2 * (k + 1) * half, at] = jnp.concatenate([one + two, one - two], axis=0).astype(BF16)
+
+
+def turn_half(u, table_ref, share, t, sign):
+    at = table_ref.shape[1] - 2
+    one = u * table_ref[share, at:at + 1, part(t)]
+    two = swap_halves(u) * table_ref[share, at + 1:at + 2, part(t)]
+    return one + two if sign > 0 else one - two
 
 
 def forward_kernel(
@@ -243,8 +272,8 @@
     shares, days, rows, cols = got.shape
     assert shares % 2 == 0
     b = rows // 2
-    n_fine = fine.shape[1] // 2
-    n_coarse = coarse.shape[1] // 2
+    n_fine = fine.shape[1] - 2
+    n_coarse = coarse.shape[1]
     vmem = pl.BlockSpec(memory_space=pltpu.VMEM)
     return pl.pallas_call(
         functools.partial(forward_kernel, b),
@@ -276,8 +305,8 @@
 ):
     b, scale, group = sizes
     shares, days, _, cols = out_ref.shape
-    n_fine = fine_ref.shape[1] // 2
-    n_coarse = coarse_ref.shape[1] // 2
+    n_fine = fine_ref.shape[1] - 2
+    n_coarse = coarse_ref.shape[1]
     slabs = n_coarse // 2
     tiles = cols // TILE
     block = group * n_fine
@@ -347,17 +376,21 @@
     lax.fori_loop(0, n_fine, round_rows, 0)
 
     def collect(share, side, table, n, sums):
+        half = n // 2
         for d in range(days):
             for t in range(tiles):
                 at = tile_lanes(tiles, d, t)
                 p = jnp.zeros((b, TILE), F32)
                 q = jnp.zeros((b, TILE), F32)
-                for k in range(n):
-                    h = sums[k * b:(k + 1) * b, at]
-                    p = p + h * table[share, k:k + 1, part(t)]
-                    q = q + h * table[share, n + k:n + k + 1, part(t)]
-                value = (p + swap_halves(q)) * (scalars_ref[d] * scale)
-                out_ref[share, d, side * b:(side + 1) * b, part(t)] = value.astype(BF16)
+                for k in range(half):
+                    one = sums[k * b:(k + 1) * b, at]
+                    two = sums[(half + k) * b:(half + k + 1) * b, at]
+                    p = p + (one + two) * table[share, k:k + 1, part(t)]
+                    q = q + (one - two) * table[share, half + k:half + k + 1, part(t)]
+                value = p + swap_halves(q)
+                if side == 0:
+                    value = turn_half(value, table, share, t, -1)
+                out_ref[share, d, side * b:(side + 1) * b, part(t)] = (value * (scalars_ref[d] * scale)).astype(BF16)
 
     for copy in later:
         copy.wait()
@@ -377,31 +410,33 @@
     collect(shares - 1, 1, coarse_ref, n_coarse, sums_b)
 
 
-def turn_tables(columns, lags, shares):
+def turn_tables(columns, lags, shares, n_fine):
     freqs = columns // 2
-    n_fine = 16
     n_coarse = lags // n_fine
     column = np.arange(columns)
     frequency = column // TILE * HALF + column % HALF
     is_real = column % TILE < HALF
 
-    def table(steps, sign):
-        phase = frequency[None, :] * steps[:, None] % (2 * freqs)
-        angles = np.pi * phase / freqs
+    def table(halves, sign):
+        phase = frequency[None, :] * halves[:, None] % (4 * freqs)
+        angles = np.pi * phase / (2 * freqs)
         sine = np.where(is_real[None, :], -sign, sign) * np.sin(angles)
-        rows = np.concatenate([np.cos(angles), sine]).astype(np.float32)
-        return rows.reshape(rows.shape[0], shares, columns // shares).transpose(1, 0, 2)
-
-    fine = table(np.arange(n_fine), 1)
-    coarse = table(n_fine * np.arange(n_coarse) - lags // 2, -1)
-    return np.ascontiguousarray(fine), np.ascontiguousarray(coarse)
+        return np.concatenate([np.cos(angles), sine])
+
+    def place(rows):
+        rows = rows.astype(np.float32).reshape(rows.shape[0], shares, columns // shares)
+        return np.ascontiguousarray(rows.transpose(1, 0, 2))
+
+    fine = table(2 * np.arange(n_fine // 2) + 1, 1)
+    coarse = table(n_fine * (2 * np.arange(n_coarse // 2) + 1), -1)
+    return place(np.concatenate([fine, table(np.array([1]), -1)])), place(coarse)
 
 
 def adjoint_pass(scalars, mine, other, seen, env, hilbert, kept, fine, coarse, parts):
     shares, days, rows, cols = kept.shape
     b = rows // 2
-    n_fine = fine.shape[1] // 2
-    n_coarse = coarse.shape[1] // 2
+    n_fine = fine.shape[1] - 2
+    n_coarse = coarse.shape[1]
     scale = 1.0 / math.sqrt(shares * cols // 2)
     group = b // parts
     lanes = days * cols
@@ -438,8 +473,9 @@
     shares = lax.axis_size("pairs")
     slots, b, _, lags = observed.shape
     _, stations, cols = spectra.shape
-    fine, coarse = turn_tables(shares * cols, lags, shares)
-    hilbert = hilbert_parts(lags)
+    n_fine = 16
+    fine, coarse = turn_tables(shares * cols, lags, shares, n_fine)
+    orders, hilbert = hilbert_parts(lags, n_fine)
     slot = lax.axis_index("slot")
     members = members.reshape(1, stations)
     pair_blocks = pair_blocks.T
@@ -454,8 +490,8 @@
     got = lax.all_to_all(sent, ("pairs", "slot"), 0, 0, tiled=True)
     got = got.reshape(shares, slots, 2 * b, cols)
     parts = 4
-    hilbert, fine, coarse = [jnp.asarray(x) for x in (hilbert, fine, coarse)]
-    seen, env = prepare(slot[None], observed.reshape(slots, b * b, lags), hilbert, parts)
+    orders, hilbert, fine, coarse = [jnp.asarray(x) for x in (orders, hilbert, fine, coarse)]
+    seen, env = prepare(slot[None], observed.reshape(slots, b * b, lags), orders, parts)
     got, seen, env = lax.optimization_barrier((got, seen, env))
     mine, sent, kept = forward_pass(mask_here, got, fine, coarse)
     for axis in ("outer", "core"):

time: 104 us -> 103 us (level)
  Pallas kernels: 39.8 us -> 37.8 us
  waiting for transfers between devices: 18.3 us -> 19.4 us
    pallas_call x1, Pallas kernels: 22.3 us -> 20.8 us  [adjoint_pass(): pl.pallas_call(functools.partial(adjoint_kernel, (b, scale, group)), out_...]
    all_to_all x1, waiting for transfers between devices: 16.2 us -> 17.3 us  [body(): got = lax.all_to_all(sent, ('pairs', 'slot'), 0, 0, tiled=True)]
where the time goes in v8:
time: 103 us; the launch traced here: 102 us
  Pallas kernels  37.8 us (37%)
  blocking collectives  32.4 us (31%)
  waiting for transfers between devices  19.4 us (19%)
  starting transfers between devices  8.54 us (8%)
  other arithmetic  2.78 us (3%)
    all_to_all x1, blocking collectives, body(): lax.all_to_all(contrib.reshape(shares * slots, 2 * b, cols), ('pairs', 's...  32.4 us
    pallas_call x1, Pallas kernels, adjoint_pass(): pl.pallas_call(functools.partial(adjoint_kernel, (b, scale, group)), out_...  20.8 us
    all_to_all x1, waiting for transfers between devices, body(): got = lax.all_to_all(sent, ('pairs', 'slot'), 0, 0, tiled=True)  17.3 us
    pallas_call x1, Pallas kernels, forward_pass(): pl.pallas_call(functools.partial(forward_kernel, b), out_shape=[pltpu.VME...  8.54 us
    all_to_all x1, starting transfers between devices, body(): got = lax.all_to_all(sent, ('pairs', 'slot'), 0, 0, tiled=True)  8.47 us
    pallas_call x1, Pallas kernels, prepare(): pl.pallas_call(functools.partial(prepare_kernel, b), out_shape=[pltpu.HBM...  3.62 us
    pallas_call x1, Pallas kernels, pack(): pl.pallas_call(pack_kernel, out_shape=jax.ShapeDtypeStruct((n_pairs, 2 *...  2.54 us
    pallas_call x1, Pallas kernels, unpack(): pl.pallas_call(unpack_kernel, out_shape=jax.ShapeDtypeStruct((1, stations...  2.31 us
  transfers between devices with their start and end apart: 2, of which 2 were waited for; matrix products, arithmetic and copies ran while one was open for 3% of the time, Pallas kernels for 4%

profile of v8, /device:TPU:0, one launch (start us, length us, event | category | flops | bytes accessed | tf_op | source)
XLA Modules:
  0.0 102.4 jit_solution(9408043872553687510)
XLA Ops:
  0.0 0.0 copy-start.3
  0.0 0.0 copy-start.6
  0.0 0.0 copy-start
  0.0 2.5 %pack.1 = bf16[16,128,256]{2,1,0:T(8,128)(2,1)} custom-call(s32[2,16]{1,0:T(2,128)} %bitcast.14, s32[1,512]{1,0:T(1,128)} %bitcast.12, bf16[1,512,256]{2,1,0:T(8,128)(2,1)} %spectra_hbm.1), custom_call_target="tpu_custom_call" | custom-call | tf_op jit(solution)/shard_map/pack/pallas_call | solution.py:90
  2.6 0.0 copy-start.1
  2.6 0.0 copy-start.2
  2.6 8.5 %all-to-all-start = ((bf16[16,128,256]{2,1,0:T(8,128)(2,1)}), bf16[16,128,256]{2,1,0:T(8,128)(2,1)S(1)}, u32[]{:S(2)}, u32[]{:S(2)}) async-start(bf16[16,128,256]{2,1,0:T(8,128)(2,1)} %pack.1), calls=%async_computation | async-start | bytes 2097152 | tf_op jit(solution)/shard_map/all_to_all | solution.py:490
  11.1 0.0 copy-done.6
  11.1 0.6 fusion.1
  11.7 0.7 constant_dynamic-slice_fusion.1
  12.4 0.0 copy-done.3
  12.4 0.0 copy-done
  12.4 3.6 %prepare.1 = (bf16[32,128,128]{2,1,0:T(8,128)(2,1)}, f32[32,128,128]{2,1,0:T(8,128)}) custom-call(s32[1]{0:T(128)} %bitcast.6.slot_ref, bf16[2,4096,128]{2,1,0:T(8,128)(2,1)S(1)} %bitcast.11, bf16[384,128]{1,0:T(8,128)(2,1)S(1)} %copy-done.3), custom_call_target="tpu_custom_call" | custom-call | flops 134217728 | bytes 4194304 | tf_op jit(solution)/shard_map/prepare/pallas_call | solution.py:172
  16.0 2.1 %broadcast_divide_fusion = (f32[2]{0:T(128)S(1)}, f32[2]{0:T(128)S(1)}) fusion(f32[]{:T(128)} %get-tuple-element.23, f32[1]{0:T(128)} %bitcast.3, f32[1]{0:T(128)} %bitcast.2), kind=kLoop, calls=%fused_computation.6 | loop fusion | flops 4 | bytes 28 | tf_op jit(solution)/shard_map/div | solution.py:487
  18.1 17.3 %all-to-all-done = bf16[16,128,256]{2,1,0:T(8,128)(2,1)S(1)} async-done(((bf16[16,128,256]{2,1,0:T(8,128)(2,1)}), bf16[16,128,256]{2,1,0:T(8,128)(2,1)S(1)}, u32[]{:S(2)}, u32[]{:S(2)}) %all-to-all-start) | async-done | bytes 1048608 | tf_op jit(solution)/shard_map/all_to_all | solution.py:490
  35.4 0.0 copy-done.1
  35.4 0.0 copy-done.2
  35.4 8.5 %forward.1 = (f32[1024,512]{1,0:T(8,128)S(1)}, bf16[1024,512]{1,0:T(8,128)(2,1)}, bf16[8,2,128,256]{3,2,1,0:T(8,128)(2,1)}) custom-call(f32[2]{0:T(128)S(1)} %get-tuple-element.22.mask_ref, bf16[8,2,128,256]{3,2,1,0:T(8,128)(2,1)S(1)} %bitcast.10, f32[8,18,256]{2,1,0:T(8,128)S(1)} %copy-done.1, f32[8,8,256]{2,1,0:T(8,128)S(1)} %copy-done.2), custom_call_target="tpu_custom_call" | custom-call | tf_op jit(solution)/shard_map/forward/pallas_call | solution.py:278
  43.9 0.1 collective-permute-start
  44.7 0.1 pad_maximum_fusion.1.scalars_ref
  44.7 2.1 %collective-permute-done.other_ref = bf16[1024,512]{1,0:T(8,128)(2,1)S(1)} collective-permute-done((bf16[1024,512]{1,0:T(8,128)(2,1)}, bf16[1024,512]{1,0:T(8,128)(2,1)S(1)}, u32[]{:S(2)}, u32[]{:S(2)}) %collective-permute-start) | collective-permute-done | bytes 1048608 | tf_op jit(solution)/shard_map/ppermute | solution.py:499
  46.9 20.8 %adjoint.1 = bf16[8,2,128,256]{3,2,1,0:T(8,128)(2,1)S(1)} custom-call(f32[3]{0:T(128)S(1)} %pad_maximum_fusion.1.scalars_ref, f32[1024,512]{1,0:T(8,128)S(1)} %get-tuple-element.16.mine_ref, bf16[1024,512]{1,0:T(8,128)(2,1)S(1)} %collective-permute-done.other_ref, bf16[32,128,128]{2,1,0:T(8,128)(2,1)} %get-tuple-element.18.seen_hbm, ...), custom_call_target="tpu_custom_call" | custom-call | tf_op jit(solution)/shard_map/adjoint/pallas_call | solution.py:446
  67.7 0.0 copy-start.4
  67.7 0.0 copy-start.5
  67.7 32.4 %all_to_all.10.got_ref = bf16[16,128,256]{2,1,0:T(8,128)(2,1)S(1)} all-to-all(bf16[16,128,256]{2,1,0:T(8,128)(2,1)S(1)} %bitcast.9), channel_id=1, replica_groups=mesh['pairs'=8,'outer'=1,'slot'=2,'core'=2] {'pairs','slot'}, dimensions={0} | all-to-all | bytes 2097152 | tf_op jit(solution)/shard_map/all_to_all | solution.py:505
  100.1 0.0 copy-done.4
  100.1 0.0 copy-done.5
  100.1 2.3 %unpack.1 = f32[1,512,256]{2,1,0:T(8,128)} custom-call(s32[2,16]{1,0:T(2,128)S(1)} %bitcast.15, s32[1,512]{1,0:T(1,128)S(1)} %bitcast.13, bf16[16,128,256]{2,1,0:T(8,128)(2,1)S(1)} %all_to_all.10.got_ref), custom_call_target="tpu_custom_call" | custom-call | tf_op jit(solution)/shard_map/unpack/pallas_call | solution.py:127
Async XLA Ops:
  0.0 12.4 %copy-start.3 = (bf16[384,128]{1,0:T(8,128)(2,1)S(1)}, bf16[384,128]{1,0:T(8,128)(2,1)}, u32[]{:S(2)}) copy-start(bf16[384,128]{1,0:T(8,128)(2,1)} %constant.40.clone.orders_ref) | copy-start | bytes 294916
  0.0 11.1 %copy-start.6 = (s32[2,4]{1,0:T(2,128)S(1)}, s32[2,4]{1,0:T(2,128)}, u32[]{:S(2)}) copy-start(s32[2,4]{1,0:T(2,128)} %param.13) | copy-start | bytes 100
  0.0 12.4 %copy-start = (bf16[2,64,64,128]{3,2,1,0:T(8,128)(2,1)S(1)}, bf16[2,64,64,128]{3,2,1,0:T(8,128)(2,1)}, u32[]{:S(2)}) copy-start(bf16[2,64,64,128]{3,2,1,0:T(8,128)(2,1)} %param.10) | copy-start | bytes 6291460
  2.6 32.8 %copy-start.1 = (f32[8,18,256]{2,1,0:T(8,128)S(1)}, f32[8,18,256]{2,1,0:T(8,128)}, u32[]{:S(2)}) copy-start(f32[8,18,256]{2,1,0:T(8,128)} %constant.42.clone.fine_ref.fine_hbm) | copy-start | bytes 442372
  2.6 32.8 %copy-start.2 = (f32[8,8,256]{2,1,0:T(8,128)S(1)}, f32[8,8,256]{2,1,0:T(8,128)}, u32[]{:S(2)}) copy-start(f32[8,8,256]{2,1,0:T(8,128)} %constant.43.clone.coarse_ref.coarse_hbm) | copy-start | bytes 196612
  2.6 32.8 %all-to-all-start = ((bf16[16,128,256]{2,1,0:T(8,128)(2,1)}), bf16[16,128,256]{2,1,0:T(8,128)(2,1)S(1)}, u32[]{:S(2)}, u32[]{:S(2)}) async-start(bf16[16,128,256]{2,1,0:T(8,128)(2,1)} %pack.1), calls=%async_computation | async-start | bytes 2097152 | tf_op jit(solution)/shard_map/all_to_all | solution.py:490
  43.9 2.9 %collective-permute-start = (bf16[1024,512]{1,0:T(8,128)(2,1)}, bf16[1024,512]{1,0:T(8,128)(2,1)S(1)}, u32[]{:S(2)}, u32[]{:S(2)}) collective-permute-start(bf16[1024,512]{1,0:T(8,128)(2,1)} %get-tuple-element.17), channel_id=1, source_target_pairs={{0,1},{1,0},{2,3},{3,2},{4,5},{5,4},{6,7},{7,6},{8,9},{9,8},{10,11... | collective-permute-start | bytes 3145736 | tf_op jit(solution)/shard_map/ppermute | solution.py:499
  67.7 32.4 %copy-start.4 = (s32[512]{0:T(512)S(1)}, s32[512]{0:T(512)}, u32[]{:S(2)}) copy-start(s32[512]{0:T(512)} %param.12) | copy-start | bytes 6148
  67.7 32.4 %copy-start.5 = (s32[16,2]{0,1:T(2,128)S(1)}, s32[16,2]{0,1:T(2,128)}, u32[]{:S(2)}) copy-start(s32[16,2]{0,1:T(2,128)} %param.11) | copy-start | bytes 388

commit v9 on v8

--- a/solution.py
+++ b/solution.py
@@ -89,7 +89,7 @@
     arrays = [pltpu.with_memory_space_constraint(x, pltpu.HBM) for x in (pair_blocks, members, spectra)]
     return pl.pallas_call(
         pack_kernel,
-        out_shape=jax.ShapeDtypeStruct((n_pairs, 2 * b, cols), BF16),
+        out_shape=pltpu.VMEM((n_pairs, 2 * b, cols), BF16),
         in_specs=[pl.BlockSpec(memory_space=pltpu.HBM)] * 3,
         out_specs=pl.BlockSpec(memory_space=pltpu.VMEM),
         scratch_shapes=[
@@ -104,39 +104,58 @@
     )(*arrays)
 
 
-def unpack_kernel(blocks_ref, members_ref, got_ref, out_ref, total):
-    stations = out_ref.shape[1]
+def add_blocks(blocks_ref, got_ref, total):
     b = got_ref.shape[1] // 2
-    total[...] = jnp.zeros_like(total)
     for p in range(got_ref.shape[0]):
         for side in range(2):
             rows = pl.ds(pl.multiple_of(blocks_ref[side, p] * b, b), b)
             total[rows, :] += got_ref[p, side * b:(side + 1) * b, :].astype(F32)
+
+
+def gather_kernel(blocks_ref, got_ref, out_ref, total):
+    total[...] = jnp.zeros_like(total)
+    add_blocks(blocks_ref, got_ref, total)
+    out_ref[...] = total[...].astype(out_ref.dtype)
+
+
+def gather(pair_blocks, got, stations):
+    cols = got.shape[2]
+    vmem = pl.BlockSpec(memory_space=pltpu.VMEM)
+    return pl.pallas_call(
+        gather_kernel,
+        out_shape=jax.ShapeDtypeStruct((stations, cols), BF16),
+        in_specs=[pl.BlockSpec(memory_space=pltpu.SMEM), vmem],
+        out_specs=vmem,
+        scratch_shapes=[pltpu.VMEM((stations, cols), F32)],
+        compiler_params=pltpu.CompilerParams(vmem_limit_bytes=8 << 20),
+        name="gather",
+    )(pair_blocks, got)
+
+
+def unpack_kernel(blocks_ref, members_ref, got_ref, far_ref, out_ref, total):
+    stations = out_ref.shape[1]
+    total[...] = far_ref[...].astype(F32)
+    add_blocks(blocks_ref, got_ref, total)
     station = lax.broadcasted_iota(jnp.int32, (stations, stations), 0)
     chosen = (station == members_ref[...]).astype(F32).astype(BF16)
     whole = total[...]
     high = whole.astype(BF16)
-    rest = whole - high.astype(F32)
-    mid = rest.astype(BF16)
-    low = (rest - mid.astype(F32)).astype(BF16)
-    out_ref[0] = dot(chosen, high) + (dot(chosen, mid) + dot(chosen, low))
-
-
-def unpack(pair_blocks, members, got, stations):
-    cols = got.shape[2]
+    low = (whole - high.astype(F32)).astype(BF16)
+    out_ref[0] = dot(chosen, high) + dot(chosen, low)
+
+
+def unpack(pair_blocks, members, got, far):
+    stations, cols = far.shape
+    vmem = pl.BlockSpec(memory_space=pltpu.VMEM)
     return pl.pallas_call(
         unpack_kernel,
         out_shape=jax.ShapeDtypeStruct((1, stations, cols), F32),
-        in_specs=[
-            pl.BlockSpec(memory_space=pltpu.SMEM),
-            pl.BlockSpec(memory_space=pltpu.VMEM),
-            pl.BlockSpec(memory_space=pltpu.VMEM),
-        ],
-        out_specs=pl.BlockSpec(memory_space=pltpu.VMEM),
+        in_specs=[pl.BlockSpec(memory_space=pltpu.SMEM)] + [vmem] * 3,
+        out_specs=vmem,
         scratch_shapes=[pltpu.VMEM((stations, cols), F32)],
         compiler_params=pltpu.CompilerParams(vmem_limit_bytes=8 << 20),
         name="unpack",
-    )(pair_blocks, members, got)
+    )(pair_blocks, members, got, far)
 
 
 def prepare_kernel(b, slot_ref, observed_ref, orders_ref, seen_ref, env_ref):
@@ -298,17 +317,13 @@
     )(mask, got, fine, coarse)
 
 
-def adjoint_kernel(
-    sizes, scalars_ref, mine_ref, other_ref, seen_hbm, env_hbm, hilbert_hbm, kept_ref, fine_hbm, coarse_hbm, out_ref,
-    seen_ref, env_ref, hilbert_ref, got_ref, fine_ref, coarse_ref, lagged, back, res, res_t, sums_a, sums_b,
-    turned_a, turned_b, rows_u, rows_v, sems_s, sems_e, sems,
+def residual_stage(
+    b, group, scalars_ref, mine_ref, other_ref, seen_hbm, env_hbm, hilbert_hbm, seen_ref, env_ref, hilbert_ref, lagged,
+    back, res, res_t, sems_s, sems_e, sem, begin,
 ):
-    b, scale, group = sizes
-    shares, days, _, cols = out_ref.shape
-    n_fine = fine_ref.shape[1] - 2
-    n_coarse = coarse_ref.shape[1]
-    slabs = n_coarse // 2
-    tiles = cols // TILE
+    n_fine = mine_ref.shape[0] // b
+    slabs = mine_ref.shape[1] // TILE
+    days = scalars_ref.shape[0] - 1
     block = group * n_fine
     left = left_lanes((n_fine, 2 * b))
 
@@ -319,18 +334,12 @@
             pltpu.make_async_copy(env_hbm.at[some], env_ref.at[some], sems_e.at[step]),
         )
 
-    first = pltpu.make_async_copy(hilbert_hbm, hilbert_ref, sems.at[0])
-    later = (
-        pltpu.make_async_copy(kept_ref, got_ref, sems.at[1]),
-        pltpu.make_async_copy(fine_hbm, fine_ref, sems.at[2]),
-        pltpu.make_async_copy(coarse_hbm, coarse_ref, sems.at[3]),
-    )
+    first = pltpu.make_async_copy(hilbert_hbm, hilbert_ref, sem)
     first.start()
     for step in range(b // group):
         for copy in bring(step):
             copy.start()
-    for copy in later:
-        copy.start()
+    begin()
     first.wait()
 
     def residual_rows(step, carry):
@@ -375,6 +384,29 @@
 
     lax.fori_loop(0, n_fine, round_rows, 0)
 
+
+def adjoint_stage(
+    sizes, offset, scalars_ref, kept_ref, fine_hbm, coarse_hbm, out_ref, got_ref, fine_ref, coarse_ref, res, res_t,
+    sums_a, sums_b, turned_a, turned_b, rows_u, rows_v, sems, before,
+):
+    b, scale = sizes
+    shares, days, _, cols = out_ref.shape
+    n_fine = fine_ref.shape[1] - 2
+    n_coarse = coarse_ref.shape[1]
+    tiles = cols // TILE
+    some = pl.ds(offset, shares)
+    later = (
+        pltpu.make_async_copy(kept_ref.at[some], got_ref, sems.at[0]),
+        pltpu.make_async_copy(fine_hbm.at[some], fine_ref, sems.at[1]),
+        pltpu.make_async_copy(coarse_hbm.at[some], coarse_ref, sems.at[2]),
+    )
+
+    def begin():
+        for copy in later:
+            copy.start()
+
+    before(begin)
+
     def collect(share, side, table, n, sums):
         half = n // 2
         for d in range(days):
@@ -410,6 +442,55 @@
     collect(shares - 1, 1, coarse_ref, n_coarse, sums_b)
 
 
+def far_kernel(
+    sizes, offset_ref, scalars_ref, mine_ref, other_ref, seen_hbm, env_hbm, hilbert_hbm, kept_ref, fine_hbm, coarse_hbm,
+    out_ref, res_hbm, res_t_hbm, seen_ref, env_ref, hilbert_ref, lagged, back, got_ref, fine_ref, coarse_ref, res, res_t,
+    sums_a, sums_b, turned_a, turned_b, rows_u, rows_v, sems_s, sems_e, sems,
+):
+    b, scale, group = sizes
+    out = (
+        pltpu.make_async_copy(res, res_hbm, sems.at[4]),
+        pltpu.make_async_copy(res_t, res_t_hbm, sems.at[5]),
+    )
+
+    def before(begin):
+        residual_stage(
+            b, group, scalars_ref, mine_ref, other_ref, seen_hbm, env_hbm, hilbert_hbm, seen_ref, env_ref, hilbert_ref,
+            lagged, back, res, res_t, sems_s, sems_e, sems.at[3], begin,
+        )
+        for copy in out:
+            copy.start()
+
+    adjoint_stage(
+        (b, scale), offset_ref[0], scalars_ref, kept_ref, fine_hbm, coarse_hbm, out_ref, got_ref, fine_ref, coarse_ref,
+        res, res_t, sums_a, sums_b, turned_a, turned_b, rows_u, rows_v, sems, before,
+    )
+    for copy in out:
+        copy.wait()
+
+
+def near_kernel(
+    sizes, offset_ref, scalars_ref, res_hbm, res_t_hbm, kept_ref, fine_hbm, coarse_hbm, out_ref, got_ref, fine_ref,
+    coarse_ref, res, res_t, sums_a, sums_b, turned_a, turned_b, rows_u, rows_v, sems,
+):
+    copies = (
+        pltpu.make_async_copy(res_hbm, res, sems.at[3]),
+        pltpu.make_async_copy(res_t_hbm, res_t, sems.at[4]),
+    )
+
+    def before(begin):
+        for copy in copies:
+            copy.start()
+        begin()
+        for copy in copies:
+            copy.wait()
+
+    adjoint_stage(
+        sizes, offset_ref[0], scalars_ref, kept_ref, fine_hbm, coarse_hbm, out_ref, got_ref, fine_ref, coarse_ref, res,
+        res_t, sums_a, sums_b, turned_a, turned_b, rows_u, rows_v, sems, before,
+    )
+
+
 def turn_tables(columns, lags, shares, n_fine):
     freqs = columns // 2
     n_coarse = lags // n_fine
@@ -432,45 +513,80 @@
     return place(np.concatenate([fine, table(np.array([1]), -1)])), place(coarse)
 
 
-def adjoint_pass(scalars, mine, other, seen, env, hilbert, kept, fine, coarse, parts):
+def adjoint_scratch(kept, fine, coarse, part_shares):
+    _, days, rows, cols = kept.shape
+    b = rows // 2
+    n_fine = fine.shape[1] - 2
+    n_coarse = coarse.shape[1]
+    lanes = days * cols
+    return [pltpu.VMEM((part_shares,) + x.shape[1:], x.dtype) for x in (kept, fine, coarse)] + [
+        pltpu.VMEM((n_fine * b, n_coarse * b), BF16),
+        pltpu.VMEM((n_coarse * b, n_fine * b), BF16),
+        pltpu.VMEM((n_fine * b, lanes), F32),
+        pltpu.VMEM((n_coarse * b, lanes), F32),
+        pltpu.VMEM((n_fine * b, lanes), BF16),
+        pltpu.VMEM((n_coarse * b, lanes), BF16),
+        pltpu.VMEM((b, lanes), F32),
+        pltpu.VMEM((b, lanes), F32),
+    ]
+
+
+def far_pass(offset, scalars, mine, other, seen, env, hilbert, kept, fine, coarse, parts):
     shares, days, rows, cols = kept.shape
     b = rows // 2
     n_fine = fine.shape[1] - 2
     n_coarse = coarse.shape[1]
     scale = 1.0 / math.sqrt(shares * cols // 2)
     group = b // parts
-    lanes = days * cols
     vmem = pl.BlockSpec(memory_space=pltpu.VMEM)
     hbm = pl.BlockSpec(memory_space=pltpu.HBM)
+    smem = pl.BlockSpec(memory_space=pltpu.SMEM)
     apart = [pltpu.with_memory_space_constraint(x, pltpu.HBM) for x in (seen, env, hilbert, kept, fine, coarse)]
     return pl.pallas_call(
-        functools.partial(adjoint_kernel, (b, scale, group)),
-        out_shape=jax.ShapeDtypeStruct(kept.shape, BF16),
-        in_specs=[pl.BlockSpec(memory_space=pltpu.SMEM), vmem, vmem] + [hbm] * len(apart),
-        out_specs=vmem,
-        scratch_shapes=[pltpu.VMEM(x.shape, x.dtype) for x in apart]
+        functools.partial(far_kernel, (b, scale, group)),
+        out_shape=[
+            jax.ShapeDtypeStruct((shares // 2,) + kept.shape[1:], BF16),
+            pltpu.HBM((n_fine * b, n_coarse * b), BF16),
+            pltpu.HBM((n_coarse * b, n_fine * b), BF16),
+        ],
+        in_specs=[smem, smem, vmem, vmem] + [hbm] * len(apart),
+        out_specs=[vmem, hbm, hbm],
+        scratch_shapes=[pltpu.VMEM(x.shape, x.dtype) for x in apart[:3]]
         + [
             pltpu.VMEM((n_coarse // 2, n_fine * b, 2 * b), F32),
             pltpu.VMEM((group * n_fine, n_coarse * b), F32),
-            pltpu.VMEM((n_fine * b, n_coarse * b), BF16),
-            pltpu.VMEM((n_coarse * b, n_fine * b), BF16),
-            pltpu.VMEM((n_fine * b, lanes), F32),
-            pltpu.VMEM((n_coarse * b, lanes), F32),
-            pltpu.VMEM((n_fine * b, lanes), BF16),
-            pltpu.VMEM((n_coarse * b, lanes), BF16),
-            pltpu.VMEM((b, lanes), F32),
-            pltpu.VMEM((b, lanes), F32),
+        ]
+        + adjoint_scratch(kept, fine, coarse, shares // 2)
+        + [
             pltpu.SemaphoreType.DMA((parts,)),
             pltpu.SemaphoreType.DMA((parts,)),
-            pltpu.SemaphoreType.DMA((4,)),
+            pltpu.SemaphoreType.DMA((6,)),
         ],
         compiler_params=pltpu.CompilerParams(vmem_limit_bytes=24 << 20),
-        name="adjoint",
-    )(scalars, mine, other, *apart)
+        name="far",
+    )(offset, scalars, mine, other, *apart)
+
+
+def near_pass(offset, scalars, res, res_t, kept, fine, coarse):
+    shares, days, rows, cols = kept.shape
+    scale = 1.0 / math.sqrt(shares * cols // 2)
+    hbm = pl.BlockSpec(memory_space=pltpu.HBM)
+    smem = pl.BlockSpec(memory_space=pltpu.SMEM)
+    apart = [pltpu.with_memory_space_constraint(x, pltpu.HBM) for x in (res, res_t, kept, fine, coarse)]
+    return pl.pallas_call(
+        functools.partial(near_kernel, (rows // 2, scale)),
+        out_shape=jax.ShapeDtypeStruct((shares // 2,) + kept.shape[1:], BF16),
+        in_specs=[smem, smem] + [hbm] * len(apart),
+        out_specs=pl.BlockSpec(memory_space=pltpu.VMEM),
+        scratch_shapes=adjoint_scratch(kept, fine, coarse, shares // 2) + [pltpu.SemaphoreType.DMA((5,))],
+        compiler_params=pltpu.CompilerParams(vmem_limit_bytes=24 << 20),
+        name="near",
+    )(offset, scalars, *apart)
 
 
 def body(spectra, observed, pair_blocks, members, day_mask):
-    shares = lax.axis_size("pairs")
+    half_shares = lax.axis_size("near")
+    shares = 2 * half_shares
     slots, b, _, lags = observed.shape
     _, stations, cols = spectra.shape
     n_fine = 16
@@ -487,7 +603,7 @@
     scalars = jnp.concatenate([mask_here / count, scale / count[None]])
 
     sent = pack(pair_blocks, members, spectra, b)
-    got = lax.all_to_all(sent, ("pairs", "slot"), 0, 0, tiled=True)
+    got = lax.all_to_all(sent, ("half", "near", "slot"), 0, 0, tiled=True)
     got = got.reshape(shares, slots, 2 * b, cols)
     parts = 4
     orders, hilbert, fine, coarse = [jnp.asarray(x) for x in (orders, hilbert, fine, coarse)]
@@ -501,33 +617,48 @@
             for other in others:
                 mine = mine + other.astype(F32)
             sent = mine.astype(BF16)
-    contrib = adjoint_pass(scalars, mine, others[0], seen, env, hilbert, kept, fine, coarse, parts)
-    returned = lax.all_to_all(
-        contrib.reshape(shares * slots, 2 * b, cols), ("pairs", "slot"), 0, 0, tiled=True
-    )
-    return unpack(pair_blocks, members, returned, stations)
+    half = lax.axis_index("half")
+    own_blocks = lax.dynamic_slice_in_dim(pair_blocks, half * half_shares * slots, half_shares * slots, 1)
+
+    def exchange(contrib):
+        flat = contrib.reshape(half_shares * slots, 2 * b, cols)
+        return lax.all_to_all(flat, ("near", "slot"), 0, 0, tiled=True)
+
+    start_far = ((1 - half) * half_shares)[None]
+    start_near = (half * half_shares)[None]
+    contrib, res, res_t = far_pass(
+        start_far, scalars, mine, others[0], seen, env, hilbert, kept, fine, coarse, parts
+    )
+    got_far = exchange(contrib)
+    contrib = near_pass(start_near, scalars, res, res_t, kept, fine, coarse)
+    across = gather(own_blocks, got_far, stations)
+    contrib, across = lax.optimization_barrier((contrib, across))
+    across = lax.ppermute(across, "half", [(0, 1), (1, 0)])
+    got_near = exchange(contrib)
+    return unpack(own_blocks, members, got_near, across)
 
 
 def solution(mesh):
     shares, days = mesh.devices.shape
-    names = ("pairs", "outer", "slot", "core")
+    names = ("half", "near", "outer", "slot", "core")
 
     def run(spectra, observed, pair_blocks, members, day_mask):
         slots = observed.shape[0] // shares
-        split = (shares, days // CORES // slots, slots, CORES)
+        split = (2, shares // 2, days // CORES // slots, slots, CORES)
         finer = Mesh(mesh.devices.reshape(split), names)
-        day_axes = names[1:]
+        day_axes = names[2:]
+        pair_axes = names[:2]
         return jax.shard_map(
             body,
             mesh=finer,
             in_specs=(
-                P(day_axes, None, "pairs"),
-                P("pairs", None, None, None),
+                P(day_axes, None, pair_axes),
+                P(pair_axes, None, None, None),
                 P(),
                 P(),
-                P("pairs", None),
+                P(pair_axes, None),
             ),
-            out_specs=P(day_axes, None, "pairs"),
+            out_specs=P(day_axes, None, pair_axes),
             check_vma=False,
         )(spectra, observed, pair_blocks, members, day_mask)
 

time: 103 us -> 100 us (0.971)
  blocking collectives: 32.4 us -> 0 us
  waiting for transfers between devices: 19.4 us -> 32.7 us
  starting transfers between devices: 8.54 us -> 20.1 us
  Pallas kernels: 37.8 us -> 41.7 us
    all_to_all x1 -> x0, blocking collectives: 32.4 us -> none  [body(): lax.all_to_all(contrib.reshape(shares * slots, 2 * b, cols), ('pairs', 's...]
    ppermute x0 -> x1, waiting for transfers between devices: none -> 13.4 us  [body(): across = lax.ppermute(across, 'half', [(0, 1), (1, 0)])]
    all_to_all x1 -> x3, starting transfers between devices: 8.47 us -> 19.3 us  [the longest x2 10.8 us: exchange(): return lax.all_to_all(flat, ('near', 'slot'), 0, 0, tiled=True)]
    pallas_call x2 -> x4, Pallas kernels: 23.4 us -> 27.6 us  [the longest x1 13.8 us: far_pass(): pl.pallas_call(functools.partial(far_kernel, (b, scale, group)), out_shap...]
    all_to_all x1 -> x3, waiting for transfers between devices: 17.3 us -> 17.3 us  [the longest x1 17.3 us: body(): got = lax.all_to_all(sent, ('half', 'near', 'slot'), 0, 0, tiled=True)]
  transfers between devices with their start and end apart: 2 -> 5, of which waited for: 2 -> 3; matrix products, arithmetic and copies ran while one was open for 3% -> 4% of each run, Pallas kernels for 4% -> 14%
where the time goes in v9:
time: 100 us; the launch traced here: 99.6 us
  Pallas kernels  41.7 us (42%)
  waiting for transfers between devices  32.7 us (33%)
  starting transfers between devices  20.1 us (20%)
  other arithmetic  2.79 us (3%)
  local copies, waits for them, and re-layouts  1.55 us (2%)
    all_to_all x1, waiting for transfers between devices, body(): got = lax.all_to_all(sent, ('half', 'near', 'slot'), 0, 0, tiled=True)  17.3 us
    pallas_call x1, Pallas kernels, far_pass(): pl.pallas_call(functools.partial(far_kernel, (b, scale, group)), out_shap...  13.8 us
    ppermute x1, waiting for transfers between devices, body(): across = lax.ppermute(across, 'half', [(0, 1), (1, 0)])  13.4 us
    all_to_all x2, starting transfers between devices, exchange(): return lax.all_to_all(flat, ('near', 'slot'), 0, 0, tiled=True)  10.8 us
    pallas_call x1, Pallas kernels, near_pass(): pl.pallas_call(functools.partial(near_kernel, (rows // 2, scale)), out_sh...  10.5 us
    pallas_call x1, Pallas kernels, forward_pass(): pl.pallas_call(functools.partial(forward_kernel, b), out_shape=[pltpu.VME...  8.54 us
    all_to_all x1, starting transfers between devices, body(): got = lax.all_to_all(sent, ('half', 'near', 'slot'), 0, 0, tiled=True)  8.47 us
    pallas_call x1, Pallas kernels, prepare(): pl.pallas_call(functools.partial(prepare_kernel, b), out_shape=[pltpu.HBM...  3.64 us
  transfers between devices with their start and end apart: 5, of which 3 were waited for; matrix products, arithmetic and copies ran while one was open for 4% of the time, Pallas kernels for 14%

profile of v9, /device:TPU:0, one launch (start us, length us, event | category | flops | bytes accessed | tf_op | source)
XLA Modules:
  0.0 99.6 jit_solution(10992836901197445554)
XLA Ops:
  0.0 2.5 %pack.1 = bf16[16,128,256]{2,1,0:T(8,128)(2,1)} custom-call(s32[2,16]{1,0:T(2,128)} %bitcast.19, s32[1,512]{1,0:T(1,128)} %bitcast.17, bf16[1,512,256]{2,1,0:T(8,128)(2,1)} %spectra_hbm.1), custom_call_target="tpu_custom_call" | custom-call | tf_op jit(solution)/shard_map/pack/pallas_call | solution.py:90
  2.6 0.0 copy-start.1
  2.6 0.0 copy-start.2
  2.6 8.5 %all-to-all-start = ((bf16[16,128,256]{2,1,0:T(8,128)(2,1)}), bf16[16,128,256]{2,1,0:T(8,128)(2,1)S(1)}, u32[]{:S(2)}, u32[]{:S(2)}) async-start(bf16[16,128,256]{2,1,0:T(8,128)(2,1)} %pack.1), calls=%async_computation | async-start | bytes 2097152 | tf_op jit(solution)/shard_map/all_to_all | solution.py:606
  11.1 0.0 copy-done.7
  11.1 0.7 fusion.1
  11.8 0.7 constant_dynamic-slice_fusion.1
  12.4 0.0 copy-done.4
  12.4 0.0 copy-done
  12.4 3.6 %prepare.1 = (bf16[32,128,128]{2,1,0:T(8,128)(2,1)}, f32[32,128,128]{2,1,0:T(8,128)}) custom-call(s32[1]{0:T(128)} %bitcast.9.slot_ref, bf16[2,4096,128]{2,1,0:T(8,128)(2,1)S(1)} %bitcast.15, bf16[384,128]{1,0:T(8,128)(2,1)S(1)} %copy-done.4), custom_call_target="tpu_custom_call" | custom-call | flops 134217728 | bytes 4194304 | tf_op jit(solution)/shard_map/prepare/pallas_call | solution.py:191
  16.1 2.0 %broadcast_divide_fusion = (f32[2]{0:T(128)S(1)}, f32[2]{0:T(128)S(1)}) fusion(f32[]{:T(128)} %get-tuple-element.33, f32[1]{0:T(128)} %bitcast.4, f32[1]{0:T(128)} %bitcast.3), kind=kLoop, calls=%fused_computation.7 | loop fusion | flops 4 | bytes 28 | tf_op jit(solution)/shard_map/div | solution.py:603
  18.1 17.3 %all-to-all-done = bf16[16,128,256]{2,1,0:T(8,128)(2,1)S(1)} async-done(((bf16[16,128,256]{2,1,0:T(8,128)(2,1)}), bf16[16,128,256]{2,1,0:T(8,128)(2,1)S(1)}, u32[]{:S(2)}, u32[]{:S(2)}) %all-to-all-start) | async-done | bytes 1048608 | tf_op jit(solution)/shard_map/all_to_all | solution.py:606
  35.4 0.0 copy-done.1
  35.4 0.0 copy-done.2
  35.4 8.5 %forward.1 = (f32[1024,512]{1,0:T(8,128)S(1)}, bf16[1024,512]{1,0:T(8,128)(2,1)}, bf16[8,2,128,256]{3,2,1,0:T(8,128)(2,1)}) custom-call(f32[2]{0:T(128)S(1)} %get-tuple-element.32.mask_ref, bf16[8,2,128,256]{3,2,1,0:T(8,128)(2,1)S(1)} %bitcast.14, f32[8,18,256]{2,1,0:T(8,128)S(1)} %copy-done.1, f32[8,8,256]{2,1,0:T(8,128)S(1)} %copy-done.2), custom_call_target="tpu_custom_call" | custom-call | tf_op jit(solution)/shard_map/forward/pallas_call | solution.py:297
  43.9 0.1 collective-permute-start
  44.7 0.1 pad_maximum_fusion.1.scalars_ref
  44.8 2.0 %collective-permute-done.other_ref = bf16[1024,512]{1,0:T(8,128)(2,1)S(1)} collective-permute-done((bf16[1024,512]{1,0:T(8,128)(2,1)}, bf16[1024,512]{1,0:T(8,128)(2,1)S(1)}, u32[]{:S(2)}, u32[]{:S(2)}) %collective-permute-start) | collective-permute-done | bytes 1048608 | tf_op jit(solution)/shard_map/ppermute | solution.py:615
  46.9 13.8 %far.1 = (bf16[4,2,128,256]{3,2,1,0:T(8,128)(2,1)S(1)}, bf16[1024,512]{1,0:T(8,128)(2,1)}, bf16[512,1024]{1,0:T(8,128)(2,1)}) custom-call(s32[1]{0:T(128)} %bitcast.6.offset_ref, f32[3]{0:T(128)S(1)} %pad_maximum_fusion.1.scalars_ref, f32[1024,512]{1,0:T(8,128)S(1)} %get-tuple-element.21.mine_ref, bf16[1024,512]{1,0:T(8,128)(2,1)S(1)} %collective-permute-done.other_ref, ...), custom_call_target="tpu_custom_call" | custom-call | tf_op jit(solution)/shard_map/far/pallas_call | solution.py:545
  60.7 0.0 copy-start.3
  60.7 0.8 copy-done.3
  61.5 5.7 %all-to-all-start.1 = ((bf16[8,128,256]{2,1,0:T(8,128)(2,1)}), bf16[8,128,256]{2,1,0:T(8,128)(2,1)S(1)}, u32[]{:S(2)}, u32[]{:S(2)}) async-start(bf16[8,128,256]{2,1,0:T(8,128)(2,1)} %bitcast.16), calls=%async_computation.1 | async-start | bytes 1048576 | tf_op jit(solution)/shard_map/all_to_all | solution.py:625
  67.2 0.0 copy-done.6
  67.2 0.1 dynamic-slice_bitcast_fusion.blocks_ref
  67.2 10.5 %near.1 = bf16[4,2,128,256]{3,2,1,0:T(8,128)(2,1)} custom-call(s32[1]{0:T(128)} %bitcast.2.offset_ref, f32[3]{0:T(128)S(1)} %pad_maximum_fusion.1.scalars_ref, bf16[1024,512]{1,0:T(8,128)(2,1)} %get-tuple-element.26.res_hbm, bf16[512,1024]{1,0:T(8,128)(2,1)} %get-tuple-element.27.res_t_hbm, bf16[8,2,128,256]{3,2,1,0:T(8,128)(2,1)} %get-tuple-element.25.kept_ref, ...), custom_call_target="tpu_custom_call" | custom-call | tf_op jit(solution)/shard_map/near/pallas_call | solution.py:576
  77.7 0.0 all-to-all-done.1.got_ref
  77.8 0.7 gather.1
  78.5 5.1 %all-to-all-start.2 = ((bf16[8,128,256]{2,1,0:T(8,128)(2,1)}), bf16[8,128,256]{2,1,0:T(8,128)(2,1)S(1)}, u32[]{:S(2)}, u32[]{:S(2)}) async-start(bf16[8,128,256]{2,1,0:T(8,128)(2,1)} %bitcast.12), calls=%async_computation.2 | async-start | bytes 1048576 | tf_op jit(solution)/shard_map/all_to_all | solution.py:625
  83.6 0.7 collective-permute-start.1
  84.3 13.4 %collective-permute-done.1.far_ref = bf16[512,256]{1,0:T(8,128)(2,1)S(1)} collective-permute-done((bf16[512,256]{1,0:T(8,128)(2,1)S(1)}, bf16[512,256]{1,0:T(8,128)(2,1)S(1)}, u32[]{:S(2)}, u32[]{:S(2)}) %collective-permute-start.1) | collective-permute-done | bytes 262176 | tf_op jit(solution)/shard_map/ppermute | solution.py:636
  97.7 0.0 all-to-all-done.2.got_ref
  97.7 2.0 %unpack.1 = f32[1,512,256]{2,1,0:T(8,128)} custom-call(s32[2,8]{1,0:T(2,128)S(1)} %dynamic-slice_bitcast_fusion.blocks_ref, s32[1,512]{1,0:T(1,128)S(1)} %bitcast.18, bf16[8,128,256]{2,1,0:T(8,128)(2,1)S(1)} %all-to-all-done.2.got_ref, bf16[512,256]{1,0:T(8,128)(2,1)S(1)} %collective-permute-done.1.far_ref), custom_call_target="tpu_custom_call" | custom-call | tf_op jit(solution)/shard_map/unpack/pallas_call | solution.py:150
  (6 shorter events, 0.0 us)
Async XLA Ops:
  0.0 12.4 %copy-start.4 = (bf16[384,128]{1,0:T(8,128)(2,1)S(1)}, bf16[384,128]{1,0:T(8,128)(2,1)}, u32[]{:S(2)}) copy-start(bf16[384,128]{1,0:T(8,128)(2,1)} %constant.51.clone.orders_ref) | copy-start | bytes 294916
  0.0 11.1 %copy-start.7 = (s32[2,4]{1,0:T(2,128)S(1)}, s32[2,4]{1,0:T(2,128)}, u32[]{:S(2)}) copy-start(s32[2,4]{1,0:T(2,128)} %param.13) | copy-start | bytes 100
  0.0 12.4 %copy-start = (bf16[2,64,64,128]{3,2,1,0:T(8,128)(2,1)S(1)}, bf16[2,64,64,128]{3,2,1,0:T(8,128)(2,1)}, u32[]{:S(2)}) copy-start(bf16[2,64,64,128]{3,2,1,0:T(8,128)(2,1)} %param.10) | copy-start | bytes 6291460
  2.6 32.8 %copy-start.1 = (f32[8,18,256]{2,1,0:T(8,128)S(1)}, f32[8,18,256]{2,1,0:T(8,128)}, u32[]{:S(2)}) copy-start(f32[8,18,256]{2,1,0:T(8,128)} %constant.53.clone.fine_ref.fine_hbm) | copy-start | bytes 442372
  2.6 32.8 %copy-start.2 = (f32[8,8,256]{2,1,0:T(8,128)S(1)}, f32[8,8,256]{2,1,0:T(8,128)}, u32[]{:S(2)}) copy-start(f32[8,8,256]{2,1,0:T(8,128)} %constant.54.clone.coarse_ref.coarse_hbm) | copy-start | bytes 196612
  2.6 32.8 %all-to-all-start = ((bf16[16,128,256]{2,1,0:T(8,128)(2,1)}), bf16[16,128,256]{2,1,0:T(8,128)(2,1)S(1)}, u32[]{:S(2)}, u32[]{:S(2)}) async-start(bf16[16,128,256]{2,1,0:T(8,128)(2,1)} %pack.1), calls=%async_computation | async-start | bytes 2097152 | tf_op jit(solution)/shard_map/all_to_all | solution.py:606
  43.9 2.9 %collective-permute-start = (bf16[1024,512]{1,0:T(8,128)(2,1)}, bf16[1024,512]{1,0:T(8,128)(2,1)S(1)}, u32[]{:S(2)}, u32[]{:S(2)}) collective-permute-start(bf16[1024,512]{1,0:T(8,128)(2,1)} %get-tuple-element.22), channel_id=1, source_target_pairs={{0,1},{1,0},{2,3},{3,2},{4,5},{5,4},{6,7},{7,6},{8,9},{9,8},{10,11... | collective-permute-start | bytes 3145736 | tf_op jit(solution)/shard_map/ppermute | solution.py:615
  46.9 20.3 %copy-start.6 = (s32[16,2]{0,1:T(2,128)S(1)}, s32[16,2]{0,1:T(2,128)}, u32[]{:S(2)}) copy-start(s32[16,2]{0,1:T(2,128)} %param.11) | copy-start | bytes 388
  60.7 0.8 copy-start.3
  61.5 16.3 %all-to-all-start.1 = ((bf16[8,128,256]{2,1,0:T(8,128)(2,1)}), bf16[8,128,256]{2,1,0:T(8,128)(2,1)S(1)}, u32[]{:S(2)}, u32[]{:S(2)}) async-start(bf16[8,128,256]{2,1,0:T(8,128)(2,1)} %bitcast.16), calls=%async_computation.1 | async-start | bytes 1048576 | tf_op jit(solution)/shard_map/all_to_all | solution.py:625
  67.2 30.4 %copy-start.5 = (s32[512]{0:T(512)S(1)}, s32[512]{0:T(512)}, u32[]{:S(2)}) copy-start(s32[512]{0:T(512)} %param.12) | copy-start | bytes 6148
  78.5 19.2 %all-to-all-start.2 = ((bf16[8,128,256]{2,1,0:T(8,128)(2,1)}), bf16[8,128,256]{2,1,0:T(8,128)(2,1)S(1)}, u32[]{:S(2)}, u32[]{:S(2)}) async-start(bf16[8,128,256]{2,1,0:T(8,128)(2,1)} %bitcast.12), calls=%async_computation.2 | async-start | bytes 1048576 | tf_op jit(solution)/shard_map/all_to_all | solution.py:625
  83.6 14.1 %collective-permute-start.1 = (bf16[512,256]{1,0:T(8,128)(2,1)S(1)}, bf16[512,256]{1,0:T(8,128)(2,1)S(1)}, u32[]{:S(2)}, u32[]{:S(2)}) collective-permute-start(bf16[512,256]{1,0:T(8,128)(2,1)S(1)} %gather.1), channel_id=1, source_target_pairs={{0,16},{16,0},{1,17},{17,1},{2,18},{18,2},{3,19},{19,3},{4,20},{20... | collective-permute-start | bytes 786440 | tf_op jit(solution)/shard_map/ppermute | solution.py:636

commit v10 on v8

--- a/solution.py
+++ b/solution.py
@@ -59,7 +59,7 @@
     return jnp.dot(a, b, preferred_element_type=F32)
 
 
-def pack_kernel(blocks_hbm, members_hbm, spectra_hbm, out_ref, blocks_ref, members_ref, spectra_ref, ordered, sems):
+def pack_kernel(first_ref, blocks_hbm, members_hbm, spectra_hbm, out_ref, blocks_ref, members_ref, spectra_ref, ordered, sems):
     stations = spectra_ref.shape[1]
     b = out_ref.shape[1] // 2
     copies = (
@@ -79,18 +79,18 @@
     copies[2].wait()
     for p in range(out_ref.shape[0]):
         for side in range(2):
-            row = pl.multiple_of(blocks_ref[side, p] * b, b)
+            row = pl.multiple_of(blocks_ref[side, first_ref[0] + p] * b, b)
             out_ref[p, side * b:(side + 1) * b, :] = ordered[pl.ds(row, b), :]
 
 
-def pack(pair_blocks, members, spectra, b):
+def pack(first, pair_blocks, members, spectra, b):
     _, stations, cols = spectra.shape
-    n_pairs = pair_blocks.shape[1]
+    n_pairs = pair_blocks.shape[1] // 2
     arrays = [pltpu.with_memory_space_constraint(x, pltpu.HBM) for x in (pair_blocks, members, spectra)]
     return pl.pallas_call(
         pack_kernel,
-        out_shape=jax.ShapeDtypeStruct((n_pairs, 2 * b, cols), BF16),
-        in_specs=[pl.BlockSpec(memory_space=pltpu.HBM)] * 3,
+        out_shape=pltpu.VMEM((n_pairs, 2 * b, cols), BF16),
+        in_specs=[pl.BlockSpec(memory_space=pltpu.SMEM)] + [pl.BlockSpec(memory_space=pltpu.HBM)] * 3,
         out_specs=pl.BlockSpec(memory_space=pltpu.VMEM),
         scratch_shapes=[
             pltpu.SMEM(pair_blocks.shape, pair_blocks.dtype),
@@ -101,7 +101,7 @@
         ],
         compiler_params=pltpu.CompilerParams(vmem_limit_bytes=8 << 20),
         name="pack",
-    )(*arrays)
+    )(first, *arrays)
 
 
 def unpack_kernel(blocks_ref, members_ref, got_ref, out_ref, total):
@@ -187,39 +187,41 @@
     return slice(t * TILE, (t + 1) * TILE)
 
 
-def turn_columns(got_ref, share, b, table_ref, into):
+def turn_columns(got_ref, share, b, table_ref, into, row=None):
     _, days, _, cols = got_ref.shape
     tiles = cols // TILE
     half = table_ref.shape[1] // 2
+    row = share if row is None else row
     for d in range(days):
         for t in range(tiles):
             at = tile_lanes(tiles, d, t)
             u = got_ref[share, d, b:, part(t)].astype(F32)
             v = swap_halves(u)
             for k in range(half):
-                one = u * table_ref[share, k:k + 1, part(t)]
-                two = v * table_ref[share, half + k:half + k + 1, part(t)]
+                one = u * table_ref[row, k:k + 1, part(t)]
+                two = v * table_ref[row, half + k:half + k + 1, part(t)]
                 into[k * b:(k + 1) * b, at] = (one + two).astype(BF16)
                 into[(half + k) * b:(half + k + 1) * b, at] = (one - two).astype(BF16)
 
 
-def turn_rows(got_ref, share, b, table_ref, into, rows_u, rows_v, mask_ref=None):
+def turn_rows(got_ref, share, b, table_ref, into, rows_u, rows_v, mask_ref=None, row=None):
     _, days, _, cols = got_ref.shape
     tiles = cols // TILE
     half = table_ref.shape[1] // 2 - 1
+    row = share if row is None else row
     pieces = [(d, t) for d in range(days) for t in range(tiles)]
     for d, t in pieces:
         at = tile_lanes(tiles, d, t)
         u = got_ref[share, d, :b, part(t)].astype(F32)
         if mask_ref is not None:
             u = u * mask_ref[d]
-        u = turn_half(u, table_ref, share, t, 1)
+        u = turn_half(u, table_ref, row, t, 1)
         rows_u[:, at] = u
         rows_v[:, at] = swap_halves(u)
     for d, t in pieces:
         at = tile_lanes(tiles, d, t)
-        cosine = table_ref[share, :half, part(t)]
-        sine = table_ref[share, half:2 * half, part(t)]
+        cosine = table_ref[row, :half, part(t)]
+        sine = table_ref[row, half:2 * half, part(t)]
         for k in range(b):
             one = rows_u[k:k + 1, at] * cosine
             two = rows_v[k:k + 1, at] * sine
@@ -233,10 +235,11 @@
     return one + two if sign > 0 else one - two
 
 
-def forward_kernel(
-    b, mask_ref, got_ref, fine_ref, coarse_ref, out_ref, sent_ref, kept_ref, even_a, even_b, odd_a, odd_b, rows_u, rows_v,
-    sem,
-):
+def forward_kernel(b, last, offset_ref, mask_ref, got_ref, fine_ref, coarse_ref, *refs):
+    before_ref, refs = (refs[0], refs[1:]) if last else (None, refs)
+    out_ref, refs = refs[0], refs[1:]
+    sent_ref, refs = (refs[0], refs[1:]) if last else (None, refs)
+    kept_ref, even_a, even_b, odd_a, odd_b, rows_u, rows_v, sem = refs
     shares = got_ref.shape[0]
     even = (even_a, even_b)
     odd = (odd_a, odd_b)
@@ -244,14 +247,15 @@
     keep.start()
 
     def make(share, into):
-        turn_columns(got_ref, share, b, coarse_ref, into[1])
-        turn_rows(got_ref, share, b, fine_ref, into[0], rows_u, rows_v, mask_ref)
+        row = offset_ref[0] + share
+        turn_columns(got_ref, share, b, coarse_ref, into[1], row)
+        turn_rows(got_ref, share, b, fine_ref, into[0], rows_u, rows_v, mask_ref, row)
 
     def product(made):
         return lax.dot_general(made[0][...], made[1][...], (((1,), (1,)), ((), ())), preferred_element_type=F32)
 
     make(0, even)
-    out_ref[...] = product(even)
+    out_ref[...] = before_ref[...] + product(even) if last else product(even)
     make(1, odd)
 
     def two_shares(step, carry):
@@ -264,26 +268,27 @@
     lax.fori_loop(0, shares // 2 - 1, two_shares, 0)
     total = out_ref[...] + product(odd)
     out_ref[...] = total
-    sent_ref[...] = total.astype(sent_ref.dtype)
+    if last:
+        sent_ref[...] = total.astype(sent_ref.dtype)
     keep.wait()
 
 
-def forward_pass(mask, got, fine, coarse):
+def forward_pass(offset, mask, got, fine, coarse, before):
     shares, days, rows, cols = got.shape
     assert shares % 2 == 0
     b = rows // 2
     n_fine = fine.shape[1] - 2
     n_coarse = coarse.shape[1]
     vmem = pl.BlockSpec(memory_space=pltpu.VMEM)
+    smem = pl.BlockSpec(memory_space=pltpu.SMEM)
+    shape = (n_fine * b, n_coarse * b)
+    sent = [jax.ShapeDtypeStruct(shape, BF16)] * len(before)
     return pl.pallas_call(
-        functools.partial(forward_kernel, b),
-        out_shape=[
-            pltpu.VMEM((n_fine * b, n_coarse * b), F32),
-            jax.ShapeDtypeStruct((n_fine * b, n_coarse * b), BF16),
-            pltpu.HBM(got.shape, BF16),
-        ],
-        in_specs=[pl.BlockSpec(memory_space=pltpu.SMEM), vmem, vmem, vmem],
-        out_specs=[vmem, vmem, pl.BlockSpec(memory_space=pltpu.HBM)],
+        functools.partial(forward_kernel, b, bool(before)),
+        out_shape=[pltpu.VMEM(shape, F32)] + sent + [pltpu.HBM(got.shape, BF16)],
+        in_specs=[smem, smem, vmem, vmem, vmem] + [vmem] * len(before),
+        out_specs=[vmem] + [vmem] * len(before) + [pl.BlockSpec(memory_space=pltpu.HBM)],
+        input_output_aliases={5: 0} if before else {},
         scratch_shapes=[
             pltpu.VMEM((n_fine * b, days * cols), BF16),
             pltpu.VMEM((n_coarse * b, days * cols), BF16),
@@ -295,20 +300,16 @@
         ],
         compiler_params=pltpu.CompilerParams(vmem_limit_bytes=16 << 20),
         name="forward",
-    )(mask, got, fine, coarse)
-
-
-def adjoint_kernel(
-    sizes, scalars_ref, mine_ref, other_ref, seen_hbm, env_hbm, hilbert_hbm, kept_ref, fine_hbm, coarse_hbm, out_ref,
-    seen_ref, env_ref, hilbert_ref, got_ref, fine_ref, coarse_ref, lagged, back, res, res_t, sums_a, sums_b,
-    turned_a, turned_b, rows_u, rows_v, sems_s, sems_e, sems,
+    )(offset, mask, got, fine, coarse, *before)
+
+
+def residual_stage(
+    b, group, scalars_ref, mine_ref, other_ref, seen_hbm, env_hbm, hilbert_hbm, seen_ref, env_ref, hilbert_ref, lagged,
+    back, res, res_t, sems_s, sems_e, sem, begin,
 ):
-    b, scale, group = sizes
-    shares, days, _, cols = out_ref.shape
-    n_fine = fine_ref.shape[1] - 2
-    n_coarse = coarse_ref.shape[1]
-    slabs = n_coarse // 2
-    tiles = cols // TILE
+    n_fine = mine_ref.shape[0] // b
+    slabs = mine_ref.shape[1] // TILE
+    days = scalars_ref.shape[0] - 1
     block = group * n_fine
     left = left_lanes((n_fine, 2 * b))
 
@@ -319,18 +320,12 @@
             pltpu.make_async_copy(env_hbm.at[some], env_ref.at[some], sems_e.at[step]),
         )
 
-    first = pltpu.make_async_copy(hilbert_hbm, hilbert_ref, sems.at[0])
-    later = (
-        pltpu.make_async_copy(kept_ref, got_ref, sems.at[1]),
-        pltpu.make_async_copy(fine_hbm, fine_ref, sems.at[2]),
-        pltpu.make_async_copy(coarse_hbm, coarse_ref, sems.at[3]),
-    )
+    first = pltpu.make_async_copy(hilbert_hbm, hilbert_ref, sem)
     first.start()
     for step in range(b // group):
         for copy in bring(step):
             copy.start()
-    for copy in later:
-        copy.start()
+    begin()
     first.wait()
 
     def residual_rows(step, carry):
@@ -375,6 +370,36 @@
 
     lax.fori_loop(0, n_fine, round_rows, 0)
 
+
+def adjoint_stage(
+    sizes, starts_ref, scalars_ref, near_ref, far_ref, fine_hbm, coarse_hbm, out_ref, got_ref, fine_ref, coarse_ref, res,
+    res_t, sums_a, sums_b, turned_a, turned_b, rows_u, rows_v, sems, before,
+):
+    b, scale = sizes
+    shares, days, _, cols = out_ref.shape
+    n_fine = fine_ref.shape[1] - 2
+    n_coarse = coarse_ref.shape[1]
+    tiles = cols // TILE
+    count = shares // 2
+    later = []
+    for k, kept_ref in enumerate((near_ref, far_ref)):
+        here = pl.ds(k * count, count)
+        some = pl.ds(starts_ref[k], count)
+        later += [
+            pltpu.make_async_copy(kept_ref, got_ref.at[here], sems.at[3 * k]),
+            pltpu.make_async_copy(fine_hbm.at[some], fine_ref.at[here], sems.at[3 * k + 1]),
+            pltpu.make_async_copy(coarse_hbm.at[some], coarse_ref.at[here], sems.at[3 * k + 2]),
+        ]
+
+    def place(share):
+        return jnp.where(share < count, starts_ref[0] + share, starts_ref[1] + share - count)
+
+    def begin():
+        for copy in later:
+            copy.start()
+
+    before(begin)
+
     def collect(share, side, table, n, sums):
         half = n // 2
         for d in range(days):
@@ -390,7 +415,7 @@
                 value = p + swap_halves(q)
                 if side == 0:
                     value = turn_half(value, table, share, t, -1)
-                out_ref[share, d, side * b:(side + 1) * b, part(t)] = (value * (scalars_ref[d] * scale)).astype(BF16)
+                out_ref[place(share), d, side * b:(side + 1) * b, part(t)] = (value * (scalars_ref[d] * scale)).astype(BF16)
 
     for copy in later:
         copy.wait()
@@ -410,6 +435,25 @@
     collect(shares - 1, 1, coarse_ref, n_coarse, sums_b)
 
 
+def adjoint_kernel(
+    sizes, starts_ref, scalars_ref, mine_ref, other_ref, seen_hbm, env_hbm, hilbert_hbm, near_ref, far_ref, fine_hbm,
+    coarse_hbm, out_ref, seen_ref, env_ref, hilbert_ref, lagged, back, got_ref, fine_ref, coarse_ref, res, res_t,
+    sums_a, sums_b, turned_a, turned_b, rows_u, rows_v, sems_s, sems_e, sems,
+):
+    b, scale, group = sizes
+
+    def before(begin):
+        residual_stage(
+            b, group, scalars_ref, mine_ref, other_ref, seen_hbm, env_hbm, hilbert_hbm, seen_ref, env_ref, hilbert_ref,
+            lagged, back, res, res_t, sems_s, sems_e, sems.at[6], begin,
+        )
+
+    adjoint_stage(
+        (b, scale), starts_ref, scalars_ref, near_ref, far_ref, fine_hbm, coarse_hbm, out_ref, got_ref, fine_ref,
+        coarse_ref, res, res_t, sums_a, sums_b, turned_a, turned_b, rows_u, rows_v, sems, before,
+    )
+
+
 def turn_tables(columns, lags, shares, n_fine):
     freqs = columns // 2
     n_coarse = lags // n_fine
@@ -432,26 +476,32 @@
     return place(np.concatenate([fine, table(np.array([1]), -1)])), place(coarse)
 
 
-def adjoint_pass(scalars, mine, other, seen, env, hilbert, kept, fine, coarse, parts):
-    shares, days, rows, cols = kept.shape
+def adjoint_pass(starts, scalars, mine, other, seen, env, hilbert, near, far, fine, coarse, parts):
+    half_shares, days, rows, cols = near.shape
+    shares = 2 * half_shares
     b = rows // 2
     n_fine = fine.shape[1] - 2
     n_coarse = coarse.shape[1]
+    lanes = days * cols
     scale = 1.0 / math.sqrt(shares * cols // 2)
     group = b // parts
-    lanes = days * cols
     vmem = pl.BlockSpec(memory_space=pltpu.VMEM)
     hbm = pl.BlockSpec(memory_space=pltpu.HBM)
-    apart = [pltpu.with_memory_space_constraint(x, pltpu.HBM) for x in (seen, env, hilbert, kept, fine, coarse)]
+    smem = pl.BlockSpec(memory_space=pltpu.SMEM)
+    apart = [pltpu.with_memory_space_constraint(x, pltpu.HBM) for x in (seen, env, hilbert, near, far, fine, coarse)]
+    shape = (shares, days, rows, cols)
     return pl.pallas_call(
         functools.partial(adjoint_kernel, (b, scale, group)),
-        out_shape=jax.ShapeDtypeStruct(kept.shape, BF16),
-        in_specs=[pl.BlockSpec(memory_space=pltpu.SMEM), vmem, vmem] + [hbm] * len(apart),
+        out_shape=jax.ShapeDtypeStruct(shape, BF16),
+        in_specs=[smem, smem, vmem, vmem] + [hbm] * len(apart),
         out_specs=vmem,
-        scratch_shapes=[pltpu.VMEM(x.shape, x.dtype) for x in apart]
+        scratch_shapes=[pltpu.VMEM(x.shape, x.dtype) for x in apart[:3]]
         + [
             pltpu.VMEM((n_coarse // 2, n_fine * b, 2 * b), F32),
             pltpu.VMEM((group * n_fine, n_coarse * b), F32),
+            pltpu.VMEM(shape, BF16),
+            pltpu.VMEM(fine.shape, F32),
+            pltpu.VMEM(coarse.shape, F32),
             pltpu.VMEM((n_fine * b, n_coarse * b), BF16),
             pltpu.VMEM((n_coarse * b, n_fine * b), BF16),
             pltpu.VMEM((n_fine * b, lanes), F32),
@@ -462,15 +512,16 @@
             pltpu.VMEM((b, lanes), F32),
             pltpu.SemaphoreType.DMA((parts,)),
             pltpu.SemaphoreType.DMA((parts,)),
-            pltpu.SemaphoreType.DMA((4,)),
+            pltpu.SemaphoreType.DMA((7,)),
         ],
         compiler_params=pltpu.CompilerParams(vmem_limit_bytes=24 << 20),
         name="adjoint",
-    )(scalars, mine, other, *apart)
+    )(starts, scalars, mine, other, *apart)
 
 
 def body(spectra, observed, pair_blocks, members, day_mask):
-    shares = lax.axis_size("pairs")
+    half_shares = lax.axis_size("near")
+    shares = 2 * half_shares
     slots, b, _, lags = observed.shape
     _, stations, cols = spectra.shape
     n_fine = 16
@@ -486,14 +537,29 @@
     scale = 1.0 / math.sqrt(shares * cols // 2)
     scalars = jnp.concatenate([mask_here / count, scale / count[None]])
 
-    sent = pack(pair_blocks, members, spectra, b)
-    got = lax.all_to_all(sent, ("pairs", "slot"), 0, 0, tiled=True)
-    got = got.reshape(shares, slots, 2 * b, cols)
+    half = lax.axis_index("half")
+    start_far = ((1 - half) * half_shares)[None]
+    start_near = (half * half_shares)[None]
+    first_pair = start_near * slots
+
+    def exchange(x):
+        flat = x.reshape(half_shares * slots, 2 * b, cols)
+        moved = lax.all_to_all(flat, ("near", "slot"), 0, 0, tiled=True)
+        return moved
+
+    shape = (half_shares, slots, 2 * b, cols)
+    opposite = lax.ppermute(spectra, "half", [(0, 1), (1, 0)])
+    got_near = exchange(pack(first_pair, pair_blocks, members, spectra, b))
+    orders, hilbert, fine, coarse = [jnp.asarray(x) for x in (orders, hilbert, fine, coarse)]
     parts = 4
-    orders, hilbert, fine, coarse = [jnp.asarray(x) for x in (orders, hilbert, fine, coarse)]
     seen, env = prepare(slot[None], observed.reshape(slots, b * b, lags), orders, parts)
-    got, seen, env = lax.optimization_barrier((got, seen, env))
-    mine, sent, kept = forward_pass(mask_here, got, fine, coarse)
+    got_near, opposite, seen, env, mask_here, scalars = lax.optimization_barrier(
+        (got_near, opposite, seen, env, mask_here, scalars)
+    )
+    got_far = exchange(pack(first_pair, pair_blocks, members, opposite, b))
+    mine, kept_near = forward_pass(start_near, mask_here, got_near.reshape(shape), fine, coarse, [])
+    got_far, mine = lax.optimization_barrier((got_far, mine))
+    mine, sent, kept_far = forward_pass(start_far, mask_here, got_far.reshape(shape), fine, coarse, [mine])
     for axis in ("outer", "core"):
         n = lax.axis_size(axis)
         others = [lax.ppermute(sent, axis, [(i, (i + k) % n) for i in range(n)]) for k in range(1, n)]
@@ -501,33 +567,37 @@
             for other in others:
                 mine = mine + other.astype(F32)
             sent = mine.astype(BF16)
-    contrib = adjoint_pass(scalars, mine, others[0], seen, env, hilbert, kept, fine, coarse, parts)
+    starts = jnp.concatenate([start_near, start_far])
+    contrib = adjoint_pass(
+        starts, scalars, mine, others[0], seen, env, hilbert, kept_near, kept_far, fine, coarse, parts
+    )
     returned = lax.all_to_all(
-        contrib.reshape(shares * slots, 2 * b, cols), ("pairs", "slot"), 0, 0, tiled=True
+        contrib.reshape(shares * slots, 2 * b, cols), ("half", "near", "slot"), 0, 0, tiled=True
     )
     return unpack(pair_blocks, members, returned, stations)
 
 
 def solution(mesh):
     shares, days = mesh.devices.shape
-    names = ("pairs", "outer", "slot", "core")
+    names = ("half", "near", "outer", "slot", "core")
 
     def run(spectra, observed, pair_blocks, members, day_mask):
         slots = observed.shape[0] // shares
-        split = (shares, days // CORES // slots, slots, CORES)
+        split = (2, shares // 2, days // CORES // slots, slots, CORES)
         finer = Mesh(mesh.devices.reshape(split), names)
-        day_axes = names[1:]
+        day_axes = names[2:]
+        pair_axes = names[:2]
         return jax.shard_map(
             body,
             mesh=finer,
             in_specs=(
-                P(day_axes, None, "pairs"),
-                P("pairs", None, None, None),
+                P(day_axes, None, pair_axes),
+                P(pair_axes, None, None, None),
                 P(),
                 P(),
-                P("pairs", None),
+                P(pair_axes, None),
             ),
-            out_specs=P(day_axes, None, "pairs"),
+            out_specs=P(day_axes, None, pair_axes),
             check_vma=False,
         )(spectra, observed, pair_blocks, members, day_mask)
 

time: 103 us -> 100 us (0.971)
  waiting for transfers between devices: 19.4 us -> 7.62 us
  starting transfers between devices: 8.54 us -> 14.3 us
  local copies, waits for them, and re-layouts: 0.7 us -> 3.18 us
  Pallas kernels: 37.8 us -> 39.5 us
  blocking collectives: 32.4 us -> 31.1 us
    all_to_all x1 -> x2, waiting for transfers between devices: 17.3 us -> 5.05 us  [exchange(): moved = lax.all_to_all(flat, ('near', 'slot'), 0, 0, tiled=True)]
    all_to_all x1 -> x2, starting transfers between devices: 8.47 us -> 11.6 us  [exchange(): moved = lax.all_to_all(flat, ('near', 'slot'), 0, 0, tiled=True)]
    ppermute x0 -> x1, starting transfers between devices: none -> 2.59 us  [body(): opposite = lax.ppermute(spectra, 'half', [(0, 1), (1, 0)])]
    unnamed x14, local copies, waits for them, and re-layouts: 0.04 us -> 2.51 us
    pallas_call x2 -> x4, Pallas kernels: 11.1 us -> 12.6 us  [the longest x2 8.25 us: forward_pass(): pl.pallas_call(functools.partial(forward_kernel, b, bool(before)), out_sh...]
    all_to_all x1, blocking collectives: 32.4 us -> 31.1 us  [body(): lax.all_to_all(contrib.reshape(shares * slots, 2 * b, cols), ('half', 'ne...]
  transfers between devices with their start and end apart: 2 -> 4, of which waited for: 2 -> 3; matrix products, arithmetic and copies ran while one was open for 3% -> 4% of each run, Pallas kernels for 4% -> 8%
where the time goes in v10:
time: 100 us; the launch traced here: 99.9 us
  Pallas kernels  39.5 us (40%)
  blocking collectives  31.1 us (31%)
  starting transfers between devices  14.3 us (14%)
  waiting for transfers between devices  7.62 us (8%)
  other arithmetic  3.46 us (3%)
  local copies, waits for them, and re-layouts  3.18 us (3%)
    all_to_all x1, blocking collectives, body(): lax.all_to_all(contrib.reshape(shares * slots, 2 * b, cols), ('half', 'ne...  31.1 us
    pallas_call x1, Pallas kernels, adjoint_pass(): pl.pallas_call(functools.partial(adjoint_kernel, (b, scale, group)), out_...  21 us
    all_to_all x2, starting transfers between devices, exchange(): moved = lax.all_to_all(flat, ('near', 'slot'), 0, 0, tiled=True)  11.6 us
    pallas_call x2, Pallas kernels, forward_pass(): pl.pallas_call(functools.partial(forward_kernel, b, bool(before)), out_sh...  8.25 us
    all_to_all x2, waiting for transfers between devices, exchange(): moved = lax.all_to_all(flat, ('near', 'slot'), 0, 0, tiled=True)  5.05 us
    pallas_call x2, Pallas kernels, pack(): pl.pallas_call(pack_kernel, out_shape=pltpu.VMEM((n_pairs, 2 * b, cols),...  4.4 us
    pallas_call x1, Pallas kernels, prepare(): pl.pallas_call(functools.partial(prepare_kernel, b), out_shape=[pltpu.HBM...  3.61 us
    ppermute x1, starting transfers between devices, body(): opposite = lax.ppermute(spectra, 'half', [(0, 1), (1, 0)])  2.59 us
  transfers between devices with their start and end apart: 4, of which 3 were waited for; matrix products, arithmetic and copies ran while one was open for 4% of the time, Pallas kernels for 8%

profile of v10, /device:TPU:0, one launch (start us, length us, event | category | flops | bytes accessed | tf_op | source)
XLA Modules:
  0.0 99.9 jit_solution(9917188743645407829)
XLA Ops:
  0.0 2.2 %pack.2 = bf16[8,128,256]{2,1,0:T(8,128)(2,1)} custom-call(s32[1]{0:T(128)S(6)} %mul.13.first_ref, s32[2,16]{1,0:T(2,128)} %bitcast.19, s32[1,512]{1,0:T(1,128)} %bitcast.16, bf16[1,512,256]{2,1,0:T(8,128)(2,1)} %spectra_hbm.1), custom_call_target="tpu_custom_call" | custom-call | tf_op jit(solution)/shard_map/pack/pallas_call | solution.py:90
  2.2 0.0 copy-start.1
  2.2 0.0 copy-start.2
  2.2 6.3 %all-to-all-start = ((bf16[8,128,256]{2,1,0:T(8,128)(2,1)}), bf16[8,128,256]{2,1,0:T(8,128)(2,1)S(1)}, u32[]{:S(2)}, u32[]{:S(2)}) async-start(bf16[8,128,256]{2,1,0:T(8,128)(2,1)} %pack.2), calls=%async_computation | async-start | bytes 1048576 | tf_op jit(solution)/shard_map/all_to_all | solution.py:547
  8.6 2.6 %collective-permute-start = (bf16[1,512,256]{2,1,0:T(8,128)(2,1)}, bf16[1,512,256]{2,1,0:T(8,128)(2,1)S(1)}, u32[]{:S(2)}, u32[]{:S(2)}) collective-permute-start(bf16[1,512,256]{2,1,0:T(8,128)(2,1)} %spectra_hbm.1), channel_id=1, source_target_pairs={{0,16},{16,0},{1,17},{17,1},{2,18},{18,2},{3,19},{19,3},{4,20},{20... | collective-permute-start | bytes 786440 | tf_op jit(solution)/shard_map/ppermute | solution.py:551
  11.2 1.4 %fusion.1 = (f32[]{:T(128)}, f32[1,4]{1,0:T(1,128)S(1)}) fusion(s32[2,4]{1,0:T(2,128)} %param.13, s32[]{:T(128)S(6)} %select_n.10), kind=kLoop, calls=%fused_computation.8 | loop fusion | flops 7 | bytes 40 | tf_op jit(solution)/shard_map/reduce_sum | solution.py:536
  13.2 0.7 constant_dynamic-slice_fusion.1
  13.9 1.6 %copy-done = bf16[2,64,64,128]{3,2,1,0:T(8,128)(2,1)S(1)} copy-done((bf16[2,64,64,128]{3,2,1,0:T(8,128)(2,1)S(1)}, bf16[2,64,64,128]{3,2,1,0:T(8,128)(2,1)}, u32[]{:S(2)}) %copy-start) | copy-done | bytes 2097176
  15.5 0.9 copy-done.3
  16.4 3.6 %prepare.1 = (bf16[32,128,128]{2,1,0:T(8,128)(2,1)}, f32[32,128,128]{2,1,0:T(8,128)}) custom-call(s32[1]{0:T(128)} %bitcast.4.slot_ref, bf16[2,4096,128]{2,1,0:T(8,128)(2,1)S(1)} %bitcast.13, bf16[384,128]{1,0:T(8,128)(2,1)S(1)} %copy-done.3), custom_call_target="tpu_custom_call" | custom-call | flops 134217728 | bytes 4194304 | tf_op jit(solution)/shard_map/prepare/pallas_call | solution.py:172
  20.0 2.0 %broadcast_divide_fusion = (f32[2]{0:T(128)S(1)}, f32[2]{0:T(128)S(1)}) fusion(f32[]{:T(128)} %get-tuple-element.37, f32[1]{0:T(128)} %bitcast.7, f32[1]{0:T(128)} %bitcast.6), kind=kLoop, calls=%fused_computation.7 | loop fusion | flops 4 | bytes 28 | tf_op jit(solution)/shard_map/div | solution.py:538
  21.9 0.1 pad_maximum_fusion.1.scalars_ref
  22.0 0.0 collective-permute-done.spectra_hbm
  22.0 1.3 %all-to-all-done = bf16[8,128,256]{2,1,0:T(8,128)(2,1)S(1)} async-done(((bf16[8,128,256]{2,1,0:T(8,128)(2,1)}), bf16[8,128,256]{2,1,0:T(8,128)(2,1)S(1)}, u32[]{:S(2)}, u32[]{:S(2)}) %all-to-all-start) | async-done | bytes 524320 | tf_op jit(solution)/shard_map/all_to_all | solution.py:547
  23.3 0.0 copy-done.6
  23.3 2.2 %pack.3 = bf16[8,128,256]{2,1,0:T(8,128)(2,1)} custom-call(s32[1]{0:T(128)S(6)} %mul.13.first_ref, s32[2,16]{1,0:T(2,128)} %bitcast.20, s32[1,512]{1,0:T(1,128)} %bitcast.17, bf16[1,512,256]{2,1,0:T(8,128)(2,1)} %copy-done.6), custom_call_target="tpu_custom_call" | custom-call | tf_op jit(solution)/shard_map/pack/pallas_call | solution.py:90
  25.5 5.3 %all-to-all-start.1 = ((bf16[8,128,256]{2,1,0:T(8,128)(2,1)}), bf16[8,128,256]{2,1,0:T(8,128)(2,1)S(1)}, u32[]{:S(2)}, u32[]{:S(2)}) async-start(bf16[8,128,256]{2,1,0:T(8,128)(2,1)} %pack.3), calls=%async_computation.1 | async-start | bytes 1048576 | tf_op jit(solution)/shard_map/all_to_all | solution.py:547
  30.8 0.0 copy-done.1
  30.8 0.0 copy-done.2
  30.8 4.1 %forward.2 = (f32[1024,512]{1,0:T(8,128)S(1)}, bf16[4,2,128,256]{3,2,1,0:T(8,128)(2,1)}) custom-call(s32[1]{0:T(128)} %bitcast.2.offset_ref, f32[2]{0:T(128)S(1)} %get-tuple-element.23.mask_ref, bf16[4,2,128,256]{3,2,1,0:T(8,128)(2,1)S(1)} %bitcast.14, f32[8,18,256]{2,1,0:T(8,128)S(1)} %copy-done.1, f32[8,8,256]{2,1,0:T(8,128)S(1)} %copy-done.2), custom_call_target="tpu_custom_call" | custom-call | tf_op jit(solution)/shard_map/forward/pallas_call | solution.py:286
  34.8 3.8 %all-to-all-done.1 = bf16[8,128,256]{2,1,0:T(8,128)(2,1)S(1)} async-done(((bf16[8,128,256]{2,1,0:T(8,128)(2,1)}), bf16[8,128,256]{2,1,0:T(8,128)(2,1)S(1)}, u32[]{:S(2)}, u32[]{:S(2)}) %all-to-all-start.1) | async-done | bytes 524320 | tf_op jit(solution)/shard_map/all_to_all | solution.py:547
  38.6 4.2 %forward.3 = (f32[1024,512]{1,0:T(8,128)S(1)}, bf16[1024,512]{1,0:T(8,128)(2,1)S(1)}, bf16[4,2,128,256]{3,2,1,0:T(8,128)(2,1)}) custom-call(s32[1]{0:T(128)} %bitcast.3.offset_ref, f32[2]{0:T(128)S(1)} %get-tuple-element.23.mask_ref, bf16[4,2,128,256]{3,2,1,0:T(8,128)(2,1)S(1)} %bitcast.15, ...), custom_call_target="tpu_custom_call", output_to_operand_aliasing={{0}: (5, {})} | custom-call | tf_op jit(solution)/shard_map/forward/pallas_call | solution.py:286
  42.8 0.1 collective-permute-start.1
  42.9 0.1 pad_add_fusion.starts_ref
  43.0 2.6 %collective-permute-done.1.other_ref = bf16[1024,512]{1,0:T(8,128)(2,1)S(1)} collective-permute-done((bf16[1024,512]{1,0:T(8,128)(2,1)S(1)}, bf16[1024,512]{1,0:T(8,128)(2,1)S(1)}, u32[]{:S(2)}, u32[]{:S(2)}) %collective-permute-start.1) | collective-permute-done | bytes 1048608 | tf_op jit(solution)/shard_map/ppermute | solution.py:565
  45.5 21.0 %adjoint.1 = bf16[8,2,128,256]{3,2,1,0:T(8,128)(2,1)S(1)} custom-call(s32[2]{0:T(128)S(1)} %pad_add_fusion.starts_ref, f32[3]{0:T(128)S(1)} %pad_maximum_fusion.1.scalars_ref, f32[1024,512]{1,0:T(8,128)S(1)} %get-tuple-element.29.mine_ref, bf16[1024,512]{1,0:T(8,128)(2,1)S(1)} %collective-permute-done.1.other_ref, ...), custom_call_target="tpu_custom_call" | custom-call | tf_op jit(solution)/shard_map/adjoint/pallas_call | solution.py:493
  66.5 0.0 copy-start.4
  66.6 0.0 copy-start.5
  66.6 31.1 %all_to_all.15.got_ref = bf16[16,128,256]{2,1,0:T(8,128)(2,1)S(1)} all-to-all(bf16[16,128,256]{2,1,0:T(8,128)(2,1)S(1)} %bitcast.12), channel_id=1, replica_groups=mesh['half'=2,'near'=4,'outer'=1,'slot'=2,'core'=2] {'half','near','slot'}, dimensions={0} | all-to-all | bytes 2097152 | tf_op jit(solution)/shard_map/all_to_all | solution.py:574
  97.6 0.0 copy-done.4
  97.6 0.0 copy-done.5
  97.6 2.3 %unpack.1 = f32[1,512,256]{2,1,0:T(8,128)} custom-call(s32[2,16]{1,0:T(2,128)S(1)} %bitcast.21, s32[1,512]{1,0:T(1,128)S(1)} %bitcast.18, bf16[16,128,256]{2,1,0:T(8,128)(2,1)S(1)} %all_to_all.15.got_ref), custom_call_target="tpu_custom_call" | custom-call | tf_op jit(solution)/shard_map/unpack/pallas_call | solution.py:127
  (3 shorter events, 0.0 us)
Async XLA Ops:
  2.2 28.5 %copy-start.1 = (f32[8,18,256]{2,1,0:T(8,128)S(1)}, f32[8,18,256]{2,1,0:T(8,128)}, u32[]{:S(2)}) copy-start(f32[8,18,256]{2,1,0:T(8,128)} %constant.51.clone.fine_ref.fine_hbm) | copy-start | bytes 442372
  2.2 28.5 %copy-start.2 = (f32[8,8,256]{2,1,0:T(8,128)S(1)}, f32[8,8,256]{2,1,0:T(8,128)}, u32[]{:S(2)}) copy-start(f32[8,8,256]{2,1,0:T(8,128)} %constant.52.clone.coarse_ref.coarse_hbm) | copy-start | bytes 196612
  2.2 21.0 %all-to-all-start = ((bf16[8,128,256]{2,1,0:T(8,128)(2,1)}), bf16[8,128,256]{2,1,0:T(8,128)(2,1)S(1)}, u32[]{:S(2)}, u32[]{:S(2)}) async-start(bf16[8,128,256]{2,1,0:T(8,128)(2,1)} %pack.2), calls=%async_computation | async-start | bytes 1048576 | tf_op jit(solution)/shard_map/all_to_all | solution.py:547
  8.6 13.4 %collective-permute-start = (bf16[1,512,256]{2,1,0:T(8,128)(2,1)}, bf16[1,512,256]{2,1,0:T(8,128)(2,1)S(1)}, u32[]{:S(2)}, u32[]{:S(2)}) collective-permute-start(bf16[1,512,256]{2,1,0:T(8,128)(2,1)} %spectra_hbm.1), channel_id=1, source_target_pairs={{0,16},{16,0},{1,17},{17,1},{2,18},{18,2},{3,19},{19,3},{4,20},{20... | collective-permute-start | bytes 786440 | tf_op jit(solution)/shard_map/ppermute | solution.py:551
  13.9 1.6 %copy-start = (bf16[2,64,64,128]{3,2,1,0:T(8,128)(2,1)S(1)}, bf16[2,64,64,128]{3,2,1,0:T(8,128)(2,1)}, u32[]{:S(2)}) copy-start(bf16[2,64,64,128]{3,2,1,0:T(8,128)(2,1)} %param.10) | copy-start | bytes 6291460
  15.5 0.9 copy-start.3
  22.0 1.3 %copy-start.6 = (bf16[1,512,256]{2,1,0:T(8,128)(2,1)}, bf16[1,512,256]{2,1,0:T(8,128)(2,1)S(1)}, u32[]{:S(2)}) copy-start(bf16[1,512,256]{2,1,0:T(8,128)(2,1)S(1)} %collective-permute-done.spectra_hbm) | copy-start | bytes 786436
  25.5 13.2 %all-to-all-start.1 = ((bf16[8,128,256]{2,1,0:T(8,128)(2,1)}), bf16[8,128,256]{2,1,0:T(8,128)(2,1)S(1)}, u32[]{:S(2)}, u32[]{:S(2)}) async-start(bf16[8,128,256]{2,1,0:T(8,128)(2,1)} %pack.3), calls=%async_computation.1 | async-start | bytes 1048576 | tf_op jit(solution)/shard_map/all_to_all | solution.py:547
  42.8 2.7 %collective-permute-start.1 = (bf16[1024,512]{1,0:T(8,128)(2,1)S(1)}, bf16[1024,512]{1,0:T(8,128)(2,1)S(1)}, u32[]{:S(2)}, u32[]{:S(2)}) collective-permute-start(bf16[1024,512]{1,0:T(8,128)(2,1)S(1)} %get-tuple-element.30), channel_id=1, source_target_pairs={{0,1},{1,0},{2,3},{3,2},{4,5},{5,4},{6,7},{7,6},{8,9},{9,8},{10,11... | collective-permute-start | bytes 3145736 | tf_op jit(solution)/shard_map/ppermute | solution.py:565
  66.5 31.1 %copy-start.4 = (s32[512]{0:T(512)S(1)}, s32[512]{0:T(512)}, u32[]{:S(2)}) copy-start(s32[512]{0:T(512)} %param.12) | copy-start | bytes 6148
  66.6 31.1 %copy-start.5 = (s32[16,2]{0,1:T(2,128)S(1)}, s32[16,2]{0,1:T(2,128)}, u32[]{:S(2)}) copy-start(s32[16,2]{0,1:T(2,128)} %param.11) | copy-start | bytes 388

commit v11 on v10

--- a/solution.py
+++ b/solution.py
@@ -59,9 +59,25 @@
     return jnp.dot(a, b, preferred_element_type=F32)
 
 
-def pack_kernel(first_ref, blocks_hbm, members_hbm, spectra_hbm, out_ref, blocks_ref, members_ref, spectra_ref, ordered, sems):
+def pack_rows(first_ref, blocks_ref, members_ref, spectra_ref, out_ref, ordered, rows_there=None, blocks_there=None):
     stations = spectra_ref.shape[1]
     b = out_ref.shape[1] // 2
+    station = lax.broadcasted_iota(jnp.int32, (stations, stations), 0)
+    chosen = (station == members_ref[...]).astype(F32).astype(BF16)
+    if rows_there is not None:
+        rows_there()
+    ordered[...] = lax.dot_general(
+        chosen, spectra_ref[0], (((0,), (0,)), ((), ())), preferred_element_type=F32
+    ).astype(BF16)
+    if blocks_there is not None:
+        blocks_there()
+    for p in range(out_ref.shape[0]):
+        for side in range(2):
+            row = pl.multiple_of(blocks_ref[side, first_ref[0] + p] * b, b)
+            out_ref[p, side * b:(side + 1) * b, :] = ordered[pl.ds(row, b), :]
+
+
+def pack_kernel(first_ref, blocks_hbm, members_hbm, spectra_hbm, out_ref, blocks_ref, members_ref, spectra_ref, ordered, sems):
     copies = (
         pltpu.make_async_copy(spectra_hbm, spectra_ref, sems.at[0]),
         pltpu.make_async_copy(members_hbm, members_ref, sems.at[1]),
@@ -69,18 +85,25 @@
     )
     for copy in copies:
         copy.start()
-    station = lax.broadcasted_iota(jnp.int32, (stations, stations), 0)
     copies[1].wait()
-    chosen = (station == members_ref[...]).astype(F32).astype(BF16)
-    copies[0].wait()
-    ordered[...] = lax.dot_general(
-        chosen, spectra_ref[0], (((0,), (0,)), ((), ())), preferred_element_type=F32
-    ).astype(BF16)
-    copies[2].wait()
-    for p in range(out_ref.shape[0]):
-        for side in range(2):
-            row = pl.multiple_of(blocks_ref[side, first_ref[0] + p] * b, b)
-            out_ref[p, side * b:(side + 1) * b, :] = ordered[pl.ds(row, b), :]
+    pack_rows(
+        first_ref, blocks_ref, members_ref, spectra_ref, out_ref, ordered, copies[0].wait, copies[2].wait
+    )
+
+
+def repack(first, pair_blocks, members, spectra, b):
+    _, stations, cols = spectra.shape
+    smem = pl.BlockSpec(memory_space=pltpu.SMEM)
+    vmem = pl.BlockSpec(memory_space=pltpu.VMEM)
+    return pl.pallas_call(
+        pack_rows,
+        out_shape=pltpu.VMEM((pair_blocks.shape[1] // 2, 2 * b, cols), BF16),
+        in_specs=[smem, smem, vmem, vmem],
+        out_specs=vmem,
+        scratch_shapes=[pltpu.VMEM((stations, cols), BF16)],
+        compiler_params=pltpu.CompilerParams(vmem_limit_bytes=8 << 20),
+        name="repack",
+    )(first, pair_blocks, members, spectra)
 
 
 def pack(first, pair_blocks, members, spectra, b):
@@ -556,7 +579,7 @@
     got_near, opposite, seen, env, mask_here, scalars = lax.optimization_barrier(
         (got_near, opposite, seen, env, mask_here, scalars)
     )
-    got_far = exchange(pack(first_pair, pair_blocks, members, opposite, b))
+    got_far = exchange(repack(first_pair, pair_blocks, members, opposite, b))
     mine, kept_near = forward_pass(start_near, mask_here, got_near.reshape(shape), fine, coarse, [])
     got_far, mine = lax.optimization_barrier((got_far, mine))
     mine, sent, kept_far = forward_pass(start_far, mask_here, got_far.reshape(shape), fine, coarse, [mine])

time: 100 us -> 99.2 us (level)
    pallas_call x2 -> x1, Pallas kernels: 4.4 us -> 2.22 us  [pack(): pl.pallas_call(pack_kernel, out_shape=pltpu.VMEM((n_pairs, 2 * b, cols),...]
    pallas_call x0 -> x1, Pallas kernels: none -> 1.74 us  [repack(): pl.pallas_call(pack_rows, out_shape=pltpu.VMEM((pair_blocks.shape[1] // 2...]
    unnamed x14 -> x12, local copies, waits for them, and re-layouts: 2.51 us -> 2.5 us
where the time goes in v11:
time: 99.2 us; the launch traced here: 98.7 us
  Pallas kernels  39.1 us (39%)
  blocking collectives  31 us (31%)
  starting transfers between devices  13.5 us (14%)
  waiting for transfers between devices  7.59 us (8%)
  other arithmetic  3.48 us (4%)
  local copies, waits for them, and re-layouts  3.16 us (3%)
    all_to_all x1, blocking collectives, body(): lax.all_to_all(contrib.reshape(shares * slots, 2 * b, cols), ('half', 'ne...  31 us
    pallas_call x1, Pallas kernels, adjoint_pass(): pl.pallas_call(functools.partial(adjoint_kernel, (b, scale, group)), out_...  21 us
    all_to_all x2, starting transfers between devices, exchange(): moved = lax.all_to_all(flat, ('near', 'slot'), 0, 0, tiled=True)  10.9 us
    pallas_call x2, Pallas kernels, forward_pass(): pl.pallas_call(functools.partial(forward_kernel, b, bool(before)), out_sh...  8.24 us
    all_to_all x2, waiting for transfers between devices, exchange(): moved = lax.all_to_all(flat, ('near', 'slot'), 0, 0, tiled=True)  5.02 us
    pallas_call x1, Pallas kernels, prepare(): pl.pallas_call(functools.partial(prepare_kernel, b), out_shape=[pltpu.HBM...  3.6 us
    ppermute x1, starting transfers between devices, body(): opposite = lax.ppermute(spectra, 'half', [(0, 1), (1, 0)])  2.58 us
    ppermute x1, waiting for transfers between devices, body(): lax.ppermute(sent, axis, [(i, (i + k) % n) for i in range(n)])  2.57 us
  transfers between devices with their start and end apart: 4, of which 3 were waited for; matrix products, arithmetic and copies ran while one was open for 4% of the time, Pallas kernels for 8%

profile of v11, /device:TPU:0, one launch (start us, length us, event | category | flops | bytes accessed | tf_op | source)
XLA Modules:
  0.0 98.7 jit_solution(247853481867756316)
XLA Ops:
  0.0 0.0 copy-start.4
  0.0 0.0 copy-start.5
  0.0 2.2 %pack.1 = bf16[8,128,256]{2,1,0:T(8,128)(2,1)} custom-call(s32[1]{0:T(128)S(6)} %mul.13.first_ref, s32[2,16]{1,0:T(2,128)} %bitcast.19, s32[1,512]{1,0:T(1,128)} %bitcast.16, bf16[1,512,256]{2,1,0:T(8,128)(2,1)} %spectra_hbm.1), custom_call_target="tpu_custom_call" | custom-call | tf_op jit(solution)/shard_map/pack/pallas_call | solution.py:113
  2.2 0.0 copy-start.1
  2.2 0.0 copy-start.2
  2.3 6.3 %all-to-all-start = ((bf16[8,128,256]{2,1,0:T(8,128)(2,1)}), bf16[8,128,256]{2,1,0:T(8,128)(2,1)S(1)}, u32[]{:S(2)}, u32[]{:S(2)}) async-start(bf16[8,128,256]{2,1,0:T(8,128)(2,1)} %pack.1), calls=%async_computation | async-start | bytes 1048576 | tf_op jit(solution)/shard_map/all_to_all | solution.py:570
  8.6 2.6 %collective-permute-start = (bf16[1,512,256]{2,1,0:T(8,128)(2,1)}, bf16[1,512,256]{2,1,0:T(8,128)(2,1)S(1)}, u32[]{:S(2)}, u32[]{:S(2)}) collective-permute-start(bf16[1,512,256]{2,1,0:T(8,128)(2,1)} %spectra_hbm.1), channel_id=1, source_target_pairs={{0,16},{16,0},{1,17},{17,1},{2,18},{18,2},{3,19},{19,3},{4,20},{20... | collective-permute-start | bytes 786440 | tf_op jit(solution)/shard_map/ppermute | solution.py:574
  11.2 1.4 %fusion.1 = (f32[]{:T(128)}, f32[1,4]{1,0:T(1,128)S(1)}) fusion(s32[2,4]{1,0:T(2,128)} %param.13, s32[]{:T(128)S(6)} %select_n.10), kind=kLoop, calls=%fused_computation.8 | loop fusion | flops 7 | bytes 40 | tf_op jit(solution)/shard_map/reduce_sum | solution.py:559
  13.3 0.7 constant_dynamic-slice_fusion.1
  13.9 0.0 copy-start
  13.9 1.6 %copy-done = bf16[2,64,64,128]{3,2,1,0:T(8,128)(2,1)S(1)} copy-done((bf16[2,64,64,128]{3,2,1,0:T(8,128)(2,1)S(1)}, bf16[2,64,64,128]{3,2,1,0:T(8,128)(2,1)}, u32[]{:S(2)}) %copy-start) | copy-done | bytes 2097176
  15.5 0.9 copy-done.3
  16.4 3.6 %prepare.1 = (bf16[32,128,128]{2,1,0:T(8,128)(2,1)}, f32[32,128,128]{2,1,0:T(8,128)}) custom-call(s32[1]{0:T(128)} %bitcast.4.slot_ref, bf16[2,4096,128]{2,1,0:T(8,128)(2,1)S(1)} %bitcast.13, bf16[384,128]{1,0:T(8,128)(2,1)S(1)} %copy-done.3), custom_call_target="tpu_custom_call" | custom-call | flops 134217728 | bytes 4194304 | tf_op jit(solution)/shard_map/prepare/pallas_call | solution.py:195
  20.0 2.0 %broadcast_divide_fusion = (f32[2]{0:T(128)S(1)}, f32[2]{0:T(128)S(1)}) fusion(f32[]{:T(128)} %get-tuple-element.37, f32[1]{0:T(128)} %bitcast.7, f32[1]{0:T(128)} %bitcast.6), kind=kLoop, calls=%fused_computation.7 | loop fusion | flops 4 | bytes 28 | tf_op jit(solution)/shard_map/div | solution.py:561
  22.0 0.1 pad_maximum_fusion.1.scalars_ref
  22.0 0.0 collective-permute-done.spectra_ref
  22.0 1.2 %all-to-all-done = bf16[8,128,256]{2,1,0:T(8,128)(2,1)S(1)} async-done(((bf16[8,128,256]{2,1,0:T(8,128)(2,1)}), bf16[8,128,256]{2,1,0:T(8,128)(2,1)S(1)}, u32[]{:S(2)}, u32[]{:S(2)}) %all-to-all-start) | async-done | bytes 524320 | tf_op jit(solution)/shard_map/all_to_all | solution.py:570
  23.3 0.0 copy-done.4
  23.3 0.0 copy-done.5
  23.3 1.7 %repack.1 = bf16[8,128,256]{2,1,0:T(8,128)(2,1)} custom-call(s32[1]{0:T(128)S(6)} %mul.13.first_ref, s32[2,16]{1,0:T(2,128)S(1)} %bitcast.20, s32[1,512]{1,0:T(1,128)S(1)} %bitcast.17, bf16[1,512,256]{2,1,0:T(8,128)(2,1)S(1)} %collective-permute-done.spectra_ref), custom_call_target="tpu_custom_call" | custom-call | tf_op jit(solution)/shard_map/repack/pallas_call | solution.py:98
  25.0 4.6 %all-to-all-start.1 = ((bf16[8,128,256]{2,1,0:T(8,128)(2,1)}), bf16[8,128,256]{2,1,0:T(8,128)(2,1)S(1)}, u32[]{:S(2)}, u32[]{:S(2)}) async-start(bf16[8,128,256]{2,1,0:T(8,128)(2,1)} %repack.1), calls=%async_computation.1 | async-start | bytes 1048576 | tf_op jit(solution)/shard_map/all_to_all | solution.py:570
  29.6 0.0 copy-done.1
  29.6 0.0 copy-done.2
  29.6 4.1 %forward.2 = (f32[1024,512]{1,0:T(8,128)S(1)}, bf16[4,2,128,256]{3,2,1,0:T(8,128)(2,1)}) custom-call(s32[1]{0:T(128)} %bitcast.2.offset_ref, f32[2]{0:T(128)S(1)} %get-tuple-element.23.mask_ref, bf16[4,2,128,256]{3,2,1,0:T(8,128)(2,1)S(1)} %bitcast.14, f32[8,18,256]{2,1,0:T(8,128)S(1)} %copy-done.1, f32[8,8,256]{2,1,0:T(8,128)S(1)} %copy-done.2), custom_call_target="tpu_custom_call" | custom-call | tf_op jit(solution)/shard_map/forward/pallas_call | solution.py:309
  33.7 3.8 %all-to-all-done.1 = bf16[8,128,256]{2,1,0:T(8,128)(2,1)S(1)} async-done(((bf16[8,128,256]{2,1,0:T(8,128)(2,1)}), bf16[8,128,256]{2,1,0:T(8,128)(2,1)S(1)}, u32[]{:S(2)}, u32[]{:S(2)}) %all-to-all-start.1) | async-done | bytes 524320 | tf_op jit(solution)/shard_map/all_to_all | solution.py:570
  37.5 4.2 %forward.3 = (f32[1024,512]{1,0:T(8,128)S(1)}, bf16[1024,512]{1,0:T(8,128)(2,1)S(1)}, bf16[4,2,128,256]{3,2,1,0:T(8,128)(2,1)}) custom-call(s32[1]{0:T(128)} %bitcast.3.offset_ref, f32[2]{0:T(128)S(1)} %get-tuple-element.23.mask_ref, bf16[4,2,128,256]{3,2,1,0:T(8,128)(2,1)S(1)} %bitcast.15, ...), custom_call_target="tpu_custom_call", output_to_operand_aliasing={{0}: (5, {})} | custom-call | tf_op jit(solution)/shard_map/forward/pallas_call | solution.py:309
  41.6 0.1 collective-permute-start.1
  41.7 0.1 pad_add_fusion.starts_ref
  41.8 2.6 %collective-permute-done.1.other_ref = bf16[1024,512]{1,0:T(8,128)(2,1)S(1)} collective-permute-done((bf16[1024,512]{1,0:T(8,128)(2,1)S(1)}, bf16[1024,512]{1,0:T(8,128)(2,1)S(1)}, u32[]{:S(2)}, u32[]{:S(2)}) %collective-permute-start.1) | collective-permute-done | bytes 1048608 | tf_op jit(solution)/shard_map/ppermute | solution.py:588
  44.4 21.0 %adjoint.1 = bf16[8,2,128,256]{3,2,1,0:T(8,128)(2,1)S(1)} custom-call(s32[2]{0:T(128)S(1)} %pad_add_fusion.starts_ref, f32[3]{0:T(128)S(1)} %pad_maximum_fusion.1.scalars_ref, f32[1024,512]{1,0:T(8,128)S(1)} %get-tuple-element.29.mine_ref, bf16[1024,512]{1,0:T(8,128)(2,1)S(1)} %collective-permute-done.1.other_ref, ...), custom_call_target="tpu_custom_call" | custom-call | tf_op jit(solution)/shard_map/adjoint/pallas_call | solution.py:516
  65.4 31.0 %all_to_all.15.got_ref = bf16[16,128,256]{2,1,0:T(8,128)(2,1)S(1)} all-to-all(bf16[16,128,256]{2,1,0:T(8,128)(2,1)S(1)} %bitcast.12), channel_id=1, replica_groups=mesh['half'=2,'near'=4,'outer'=1,'slot'=2,'core'=2] {'half','near','slot'}, dimensions={0} | all-to-all | bytes 2097152 | tf_op jit(solution)/shard_map/all_to_all | solution.py:597
  96.4 2.3 %unpack.1 = f32[1,512,256]{2,1,0:T(8,128)} custom-call(s32[2,16]{1,0:T(2,128)S(1)} %bitcast.21, s32[1,512]{1,0:T(1,128)S(1)} %bitcast.18, bf16[16,128,256]{2,1,0:T(8,128)(2,1)S(1)} %all_to_all.15.got_ref), custom_call_target="tpu_custom_call" | custom-call | tf_op jit(solution)/shard_map/unpack/pallas_call | solution.py:150
  (1 shorter events, 0.0 us)
Async XLA Ops:
  0.0 23.3 %copy-start.4 = (s32[512]{0:T(512)S(1)}, s32[512]{0:T(512)}, u32[]{:S(2)}) copy-start(s32[512]{0:T(512)} %param.12) | copy-start | bytes 6148
  0.0 23.3 %copy-start.5 = (s32[16,2]{0,1:T(2,128)S(1)}, s32[16,2]{0,1:T(2,128)}, u32[]{:S(2)}) copy-start(s32[16,2]{0,1:T(2,128)} %param.11) | copy-start | bytes 388
  2.2 27.3 %copy-start.1 = (f32[8,18,256]{2,1,0:T(8,128)S(1)}, f32[8,18,256]{2,1,0:T(8,128)}, u32[]{:S(2)}) copy-start(f32[8,18,256]{2,1,0:T(8,128)} %constant.51.clone.fine_ref.fine_hbm) | copy-start | bytes 442372
  2.2 27.3 %copy-start.2 = (f32[8,8,256]{2,1,0:T(8,128)S(1)}, f32[8,8,256]{2,1,0:T(8,128)}, u32[]{:S(2)}) copy-start(f32[8,8,256]{2,1,0:T(8,128)} %constant.52.clone.coarse_ref.coarse_hbm) | copy-start | bytes 196612
  2.3 21.0 %all-to-all-start = ((bf16[8,128,256]{2,1,0:T(8,128)(2,1)}), bf16[8,128,256]{2,1,0:T(8,128)(2,1)S(1)}, u32[]{:S(2)}, u32[]{:S(2)}) async-start(bf16[8,128,256]{2,1,0:T(8,128)(2,1)} %pack.1), calls=%async_computation | async-start | bytes 1048576 | tf_op jit(solution)/shard_map/all_to_all | solution.py:570
  8.6 13.5 %collective-permute-start = (bf16[1,512,256]{2,1,0:T(8,128)(2,1)}, bf16[1,512,256]{2,1,0:T(8,128)(2,1)S(1)}, u32[]{:S(2)}, u32[]{:S(2)}) collective-permute-start(bf16[1,512,256]{2,1,0:T(8,128)(2,1)} %spectra_hbm.1), channel_id=1, source_target_pairs={{0,16},{16,0},{1,17},{17,1},{2,18},{18,2},{3,19},{19,3},{4,20},{20... | collective-permute-start | bytes 786440 | tf_op jit(solution)/shard_map/ppermute | solution.py:574
  13.9 1.6 %copy-start = (bf16[2,64,64,128]{3,2,1,0:T(8,128)(2,1)S(1)}, bf16[2,64,64,128]{3,2,1,0:T(8,128)(2,1)}, u32[]{:S(2)}) copy-start(bf16[2,64,64,128]{3,2,1,0:T(8,128)(2,1)} %param.10) | copy-start | bytes 6291460
  15.5 0.9 copy-start.3
  25.0 12.4 %all-to-all-start.1 = ((bf16[8,128,256]{2,1,0:T(8,128)(2,1)}), bf16[8,128,256]{2,1,0:T(8,128)(2,1)S(1)}, u32[]{:S(2)}, u32[]{:S(2)}) async-start(bf16[8,128,256]{2,1,0:T(8,128)(2,1)} %repack.1), calls=%async_computation.1 | async-start | bytes 1048576 | tf_op jit(solution)/shard_map/all_to_all | solution.py:570
  41.6 2.7 %collective-permute-start.1 = (bf16[1024,512]{1,0:T(8,128)(2,1)S(1)}, bf16[1024,512]{1,0:T(8,128)(2,1)S(1)}, u32[]{:S(2)}, u32[]{:S(2)}) collective-permute-start(bf16[1024,512]{1,0:T(8,128)(2,1)S(1)} %get-tuple-element.30), channel_id=1, source_target_pairs={{0,1},{1,0},{2,3},{3,2},{4,5},{5,4},{6,7},{7,6},{8,9},{9,8},{10,11... | collective-permute-start | bytes 3145736 | tf_op jit(solution)/shard_map/ppermute | solution.py:588
